TPU v7x, 32 devices: a whole 2x2x4 slice. The times are simulated.
32 devices in a mesh: ty: 4 (over x, core), tx: 8 (over z, y).
Axes of the slice: x: 2, y: 2, z: 4, core: 2. Of those that a mesh axis runs over, the one named last changes fastest.
Arguments:
- pixels: bfloat16 [2, 3, 288, 288], P(None, None, 'ty', 'tx'), may hold values from -6 to 6
- pixel_mask: int32 [2, 288, 288], P(None, 'ty', 'tx'), may hold values 0 or 1
- image_sizes: int32 [2], replicated, may hold values from 160 to 288, as said below
- latents: bfloat16 [2, 512, 1024], P(None, 'tx'), may hold values from -6 to 6
- cotangent: bfloat16 [2, 512, 1024], P(None, 'tx'), may hold values from -6 to 6
- feature_gain: float32 [261], replicated, may hold values from 0.5 to 1.5
- query_gain: float32 [1024], replicated, may hold values from 0.5 to 1.5
- query_proj: bfloat16 [1024, 1024], replicated, may hold values from -0.375 to 0.375
- key_proj: bfloat16 [261, 1024], replicated, may hold values from -0.375 to 0.375
- value_proj: bfloat16 [261, 1024], replicated, may hold values from -0.375 to 0.375
- cross_proj: bfloat16 [1024, 1024], replicated, may hold values from -6 to 6
- hidden_gain: float32 [1024], replicated, may hold values from 0.5 to 1.5
- hidden_up: bfloat16 [1024, 1024], replicated, may hold values from -0.1875 to 0.1875
- hidden_down: bfloat16 [1024, 1024], replicated, may hold values from -0.1875 to 0.1875
- tower_gain: float32 [1024], replicated, may hold values from 0.5 to 1.5
- tower_query: bfloat16 [1024, 1024], replicated, may hold values from -0.375 to 0.375
- tower_key: bfloat16 [1024, 1024], replicated, may hold values from -0.1875 to 0.1875
- tower_value: bfloat16 [1024, 1024], replicated, may hold values from -0.1875 to 0.1875
- tower_proj: bfloat16 [1024, 1024], replicated, may hold values from -0.5 to 0.5
- final_gain: float32 [1024], replicated, may hold values from 0.5 to 1.5
- final_up: bfloat16 [1024, 1024], replicated, may hold values from -0.1875 to 0.1875
- final_down: bfloat16 [1024, 1024], replicated, may hold values from -0.1875 to 0.1875
Outputs:
- result: bfloat16 [2, 512, 1024], P(None, 'tx')
- latent_grad: float32 [2, 512, 1024], P(None, 'tx')
- feature_gain_grad: float32 [261], replicated
- query_gain_grad: float32 [1024], P('tx')
- query_proj_grad: float32 [1024, 1024], P('tx')
- key_proj_grad: float32 [261, 1024], replicated
- value_proj_grad: float32 [261, 1024], replicated
- cross_proj_grad: float32 [1024, 1024], P('tx')
- hidden_gain_grad: float32 [1024], P('tx')
- hidden_up_grad: float32 [1024, 1024], P('tx')
- hidden_down_grad: float32 [1024, 1024], P('tx')
- tower_gain_grad: float32 [1024], P('tx')
- tower_query_grad: float32 [1024, 1024], P('tx')
- tower_key_grad: float32 [1024, 1024], P('tx')
- tower_value_grad: float32 [1024, 1024], P('tx')
- tower_proj_grad: float32 [1024, 1024], P('tx')
- final_gain_grad: float32 [1024], P('tx')
- final_up_grad: float32 [1024, 1024], P('tx')
- final_down_grad: float32 [1024, 1024], P('tx')
Inputs may be any that keep to these rules, and one draw needn't show every extreme that they name: `image_sizes`: each image is square, with 160, 224 or 288 pixels on a side, and some image has each of the two ends.
All inputs are finite; a program needn't handle non-finite values. No bound on the sum of `pixel_mask` on one device may be relied on, other than what follows from the above.
Results may differ from a plain program's by a relative error of at most 0.025.
Values may be sent and summed in bfloat16 or wider, within the bound.
A program may use at most 192 MiB of HBM per device.

v0:
```python
import math

import jax
import jax.numpy as jnp
from jax import lax
from jax.sharding import PartitionSpec as P

BANDS = 64
FEAT = 261
HEADS = 8


EPSILON = 1e-05
FLOAT = jnp.float32
BFLOAT = jnp.bfloat16


def layer_norm(values, scales):
    centre = jnp.mean(values, axis=-1, keepdims=True)
    shifted = values - centre
    spread = jnp.mean(shifted * shifted, axis=-1, keepdims=True)
    return shifted * lax.rsqrt(spread + EPSILON) * scales


def gelu_tanh(values):
    cubic = values + 0.044715 * values * values * values
    return 0.5 * values * (1.0 + jnp.tanh(0.7978845608028654 * cubic))


def linear(inputs, weight):
    return lax.dot_general(
        inputs, weight, (((inputs.ndim - 1,), (0,)), ((), ())), preferred_element_type=FLOAT
    )


def linear_back(upstream, weight):
    return lax.dot_general(
        upstream, weight, (((upstream.ndim - 1,), (1,)), ((), ())), preferred_element_type=FLOAT
    )


def weight_grad(inputs, upstream):
    flat_inputs = inputs.reshape(-1, inputs.shape[-1])
    flat_upstream = upstream.reshape(-1, upstream.shape[-1])
    return lax.dot_general(
        flat_inputs, flat_upstream, (((0,), (0,)), ((), ())), preferred_element_type=FLOAT
    )


def pixel_features(pixels, image_sizes, row_ids, col_ids):
    item_count = pixels.shape[0]
    tile_height = pixels.shape[2]
    tile_width = pixels.shape[3]
    image_side = image_sizes.astype(FLOAT)[:, None]
    ycoord = -1.0 + 2.0 * row_ids.astype(FLOAT)[None, :] / (image_side - 1.0)
    xcoord = -1.0 + 2.0 * col_ids.astype(FLOAT)[None, :] / (image_side - 1.0)
    band_index = jnp.arange(BANDS, dtype=jnp.int32).astype(FLOAT)
    frequency = 1.0 + band_index[None, :] * (image_side * 0.5 - 1.0) / (BANDS - 1)
    yangle = math.pi * ycoord[:, :, None] * frequency[:, None, :]
    xangle = math.pi * xcoord[:, :, None] * frequency[:, None, :]
    tile_shape = (item_count, tile_height, tile_width)
    pieces = [
        jnp.transpose(pixels, (0, 2, 3, 1)).astype(FLOAT),
        jnp.broadcast_to(ycoord[:, :, None, None], tile_shape + (1,)),
        jnp.broadcast_to(xcoord[:, None, :, None], tile_shape + (1,)),
        jnp.broadcast_to(jnp.sin(yangle)[:, :, None, :], tile_shape + (BANDS,)),
        jnp.broadcast_to(jnp.cos(yangle)[:, :, None, :], tile_shape + (BANDS,)),
        jnp.broadcast_to(jnp.sin(xangle)[:, None, :, :], tile_shape + (BANDS,)),
        jnp.broadcast_to(jnp.cos(xangle)[:, None, :, :], tile_shape + (BANDS,)),
    ]
    return jnp.concatenate(pieces, axis=3).reshape(item_count, tile_height * tile_width, FEAT)


def on_device(
    pixels,
    pixel_mask,
    image_sizes,
    latents,
    cotangent,
    feature_gain,
    query_gain,
    query_proj,
    key_proj,
    value_proj,
    cross_proj,
    hidden_gain,
    hidden_up,
    hidden_down,
    tower_gain,
    tower_query,
    tower_key,
    tower_value,
    tower_proj,
    final_gain,
    final_up,
    final_down,
):
    item_count = pixels.shape[0]
    tile_height = pixels.shape[2]
    tile_width = pixels.shape[3]
    model_width = latents.shape[2]
    rows_here = latents.shape[1]
    head_count = HEADS
    head_size = model_width // head_count
    cross_scale = 1.0 / math.sqrt(model_width)
    tower_scale = 1.0 / math.sqrt(head_size)
    row_ids = lax.axis_index("ty") * tile_height + jnp.arange(tile_height, dtype=jnp.int32)
    col_ids = lax.axis_index("tx") * tile_width + jnp.arange(tile_width, dtype=jnp.int32)
    side_sizes = image_sizes[:, None, None]
    inside = (
        (pixel_mask > 0)
        & (row_ids[None, :, None] < side_sizes)
        & (col_ids[None, None, :] < side_sizes)
    )
    live_mask = inside.reshape(item_count, 1, tile_height * tile_width)
    features = pixel_features(pixels, image_sizes, row_ids, col_ids)

    def feature_norm(scales):
        return layer_norm(features, scales)

    normed, back_features = jax.vjp(feature_norm, feature_gain)
    normed_pixels = normed.astype(BFLOAT)
    pixel_keys = linear(normed_pixels, key_proj).astype(BFLOAT)
    pixel_values = linear(normed_pixels, value_proj).astype(BFLOAT)
    latent_rows = latents.astype(FLOAT)
    query_normed, back_query_norm = jax.vjp(layer_norm, latent_rows, query_gain)
    query_input = query_normed.astype(BFLOAT)
    own_queries = linear(query_input, query_proj).astype(BFLOAT)
    all_queries = lax.all_gather(own_queries, "tx", axis=1, tiled=True)
    scores = (
        jnp.einsum("blc,bpc->blp", all_queries, pixel_keys, preferred_element_type=FLOAT)
        * cross_scale
    )
    live_scores = jnp.where(live_mask, scores, -1e30)
    row_top = lax.pmax(jnp.max(live_scores, axis=2), ("ty", "tx"))
    row_exp = jnp.where(
        live_mask,
        jnp.exp(jnp.where(live_mask, scores, row_top[:, :, None]) - row_top[:, :, None]),
        0.0,
    )
    row_total = lax.psum(jnp.sum(row_exp, axis=2), ("ty", "tx"))
    cross_exact = row_exp / row_total[:, :, None]
    partial_attended = jnp.einsum(
        "blp,bpc->blc", cross_exact.astype(BFLOAT), pixel_values, preferred_element_type=FLOAT
    )
    column_sums = lax.psum_scatter(partial_attended, "tx", scatter_dimension=1, tiled=True)
    attended = lax.psum(column_sums, "ty")
    attended_input = attended.astype(BFLOAT)
    resid_one = latent_rows + linear(attended_input, cross_proj)
    hidden_normed, back_hidden_norm = jax.vjp(layer_norm, resid_one, hidden_gain)
    hidden_input = hidden_normed.astype(BFLOAT)
    hidden_lifted, back_hidden_gelu = jax.vjp(gelu_tanh, linear(hidden_input, hidden_up))
    hidden_act = hidden_lifted.astype(BFLOAT)
    resid_two = resid_one + linear(hidden_act, hidden_down)
    tower_normed, back_tower_norm = jax.vjp(layer_norm, resid_two, tower_gain)
    tower_input = tower_normed.astype(BFLOAT)
    tower_q = linear(tower_input, tower_query).astype(BFLOAT)
    tower_k = linear(tower_input, tower_key).astype(BFLOAT)
    tower_v = linear(tower_input, tower_value).astype(BFLOAT)
    all_keys, all_values = (
        lax.all_gather(tower_k, "tx", axis=1, tiled=True),
        lax.all_gather(tower_v, "tx", axis=1, tiled=True),
    )
    split_q = tower_q.reshape(item_count, rows_here, head_count, head_size)
    split_k = all_keys.reshape(item_count, -1, head_count, head_size)
    split_v = all_values.reshape(item_count, -1, head_count, head_size)
    tower_scores = (
        jnp.einsum("bqhd,bkhd->bhqk", split_q, split_k, preferred_element_type=FLOAT) * tower_scale
    )
    tower_top = jnp.max(tower_scores, axis=3, keepdims=True)
    tower_exp = jnp.exp(tower_scores - tower_top)
    tower_total = jnp.sum(tower_exp, axis=3, keepdims=True)
    tower_exact = tower_exp / tower_total
    tower_probs = tower_exact.astype(BFLOAT)
    mixed = jnp.einsum(
        "bhqk,bkhd->bqhd", tower_probs, split_v, preferred_element_type=FLOAT
    ).reshape(item_count, rows_here, model_width)
    mixed_input = mixed.astype(BFLOAT)
    resid_three = resid_two + linear(mixed_input, tower_proj)
    final_normed, back_final_norm = jax.vjp(layer_norm, resid_three, final_gain)
    final_input = final_normed.astype(BFLOAT)
    final_lifted, back_final_gelu = jax.vjp(gelu_tanh, linear(final_input, final_up))
    final_act = final_lifted.astype(BFLOAT)
    resid_four = resid_three + linear(final_act, final_down)
    grad_four = cotangent.astype(FLOAT)
    final_down_grad = weight_grad(final_act, cotangent)
    grad_final_lift = back_final_gelu(linear_back(cotangent, final_down))[0].astype(BFLOAT)
    final_up_grad = weight_grad(final_input, grad_final_lift)
    grad_rows_three, final_gain_grad = back_final_norm(linear_back(grad_final_lift, final_up))
    grad_three = grad_four + grad_rows_three
    grad_tower_out = grad_three.astype(BFLOAT)
    tower_proj_grad = weight_grad(mixed_input, grad_tower_out)
    grad_mixed_flat = linear_back(grad_tower_out, tower_proj).astype(BFLOAT)
    grad_mixed = grad_mixed_flat.reshape(item_count, rows_here, head_count, head_size)
    grad_tower_p = jnp.einsum("bqhd,bkhd->bhqk", grad_mixed, split_v, preferred_element_type=FLOAT)
    tower_delta = jnp.sum(tower_exact * grad_tower_p, axis=3, keepdims=True)
    grad_tower_scores = (tower_exact * (grad_tower_p - tower_delta)).astype(BFLOAT)
    grad_tower_q = (
        (
            jnp.einsum("bhqk,bkhd->bqhd", grad_tower_scores, split_k, preferred_element_type=FLOAT)
            * tower_scale
        )
        .astype(BFLOAT)
        .reshape(item_count, rows_here, model_width)
    )
    value_part = jnp.einsum(
        "bhqk,bqhd->bkhd", tower_probs, grad_mixed, preferred_element_type=FLOAT
    )
    key_part = (
        jnp.einsum("bhqk,bqhd->bkhd", grad_tower_scores, split_q, preferred_element_type=FLOAT)
        * tower_scale
    )
    key_sums, value_sums = (
        lax.psum_scatter(
            key_part.reshape(item_count, -1, model_width), "tx", scatter_dimension=1, tiled=True
        ),
        lax.psum_scatter(
            value_part.reshape(item_count, -1, model_width), "tx", scatter_dimension=1, tiled=True
        ),
    )
    grad_tower_k = key_sums.astype(BFLOAT)
    grad_tower_v = value_sums.astype(BFLOAT)
    tower_query_grad = weight_grad(tower_input, grad_tower_q)
    tower_key_grad = weight_grad(tower_input, grad_tower_k)
    tower_value_grad = weight_grad(tower_input, grad_tower_v)
    grad_tower_rows = (
        linear_back(grad_tower_q, tower_query)
        + linear_back(grad_tower_k, tower_key)
        + linear_back(grad_tower_v, tower_value)
    )
    grad_rows_two, tower_gain_grad = back_tower_norm(grad_tower_rows)
    grad_two = grad_three + grad_rows_two
    grad_hidden_out = grad_two.astype(BFLOAT)
    hidden_down_grad = weight_grad(hidden_act, grad_hidden_out)
    grad_hidden_lift = back_hidden_gelu(linear_back(grad_hidden_out, hidden_down))[0].astype(BFLOAT)
    hidden_up_grad = weight_grad(hidden_input, grad_hidden_lift)
    grad_rows_one, hidden_gain_grad = back_hidden_norm(linear_back(grad_hidden_lift, hidden_up))
    grad_one = grad_two + grad_rows_one
    grad_cross_out = grad_one.astype(BFLOAT)
    cross_proj_grad = weight_grad(attended_input, grad_cross_out)
    grad_attended = linear_back(grad_cross_out, cross_proj).astype(BFLOAT)
    all_upstream = lax.all_gather(grad_attended, "tx", axis=1, tiled=True)
    again_scores = (
        jnp.einsum("blc,bpc->blp", all_queries, pixel_keys, preferred_element_type=FLOAT)
        * cross_scale
    )
    again_exp = jnp.where(
        live_mask,
        jnp.exp(jnp.where(live_mask, again_scores, row_top[:, :, None]) - row_top[:, :, None]),
        0.0,
    )
    again_probs = again_exp / row_total[:, :, None]
    grad_probs = jnp.einsum(
        "blc,bpc->blp", all_upstream, pixel_values, preferred_element_type=FLOAT
    )
    cross_delta = lax.psum(jnp.sum(again_probs * grad_probs, axis=2), ("ty", "tx"))
    grad_scores = (again_probs * (grad_probs - cross_delta[:, :, None])).astype(BFLOAT)
    query_part = (
        jnp.einsum("blp,bpc->blc", grad_scores, pixel_keys, preferred_element_type=FLOAT)
        * cross_scale
    )
    query_columns = lax.psum_scatter(query_part, "tx", scatter_dimension=1, tiled=True)
    grad_queries = lax.psum(query_columns, "ty").astype(BFLOAT)
    grad_keys = (
        jnp.einsum("blp,blc->bpc", grad_scores, all_queries, preferred_element_type=FLOAT)
        * cross_scale
    ).astype(BFLOAT)
    grad_values = jnp.einsum(
        "blp,blc->bpc", again_probs.astype(BFLOAT), all_upstream, preferred_element_type=FLOAT
    ).astype(BFLOAT)
    key_proj_grad = weight_grad(normed_pixels, grad_keys)
    value_proj_grad = weight_grad(normed_pixels, grad_values)
    grad_normed = linear_back(grad_keys, key_proj) + linear_back(grad_values, value_proj)
    feature_part = back_features(grad_normed)[0]
    pixel_sums = lax.psum((key_proj_grad, value_proj_grad, feature_part), ("ty", "tx"))
    query_proj_grad = weight_grad(query_input, grad_queries)
    grad_latent_rows, query_gain_grad = back_query_norm(linear_back(grad_queries, query_proj))
    latent_grad = grad_one + grad_latent_rows
    summed = (
        lax.psum_scatter(query_gain_grad, "tx", scatter_dimension=0, tiled=True),
        lax.psum_scatter(query_proj_grad, "tx", scatter_dimension=0, tiled=True),
        lax.psum_scatter(cross_proj_grad, "tx", scatter_dimension=0, tiled=True),
        lax.psum_scatter(hidden_gain_grad, "tx", scatter_dimension=0, tiled=True),
        lax.psum_scatter(hidden_up_grad, "tx", scatter_dimension=0, tiled=True),
        lax.psum_scatter(hidden_down_grad, "tx", scatter_dimension=0, tiled=True),
        lax.psum_scatter(tower_gain_grad, "tx", scatter_dimension=0, tiled=True),
        lax.psum_scatter(tower_query_grad, "tx", scatter_dimension=0, tiled=True),
        lax.psum_scatter(tower_key_grad, "tx", scatter_dimension=0, tiled=True),
        lax.psum_scatter(tower_value_grad, "tx", scatter_dimension=0, tiled=True),
        lax.psum_scatter(tower_proj_grad, "tx", scatter_dimension=0, tiled=True),
        lax.psum_scatter(final_gain_grad, "tx", scatter_dimension=0, tiled=True),
        lax.psum_scatter(final_up_grad, "tx", scatter_dimension=0, tiled=True),
        lax.psum_scatter(final_down_grad, "tx", scatter_dimension=0, tiled=True),
    )
    return (
        resid_four.astype(BFLOAT),
        latent_grad,
        pixel_sums[2],
        summed[0],
        summed[1],
        pixel_sums[0],
        pixel_sums[1],
        summed[2],
        summed[3],
        summed[4],
        summed[5],
        summed[6],
        summed[7],
        summed[8],
        summed[9],
        summed[10],
        summed[11],
        summed[12],
        summed[13],
    )


def solution(mesh):
    in_specs = (
        P(None, None, "ty", "tx"),
        P(None, "ty", "tx"),
        P(),
        P(None, "tx", None),
        P(None, "tx", None),
        P(),
        P(),
        P(),
        P(),
        P(),
        P(),
        P(),
        P(),
        P(),
        P(),
        P(),
        P(),
        P(),
        P(),
        P(),
        P(),
        P(),
    )
    out_specs = (
        P(None, "tx", None),
        P(None, "tx", None),
        P(),
        P("tx"),
        P("tx", None),
        P(),
        P(),
        P("tx", None),
        P("tx"),
        P("tx", None),
        P("tx", None),
        P("tx"),
        P("tx", None),
        P("tx", None),
        P("tx", None),
        P("tx", None),
        P("tx"),
        P("tx", None),
        P("tx", None),
    )
    return jax.shard_map(
        on_device, mesh=mesh, in_specs=in_specs, out_specs=out_specs, check_vma=False
    )
```

profile of v0, /device:TPU:1, one launch (start us, length us, event | category | flops | bytes accessed | tf_op | source)
XLA Modules:
  0.0 1943.5 jit_solution(2078044388455915778)
XLA Ops:
  34.3 40.5 %concatenate.3 = f32[2,72,36,261]{3,0,2,1:T(2,128)} concatenate(f32[2,72,36,3]{3,0,2,1:T(2,128)} %copy.99, f32[2,72,36,1]{3,0,2,1:T(2,128)} %broadcast_in_dim.74, f32[2,72,36,1]{3,0,2,1:T(2,128)} %broadcast_in_dim.75, f32[2,72,36,64]{3,0,2,1:T(2,128)} %broadcast_in_dim.76, f32[2,72,36,64]{3,0,2,1:T(2,128)} %broadcast_in_dim.77, f32[2,72,36,64]{3,0,2,1:T(2,128)} %broadcast_in_dim.78, ...), dimensions={3} | concatenate | bytes 10824192 | tf_op jit(solution)/shard_map/concatenate | solution.py:71
  85.5 13.9 copy.101
  122.5 12.3 select_reduce_fusion
  134.8 40.5 %pmax.7 = f32[2,512]{1,0:T(2,128)S(1)} all-reduce(f32[2,512]{1,0:T(2,128)S(1)} %get-tuple-element.51), channel_id=1, replica_groups=mesh['ty'=4,'tx'=8] {'ty','tx'}, use_global_device_ids=true, to_apply=%region_9.10 | all-reduce | flops 1024 | bytes 8192 | tf_op jit(solution)/shard_map/pmax | solution.py:135
  181.2 40.2 %psum.49 = f32[2,512]{1,0:T(2,128)S(1)} all-reduce(f32[2,512]{1,0:T(2,128)S(1)} %fusion.2), channel_id=1, replica_groups=mesh['ty'=4,'tx'=8] {'ty','tx'}, use_global_device_ids=true, to_apply=%region_11.12 | all-reduce | flops 1024 | bytes 8192 | tf_op jit(solution)/shard_map/psum | solution.py:141
  221.4 12.3 fusion.4
  233.8 89.6 %reduce-scatter.15.cloned.1.call-done = f32[2,64,1024]{2,1,0:T(8,128)} async-done(((f32[2,512,1024]{2,1,0:T(8,128)}), f32[2,64,1024]{2,1,0:T(8,128)}) %reduce-scatter.15.cloned.1.call-update) | async-done | bytes 524304 | tf_op jit(solution)/shard_map/reduce_scatter | solution.py:146
  323.4 17.4 all-reduce.11
  351.8 43.2 %all-gather.9.cloned.1.call-done = bf16[2,512,1024]{2,1,0:T(8,128)(2,1)} async-done(((bf16[2,64,1024]{2,1,0:T(8,128)(2,1)}), bf16[2,512,1024]{2,1,0:T(8,128)(2,1)}) %all-gather.9.cloned.1.call-update) | async-done | bytes 2097168 | tf_op jit(solution)/shard_map/all_gather | solution.py:161
  400.8 44.9 %all-gather.7.cloned.1.call-done = bf16[2,512,1024]{2,1,0:T(8,128)(2,1)} async-done(((bf16[2,64,1024]{2,1,0:T(8,128)(2,1)}), bf16[2,512,1024]{2,1,0:T(8,128)(2,1)}) %all-gather.7.cloned.1.call-update) | async-done | bytes 2097168 | tf_op jit(solution)/shard_map/all_gather | solution.py:162
  485.9 71.9 %reduce-scatter.17.cloned.1.call-done = f32[2,64,1024]{2,1,0:T(8,128)} async-done(((f32[2,512,1024]{2,1,0:T(8,128)}), f32[2,64,1024]{2,1,0:T(8,128)}) %reduce-scatter.17.cloned.1.call-update) | async-done | bytes 524304 | tf_op jit(solution)/shard_map/reduce_scatter | solution.py:214
  561.5 87.5 %reduce-scatter.19.cloned.1.call-done = f32[2,64,1024]{2,1,0:T(8,128)} async-done(((f32[2,512,1024]{2,1,0:T(8,128)}), f32[2,64,1024]{2,1,0:T(8,128)}) %reduce-scatter.19.cloned.1.call-update) | async-done | bytes 524304 | tf_op jit(solution)/shard_map/reduce_scatter | solution.py:217
  658.0 48.0 %all-gather.11.cloned.1.call-done = bf16[2,512,1024]{2,1,0:T(8,128)(2,1)} async-done(((bf16[2,64,1024]{2,1,0:T(8,128)(2,1)}), bf16[2,512,1024]{2,1,0:T(8,128)(2,1)}) %all-gather.11.cloned.1.call-update) | async-done | bytes 2097168 | tf_op jit(solution)/shard_map/all_gather | solution.py:242
  706.0 15.0 multiply_reduce_fusion
  721.0 39.8 %psum.51 = f32[2,512]{1,0:T(2,128)S(1)} all-reduce(f32[2,512]{1,0:T(2,128)S(1)} %get-tuple-element.67), channel_id=1, replica_groups=mesh['ty'=4,'tx'=8] {'ty','tx'}, use_global_device_ids=true, to_apply=%region_32.33 | all-reduce | flops 1024 | bytes 8192 | tf_op jit(solution)/shard_map/psum | solution.py:256
  772.0 10.3 convolution_multiply_fusion
  798.1 11.2 multiply_convert_fusion
  816.6 10.6 convolution_convert_fusion
  852.4 19.1 reduce-scatter.21.cloned.1.call-done
  871.5 17.2 all-reduce.12
  909.4 40.8 %psum.53 = f32[261]{0:T(512)} all-reduce(f32[261]{0:T(512)S(1)} %multiply_reduce_fusion.2), channel_id=1, replica_groups=mesh['ty'=4,'tx'=8] {'ty','tx'}, use_global_device_ids=true, to_apply=%region_38.39 | all-reduce | flops 261 | bytes 2088 | tf_op jit(solution)/shard_map/psum | solution.py:275
  953.2 29.3 %all-reduce.5 = (f32[1024]{0:T(1024)S(1)}, f32[1024]{0:T(1024)S(1)}, f32[1024]{0:T(1024)S(1)}, f32[1024]{0:T(1024)S(1)}) all-reduce(f32[1024]{0:T(1024)S(1)} %get-tuple-element.25, f32[1024]{0:T(1024)S(1)} %copy-done.74, f32[1024]{0:T(1024)S(1)} %copy-done.73, f32[1024]{0:T(1024)S(1)} %copy-done.72), channel_id=6, replica_groups=mesh['ty'=4,'tx'=8] {'tx'}, use_global_device_ids=true, to_apply=%region_40.41.clone | all-reduce | flops 4096 | bytes 32768
  987.1 69.3 %reduce-scatter.37.cloned.1.call-done = f32[128,1024]{1,0:T(8,128)} async-done(((f32[1024,1024]{1,0:T(8,128)}), f32[128,1024]{1,0:T(8,128)}) %reduce-scatter.37.cloned.1.call-update) | async-done | bytes 524304 | tf_op jit(solution)/shard_map/reduce_scatter | solution.py:290
  1056.4 91.9 %reduce-scatter.39.cloned.1.call-done = f32[128,1024]{1,0:T(8,128)} async-done(((f32[1024,1024]{1,0:T(8,128)}), f32[128,1024]{1,0:T(8,128)}) %reduce-scatter.39.cloned.1.call-update) | async-done | bytes 524304 | tf_op jit(solution)/shard_map/reduce_scatter | solution.py:292
  1148.3 92.3 %reduce-scatter.41.cloned.1.call-done = f32[128,1024]{1,0:T(8,128)} async-done(((f32[1024,1024]{1,0:T(8,128)}), f32[128,1024]{1,0:T(8,128)}) %reduce-scatter.41.cloned.1.call-update) | async-done | bytes 524304 | tf_op jit(solution)/shard_map/reduce_scatter | solution.py:293
  1240.6 140.2 %all-reduce.10.cloned.1.call-done = (f32[261,1024]{1,0:T(8,128)}, f32[261,1024]{1,0:T(8,128)}) async-done(((f32[261,1024]{1,0:T(8,128)}, f32[261,1024]{1,0:T(8,128)}), (f32[261,1024]{1,0:T(8,128)}, f32[261,1024]{1,0:T(8,128)})) %all-reduce.10.cloned.1.call-update) | async-done | bytes 2138128 | tf_op jit(solution)/shard_map/psum | solution.py:275
  1380.8 92.5 %reduce-scatter.25.cloned.1.call-done = f32[128,1024]{1,0:T(8,128)} async-done(((f32[1024,1024]{1,0:T(8,128)}), f32[128,1024]{1,0:T(8,128)}) %reduce-scatter.25.cloned.1.call-update) | async-done | bytes 524304 | tf_op jit(solution)/shard_map/reduce_scatter | solution.py:282
  1473.3 91.7 %reduce-scatter.27.cloned.1.call-done = f32[128,1024]{1,0:T(8,128)} async-done(((f32[1024,1024]{1,0:T(8,128)}), f32[128,1024]{1,0:T(8,128)}) %reduce-scatter.27.cloned.1.call-update) | async-done | bytes 524304 | tf_op jit(solution)/shard_map/reduce_scatter | solution.py:284
  1565.0 92.2 %reduce-scatter.29.cloned.1.call-done = f32[128,1024]{1,0:T(8,128)} async-done(((f32[1024,1024]{1,0:T(8,128)}), f32[128,1024]{1,0:T(8,128)}) %reduce-scatter.29.cloned.1.call-update) | async-done | bytes 524304 | tf_op jit(solution)/shard_map/reduce_scatter | solution.py:285
  1657.2 91.9 %reduce-scatter.33.cloned.1.call-done = f32[128,1024]{1,0:T(8,128)} async-done(((f32[1024,1024]{1,0:T(8,128)}), f32[128,1024]{1,0:T(8,128)}) %reduce-scatter.33.cloned.1.call-update) | async-done | bytes 524304 | tf_op jit(solution)/shard_map/reduce_scatter | solution.py:288
  1749.1 92.2 %reduce-scatter.35.cloned.1.call-done = f32[128,1024]{1,0:T(8,128)} async-done(((f32[1024,1024]{1,0:T(8,128)}), f32[128,1024]{1,0:T(8,128)}) %reduce-scatter.35.cloned.1.call-update) | async-done | bytes 524304 | tf_op jit(solution)/shard_map/reduce_scatter | solution.py:289
  1841.3 92.1 %reduce-scatter.23.cloned.1.call-done = f32[128,1024]{1,0:T(8,128)} async-done(((f32[1024,1024]{1,0:T(8,128)}), f32[128,1024]{1,0:T(8,128)}) %reduce-scatter.23.cloned.1.call-update) | async-done | bytes 524304 | tf_op jit(solution)/shard_map/reduce_scatter | solution.py:281
  (352 shorter events, 225.6 us)
Async XLA Ops:
  7.2 445.9 %copy-start = (bf16[1024,1024]{1,0:T(8,128)(2,1)S(1)}, bf16[1024,1024]{1,0:T(8,128)(2,1)}, u32[]{:S(2)}) copy-start(bf16[1024,1024]{1,0:T(8,128)(2,1)} %param.42) | copy-start | bytes 6291460
  7.2 115.3 %all-gather.5.cloned.1.call-start = ((), (), s32[]{:S(2)}) async-start(), calls=%async_computation.14 | async-start | bytes 2359296 | tf_op jit(solution)/shard_map/all_gather | solution.py:129
  12.6 310.8 %reduce-scatter.15.cloned.1.call-start = ((), (), s32[]{:S(2)}) async-start(), calls=%async_computation.15 | async-start | bytes 4718592 | tf_op jit(solution)/shard_map/reduce_scatter | solution.py:146
  233.7 107.1 %copy-start.4 = (bf16[2,64,1024]{2,1,0:T(8,128)(2,1)S(1)}, bf16[2,64,1024]{2,1,0:T(8,128)(2,1)}, u32[]{:S(2)}) copy-start(bf16[2,64,1024]{2,1,0:T(8,128)(2,1)} %param.25) | copy-start | bytes 786436
  233.7 109.6 %copy-start.66 = (f32[1024]{0:T(1024)S(1)}, f32[1024]{0:T(1024)}, u32[]{:S(2)}) copy-start(f32[1024]{0:T(1024)} %param.33) | copy-start | bytes 12292
  233.8 161.3 %all-gather.9.cloned.1.call-start = ((), (), s32[]{:S(2)}) async-start(), calls=%async_computation.17 | async-start | bytes 2359296 | tf_op jit(solution)/shard_map/all_gather | solution.py:161
  346.9 98.8 %all-gather.7.cloned.1.call-start = ((), (), s32[]{:S(2)}) async-start(), calls=%async_computation.16 | async-start | bytes 2359296 | tf_op jit(solution)/shard_map/all_gather | solution.py:162
  349.7 208.1 %reduce-scatter.17.cloned.1.call-start = ((), (), s32[]{:S(2)}) async-start(), calls=%async_computation.18 | async-start | bytes 4718592 | tf_op jit(solution)/shard_map/reduce_scatter | solution.py:214
  351.8 49.0 %copy-start.41 = (bf16[2,8,8,8,128]{4,3,2,1,0:T(8,128)(2,1)}, bf16[2,8,8,8,128]{4,3,2,1,0:T(8,128)(2,1)S(1)}, u32[]{:S(2)}) copy-start(bf16[2,8,8,8,128]{4,3,2,1,0:T(8,128)(2,1)S(1)} %fusion.110) | copy-start | bytes 786436
  470.1 178.9 %reduce-scatter.19.cloned.1.call-start = ((), (), s32[]{:S(2)}) async-start(), calls=%async_computation.19 | async-start | bytes 4718592 | tf_op jit(solution)/shard_map/reduce_scatter | solution.py:217
  482.5 75.3 %copy-start.8 = (bf16[1024,1024]{1,0:T(8,128)(2,1)S(1)}, bf16[1024,1024]{1,0:T(8,128)(2,1)}, u32[]{:S(2)}) copy-start(bf16[1024,1024]{1,0:T(8,128)(2,1)} %param.38) | copy-start | bytes 6291460
  482.5 223.5 %all-gather.11.cloned.1.call-start = ((), (), s32[]{:S(2)}) async-start(), calls=%async_computation.20 | async-start | bytes 2359296 | tf_op jit(solution)/shard_map/all_gather | solution.py:242
  559.9 89.1 %copy-start.9 = (bf16[1024,1024]{1,0:T(8,128)(2,1)S(1)}, bf16[1024,1024]{1,0:T(8,128)(2,1)}, u32[]{:S(2)}) copy-start(bf16[1024,1024]{1,0:T(8,128)(2,1)} %param.39) | copy-start | bytes 6291460
  652.5 188.5 %copy-start.17 = (f32[2,64,1024]{2,1,0:T(8,128)}, f32[2,64,1024]{2,1,0:T(8,128)S(1)}, u32[]{:S(2)}) copy-start(f32[2,64,1024]{2,1,0:T(8,128)S(1)} %add_add_fusion.6) | copy-start | bytes 1572868
  656.2 64.8 %copy-start.22 = (f32[2,64,1024]{2,1,0:T(8,128)}, f32[2,64,1024]{2,1,0:T(8,128)S(1)}, u32[]{:S(2)}) copy-start(f32[2,64,1024]{2,1,0:T(8,128)S(1)} %get-tuple-element.38) | copy-start | bytes 1572868
  656.2 64.8 %copy-start.77 = (f32[2,64]{1,0:T(2,128)}, f32[2,64]{1,0:T(2,128)S(1)}, u32[]{:S(2)}) copy-start(f32[2,64]{1,0:T(2,128)S(1)} %negate_multiply_fusion.1) | copy-start | bytes 1540
  657.9 213.5 %reduce-scatter.21.cloned.1.call-start = ((), (), s32[]{:S(2)}) async-start(), calls=%async_computation.21 | async-start | bytes 4718592 | tf_op jit(solution)/shard_map/reduce_scatter | solution.py:262
  782.4 204.7 %reduce-scatter.31.cloned.1.call-start = ((), (), s32[]{:S(2)}) async-start(), calls=%async_computation.26 | async-start | bytes 4718592 | tf_op jit(solution)/shard_map/reduce_scatter | solution.py:287
  786.3 270.1 %reduce-scatter.37.cloned.1.call-start = ((), (), s32[]{:S(2)}) async-start(), calls=%async_computation.29 | async-start | bytes 4718592 | tf_op jit(solution)/shard_map/reduce_scatter | solution.py:290
  790.0 358.3 %reduce-scatter.39.cloned.1.call-start = ((), (), s32[]{:S(2)}) async-start(), calls=%async_computation.30 | async-start | bytes 4718592 | tf_op jit(solution)/shard_map/reduce_scatter | solution.py:292
  793.8 446.9 %reduce-scatter.41.cloned.1.call-start = ((), (), s32[]{:S(2)}) async-start(), calls=%async_computation.31 | async-start | bytes 4718592 | tf_op jit(solution)/shard_map/reduce_scatter | solution.py:293
  797.6 583.2 %all-reduce.10.cloned.1.call-start = ((), (), s32[]{:S(2)}) async-start(), calls=%async_computation.32 | async-start | bytes 4325376 | tf_op jit(solution)/shard_map/psum | solution.py:275
  834.4 638.9 %reduce-scatter.25.cloned.1.call-start = ((), (), s32[]{:S(2)}) async-start(), calls=%async_computation.23 | async-start | bytes 4718592 | tf_op jit(solution)/shard_map/reduce_scatter | solution.py:282
  837.2 727.8 %reduce-scatter.27.cloned.1.call-start = ((), (), s32[]{:S(2)}) async-start(), calls=%async_computation.24 | async-start | bytes 4718592 | tf_op jit(solution)/shard_map/reduce_scatter | solution.py:284
  840.9 816.3 %reduce-scatter.29.cloned.1.call-start = ((), (), s32[]{:S(2)}) async-start(), calls=%async_computation.25 | async-start | bytes 4718592 | tf_op jit(solution)/shard_map/reduce_scatter | solution.py:285
  844.7 904.4 %reduce-scatter.33.cloned.1.call-start = ((), (), s32[]{:S(2)}) async-start(), calls=%async_computation.27 | async-start | bytes 4718592 | tf_op jit(solution)/shard_map/reduce_scatter | solution.py:288
  848.6 992.7 %reduce-scatter.35.cloned.1.call-start = ((), (), s32[]{:S(2)}) async-start(), calls=%async_computation.28 | async-start | bytes 4718592 | tf_op jit(solution)/shard_map/reduce_scatter | solution.py:289
  852.3 1081.1 %reduce-scatter.23.cloned.1.call-start = ((), (), s32[]{:S(2)}) async-start(), calls=%async_computation.22 | async-start | bytes 4718592 | tf_op jit(solution)/shard_map/reduce_scatter | solution.py:281
  909.3 75.5 %copy-start.18 = (f32[2,64,1024]{2,1,0:T(8,128)S(1)}, f32[2,64,1024]{2,1,0:T(8,128)}, u32[]{:S(2)}) copy-start(f32[2,64,1024]{2,1,0:T(8,128)} %copy-done.17) | copy-start | bytes 1572868
  909.3 75.5 %copy-start.23 = (f32[2,64,1024]{2,1,0:T(8,128)S(1)}, f32[2,64,1024]{2,1,0:T(8,128)}, u32[]{:S(2)}) copy-start(f32[2,64,1024]{2,1,0:T(8,128)} %copy-done.22) | copy-start | bytes 1572868
  909.3 75.5 %copy-start.78 = (f32[2,64]{1,0:T(2,128)S(1)}, f32[2,64]{1,0:T(2,128)}, u32[]{:S(2)}) copy-start(f32[2,64]{1,0:T(2,128)} %copy-done.77) | copy-start | bytes 1540
  984.8 952.0 %copy-start.1 = (bf16[1024,1024]{1,0:T(8,128)(2,1)S(1)}, bf16[1024,1024]{1,0:T(8,128)(2,1)}, u32[]{:S(2)}) copy-start(bf16[1024,1024]{1,0:T(8,128)(2,1)} %param.42) | copy-start | bytes 6291460
  (80 other events, 646.2 us)
Sparse Core Ops, SparseCore 0:
  12.7 50.2 all-gather.4
  233.9 89.4 reduce-scatter.14
  347.0 47.9 all-gather.8
  397.9 47.7 all-gather.6
  470.2 87.5 reduce-scatter.16
  561.3 87.6 reduce-scatter.18
  658.1 47.8 all-gather.10
  782.5 88.9 reduce-scatter.20
  875.7 88.2 reduce-scatter.30
  968.5 87.8 reduce-scatter.36
  1060.6 87.6 reduce-scatter.38
  1152.8 87.7 reduce-scatter.40
  1247.0 133.8 all-reduce.9
  1385.3 87.9 reduce-scatter.24
  1477.4 87.6 reduce-scatter.26
  1569.5 87.6 reduce-scatter.28
  1661.3 87.8 reduce-scatter.32
  1753.6 87.6 reduce-scatter.34
  1845.5 87.8 reduce-scatter.22
where the time goes:
time: 1950 us; the launch traced here: 1940 us
  waiting for transfers between devices  1350 us (69%)
  blocking collectives  225 us (12%)
  matrix products  197 us (10%)
  local copies, waits for them, and re-layouts  111 us (6%)
  other arithmetic  42.5 us (2%)
    psum x1, waiting for transfers between devices, on_device(): lax.psum((key_proj_grad, value_proj_grad, feature_part), ('ty', 'tx'))  140 us
    reduce_scatter x1, waiting for transfers between devices, on_device(): lax.psum_scatter(cross_proj_grad, 'tx', scatter_dimension=0, tiled=True)  92.5 us
    reduce_scatter x1, waiting for transfers between devices, on_device(): lax.psum_scatter(final_down_grad, 'tx', scatter_dimension=0, tiled=True)  92.3 us
    reduce_scatter x1, waiting for transfers between devices, on_device(): lax.psum_scatter(hidden_down_grad, 'tx', scatter_dimension=0, tiled=True)  92.2 us
    reduce_scatter x1, waiting for transfers between devices, on_device(): lax.psum_scatter(tower_value_grad, 'tx', scatter_dimension=0, tiled=True)  92.2 us
    reduce_scatter x1, waiting for transfers between devices, on_device(): lax.psum_scatter(query_proj_grad, 'tx', scatter_dimension=0, tiled=True)  92.1 us
    reduce_scatter x1, waiting for transfers between devices, on_device(): lax.psum_scatter(tower_key_grad, 'tx', scatter_dimension=0, tiled=True)  91.9 us
    reduce_scatter x1, waiting for transfers between devices, on_device(): lax.psum_scatter(final_up_grad, 'tx', scatter_dimension=0, tiled=True)  91.9 us
  transfers between devices with their start and end apart: 19, of which 17 were waited for; matrix products, arithmetic and copies ran while one was open for 12% of the time, Pallas kernels for 0%

commit v1 on v0

--- a/solution.py
+++ b/solution.py
@@ -3,6 +3,8 @@
 import jax
 import jax.numpy as jnp
 from jax import lax
+from jax.experimental import pallas as pl
+from jax.experimental.pallas import tpu as pltpu
 from jax.sharding import PartitionSpec as P
 
 BANDS = 64
@@ -47,28 +49,477 @@
     )
 
 
-def pixel_features(pixels, image_sizes, row_ids, col_ids):
+def axis_tables(image_sizes, ids, coord_lane, first_lane):
+    side = image_sizes.astype(FLOAT)[:, None]
+    coord = -1.0 + 2.0 * ids.astype(FLOAT)[None, :] / (side - 1.0)
+    band = jnp.arange(BANDS, dtype=jnp.int32).astype(FLOAT)
+    frequency = 1.0 + band[None, :] * (side * 0.5 - 1.0) / (BANDS - 1)
+    angle = math.pi * coord[:, :, None] * frequency[:, None, :]
+    waves = jnp.concatenate([jnp.sin(angle), jnp.cos(angle)], axis=2)
+    count, length = coord.shape
+    lead = jnp.zeros((count, length, coord_lane), FLOAT)
+    gap = jnp.zeros((count, length, first_lane - coord_lane - 1), FLOAT)
+    tail = jnp.zeros((count, length, FEAT - first_lane - 2 * BANDS), FLOAT)
+    table = jnp.concatenate([lead, coord[:, :, None], gap, waves, tail], axis=2)
+    return table, coord, jnp.sum(waves, axis=2) + coord
+
+
+MESH = pl.DeviceIdType.MESH
+
+
+def peer_ty(ty, d):
+    return lax.rem(ty + d, lax.axis_size("ty"))
+
+
+def send(src, dst, send_sem, recv_sem, where):
+    copy = pltpu.make_async_remote_copy(
+        src_ref=src, dst_ref=dst, send_sem=send_sem, recv_sem=recv_sem,
+        device_id=where, device_id_type=MESH,
+    )
+    copy.start()
+    return copy
+
+
+def greet(places):
+    barrier = pltpu.get_barrier_semaphore()
+    for place in places:
+        pl.semaphore_signal(barrier, inc=1, device_id=place, device_id_type=MESH)
+    pl.semaphore_wait(barrier, len(places))
+
+
+def column_chunk(ref, index, width):
+    return ref[:, pl.ds(pl.multiple_of(index * width, width), width)]
+
+
+def outer(left, right):
+    return lax.dot_general(left, right, (((0,), (0,)), ((), ())), preferred_element_type=FLOAT)
+
+
+def weight_sums_kernel(
+    x_ref, g_ref, out_ref,
+    xs, gs, ysend, yrecv, own, zsend, zrecv, last,
+    local_sem, xg_send, xg_recv, y_send, y_recv, z_send, z_recv, o_send, o_recv,
+):
+    ty, tx = lax.axis_index("ty"), lax.axis_index("tx")
+    z, y = tx // 2, lax.rem(tx, 2)
+    tys = [{"ty": lax.rem(ty + d, 4), "tx": tx} for d in (1, 2, 3)]
+    beside = {"ty": ty, "tx": 2 * z + 1 - y}
+    zs = [{"ty": ty, "tx": 2 * lax.rem(z + d, 4) + y} for d in (1, 2, 3)]
+    greet(tys + [beside] + zs)
+    rows = x_ref.shape[1]
+    started = []
+    gathers = [[], []]
+    for k in range(2):
+        for s, (src, dst) in enumerate(((x_ref, xs), (g_ref, gs))):
+            for d in (1, 2, 3):
+                gathers[k].append(send(
+                    src.at[4 * k + lax.rem(ty + d, 4)], dst.at[k, ty],
+                    xg_send.at[k, s, d - 1], xg_recv.at[k, s, d - 1], tys[d - 1],
+                ))
+            mine = pltpu.make_async_copy(src.at[4 * k + ty], dst.at[k, ty], local_sem.at[k, s])
+            mine.start()
+            gathers[k].append(mine)
+    ycopies = [[], []]
+    for k in range(2):
+        for copy in gathers[k]:
+            copy.wait()
+        gk = gs[k].reshape(4 * rows, -1)
+        for c in range(4):
+            part = xs[k, :, :, pl.ds(pl.multiple_of((2 * c + 1 - y) * 128, 128), 128)]
+            ysend[k, c] = outer(part.reshape(4 * rows, 128), gk).astype(BFLOAT)
+            ycopies[k].append(send(
+                ysend.at[k, c], yrecv.at[k, c], y_send.at[k, c], y_recv.at[k, c], beside
+            ))
+        for c in range(4):
+            at = lax.rem(z + c, 4)
+            part = xs[k, :, :, pl.ds(pl.multiple_of((2 * at + y) * 128, 128), 128)]
+            own[k, c] = outer(part.reshape(4 * rows, 128), gk)
+    zcopies = [[], []]
+    for k in range(2):
+        for copy in ycopies[k]:
+            copy.wait()
+        for c in (1, 2, 3, 0):
+            at = lax.rem(z + c, 4)
+            total = own[k, c] + yrecv[k, at].astype(FLOAT)
+            if c == 0:
+                own[k, c] = total
+            else:
+                zsend[k, c - 1] = total.astype(BFLOAT)
+                zcopies[k].append(send(
+                    zsend.at[k, c - 1], zrecv.at[k, c - 1],
+                    z_send.at[k, c - 1], z_recv.at[k, c - 1], zs[c - 1],
+                ))
+    for k in range(2):
+        for copy in zcopies[k]:
+            copy.wait()
+        total = own[k, 0]
+        for c in range(3):
+            total = total + zrecv[k, c].astype(FLOAT)
+        last[k] = total.astype(BFLOAT)
+        for d in (1, 2, 3):
+            started.append(send(
+                last.at[k], out_ref.at[4 * k + ty], o_send.at[k, d - 1], o_recv.at[k, d - 1],
+                tys[d - 1],
+            ))
+        mine = pltpu.make_async_copy(last.at[k], out_ref.at[4 * k + ty], local_sem.at[k, 0])
+        mine.start()
+        started.append(mine)
+    for copy in started:
+        copy.wait()
+
+
+def weight_sums(x, g):
+    count, rows, width = x.shape
+    dma = pltpu.SemaphoreType.DMA
+    block = (width // 8, width)
+    return pl.pallas_call(
+        weight_sums_kernel,
+        out_shape=jax.ShapeDtypeStruct((count,) + block, BFLOAT),
+        in_specs=[pl.BlockSpec(memory_space=pl.ANY)] * 2,
+        out_specs=pl.BlockSpec(memory_space=pl.ANY),
+        scratch_shapes=[
+            pltpu.VMEM((2, 4, rows, width), BFLOAT),
+            pltpu.VMEM((2, 4, rows, width), BFLOAT),
+            pltpu.VMEM((2, 4) + block, BFLOAT),
+            pltpu.VMEM((2, 4) + block, BFLOAT),
+            pltpu.VMEM((2, 4) + block, FLOAT),
+            pltpu.VMEM((2, 3) + block, BFLOAT),
+            pltpu.VMEM((2, 3) + block, BFLOAT),
+            pltpu.VMEM((2,) + block, BFLOAT),
+            dma((2, 2)), dma((2, 2, 3)), dma((2, 2, 3)), dma((2, 4)), dma((2, 4)),
+            dma((2, 3)), dma((2, 3)), dma((2, 3)), dma((2, 3)),
+        ],
+        compiler_params=pltpu.CompilerParams(
+            collective_id=1, has_side_effects=True, vmem_limit_bytes=48 << 20
+        ),
+        name="weight_sums",
+    )(x, g)
+
+
+def all_sum_kernel(
+    v_ref, out_ref, recv1, quarter, recv2, recv3, s1, r1, s2, r2, s3, r3, s4, r4, local_sem
+):
+    ty, tx = lax.axis_index("ty"), lax.axis_index("tx")
+    tys = [{"ty": lax.rem(ty + d, 4), "tx": tx} for d in (1, 2, 3)]
+    txs = [{"ty": ty, "tx": lax.rem(tx + d, 8)} for d in range(1, 8)]
+    greet(tys + txs)
+    copies = [
+        send(v_ref.at[lax.rem(ty + d, 4)], recv1.at[d - 1], s1.at[d - 1], r1.at[d - 1], tys[d - 1])
+        for d in (1, 2, 3)
+    ]
+    total = v_ref[ty].astype(FLOAT)
+    for d, copy in enumerate(copies):
+        copy.wait()
+        total = total + recv1[d].astype(FLOAT)
+    for c in range(8):
+        quarter[c] = total[:, c * 128 : c * 128 + 128].astype(BFLOAT)
+    copies = [
+        send(quarter.at[lax.rem(tx + d, 8)], recv2.at[d - 1], s2.at[d - 1], r2.at[d - 1], txs[d - 1])
+        for d in range(1, 8)
+    ]
+    total = quarter[tx].astype(FLOAT)
+    for d, copy in enumerate(copies):
+        copy.wait()
+        total = total + recv2[d].astype(FLOAT)
+    recv3[tx] = total.astype(BFLOAT)
+    copies = [
+        send(recv3.at[tx], recv3.at[tx], s3.at[d - 1], r3.at[d - 1], txs[d - 1])
+        for d in range(1, 8)
+    ]
+    for copy in copies:
+        copy.wait()
+    copies = [
+        send(recv3, out_ref.at[ty], s4.at[d - 1], r4.at[d - 1], tys[d - 1]) for d in (1, 2, 3)
+    ]
+    mine = pltpu.make_async_copy(recv3, out_ref.at[ty], local_sem)
+    mine.start()
+    for copy in copies + [mine]:
+        copy.wait()
+
+
+def all_sum(v):
+    rows, width = v.shape
+    part = rows // 4
+    dma = pltpu.SemaphoreType.DMA
+    out = pl.pallas_call(
+        all_sum_kernel,
+        out_shape=jax.ShapeDtypeStruct((4, 8, part, 128), BFLOAT),
+        in_specs=[pl.BlockSpec(memory_space=pltpu.VMEM)],
+        out_specs=pl.BlockSpec(memory_space=pl.ANY),
+        scratch_shapes=[
+            pltpu.VMEM((3, part, width), BFLOAT),
+            pltpu.VMEM((8, part, 128), BFLOAT),
+            pltpu.VMEM((7, part, 128), BFLOAT),
+            pltpu.VMEM((8, part, 128), BFLOAT),
+            dma((3,)), dma((3,)), dma((7,)), dma((7,)), dma((7,)), dma((7,)), dma((3,)), dma((3,)),
+            dma(()),
+        ],
+        compiler_params=pltpu.CompilerParams(
+            collective_id=2, has_side_effects=True, vmem_limit_bytes=32 << 20
+        ),
+        name="all_sum",
+    )(v.reshape(4, part, width))
+    return jnp.transpose(out, (0, 2, 1, 3)).reshape(rows, width)
+
+
+def on_device_fast(
+    pixels,
+    pixel_mask,
+    image_sizes,
+    latents,
+    cotangent,
+    feature_gain,
+    query_gain,
+    query_proj,
+    key_proj,
+    value_proj,
+    cross_proj,
+    hidden_gain,
+    hidden_up,
+    hidden_down,
+    tower_gain,
+    tower_query,
+    tower_key,
+    tower_value,
+    tower_proj,
+    final_gain,
+    final_up,
+    final_down,
+):
     item_count = pixels.shape[0]
     tile_height = pixels.shape[2]
     tile_width = pixels.shape[3]
-    image_side = image_sizes.astype(FLOAT)[:, None]
-    ycoord = -1.0 + 2.0 * row_ids.astype(FLOAT)[None, :] / (image_side - 1.0)
-    xcoord = -1.0 + 2.0 * col_ids.astype(FLOAT)[None, :] / (image_side - 1.0)
-    band_index = jnp.arange(BANDS, dtype=jnp.int32).astype(FLOAT)
-    frequency = 1.0 + band_index[None, :] * (image_side * 0.5 - 1.0) / (BANDS - 1)
-    yangle = math.pi * ycoord[:, :, None] * frequency[:, None, :]
-    xangle = math.pi * xcoord[:, :, None] * frequency[:, None, :]
-    tile_shape = (item_count, tile_height, tile_width)
-    pieces = [
-        jnp.transpose(pixels, (0, 2, 3, 1)).astype(FLOAT),
-        jnp.broadcast_to(ycoord[:, :, None, None], tile_shape + (1,)),
-        jnp.broadcast_to(xcoord[:, None, :, None], tile_shape + (1,)),
-        jnp.broadcast_to(jnp.sin(yangle)[:, :, None, :], tile_shape + (BANDS,)),
-        jnp.broadcast_to(jnp.cos(yangle)[:, :, None, :], tile_shape + (BANDS,)),
-        jnp.broadcast_to(jnp.sin(xangle)[:, None, :, :], tile_shape + (BANDS,)),
-        jnp.broadcast_to(jnp.cos(xangle)[:, None, :, :], tile_shape + (BANDS,)),
+    model_width = latents.shape[2]
+    rows_here = latents.shape[1]
+    head_count = HEADS
+    head_size = model_width // head_count
+    cross_scale = 1.0 / math.sqrt(model_width)
+    tower_scale = 1.0 / math.sqrt(head_size)
+    row_ids = lax.axis_index("ty") * tile_height + jnp.arange(tile_height, dtype=jnp.int32)
+    col_ids = lax.axis_index("tx") * tile_width + jnp.arange(tile_width, dtype=jnp.int32)
+    all_cols = jnp.arange(tile_width * lax.axis_size("tx"), dtype=jnp.int32)
+    wide_pixels = lax.all_gather(pixels, "tx", axis=3, tiled=True).astype(FLOAT)
+    wide_mask = lax.all_gather(pixel_mask, "tx", axis=2, tiled=True)
+    side_sizes = image_sizes[:, None, None]
+    live = (
+        (wide_mask > 0)
+        & (row_ids[None, :, None] < side_sizes)
+        & (all_cols[None, None, :] < side_sizes)
+    )[:, None]
+    row_table, row_coord, row_sum = axis_tables(image_sizes, row_ids, 3, 5)
+    col_table, col_coord, col_sum = axis_tables(image_sizes, all_cols, 4, 5 + 2 * BANDS)
+    pixel_mean = (
+        jnp.sum(wide_pixels, axis=1) + row_sum[:, :, None] + col_sum[:, None, :]
+    ) / FEAT
+    pixel_square = (
+        jnp.sum(wide_pixels * wide_pixels, axis=1)
+        + (row_coord * row_coord)[:, :, None]
+        + (col_coord * col_coord)[:, None, :]
+        + 2.0 * BANDS
+    ) / FEAT
+    pixel_rate = lax.rsqrt(pixel_square - pixel_mean * pixel_mean + EPSILON)
+    exact = lax.Precision.HIGHEST
+
+    def against_pixels(coefs):
+        by_row = jnp.einsum("blf,bif->bli", coefs, row_table, precision=exact)
+        by_col = jnp.einsum("blf,bjf->blj", coefs, col_table, precision=exact)
+        total = by_row[:, :, :, None] + by_col[:, :, None, :]
+        for c in range(3):
+            total = total + coefs[:, :, c][:, :, None, None] * wide_pixels[:, None, c]
+        total = total - jnp.sum(coefs, axis=2)[:, :, None, None] * pixel_mean[:, None]
+        return total * pixel_rate[:, None]
+
+    def over_pixels(weights):
+        scaled = weights * pixel_rate[:, None]
+        by_row = jnp.sum(scaled, axis=3)
+        by_col = jnp.sum(scaled, axis=2)
+        total = jnp.einsum("bli,bif->blf", by_row, row_table, precision=exact)
+        total = total + jnp.einsum("blj,bjf->blf", by_col, col_table, precision=exact)
+        colour = jnp.stack(
+            [jnp.sum(scaled * wide_pixels[:, None, c], axis=(2, 3)) for c in range(3)], axis=2
+        )
+        total = total + jnp.pad(colour, ((0, 0), (0, 0), (0, FEAT - 3)))
+        return total - jnp.sum(scaled * pixel_mean[:, None], axis=(2, 3))[:, :, None]
+
+    latent_rows = latents.astype(FLOAT)
+    query_normed, back_query_norm = jax.vjp(layer_norm, latent_rows, query_gain)
+    query_input = query_normed.astype(BFLOAT)
+    own_queries = linear(query_input, query_proj).astype(BFLOAT)
+    raw_query = linear_back(own_queries, key_proj) * cross_scale
+    scores = against_pixels(raw_query * feature_gain)
+    row_top = jnp.max(jnp.where(live, scores, -1e30), axis=(2, 3))
+    all_top = lax.pmax(row_top, "ty")
+    row_exp = jnp.where(live, jnp.exp(scores - all_top[:, :, None, None]), 0.0)
+    row_total = lax.psum(jnp.sum(row_exp, axis=(2, 3)), "ty")
+    cross_exact = row_exp / row_total[:, :, None, None]
+    raw_mix = lax.psum(over_pixels(cross_exact), "ty")
+    mix = raw_mix * feature_gain
+    attended = linear(mix.astype(BFLOAT), value_proj)
+    attended_input = attended.astype(BFLOAT)
+    resid_one = latent_rows + linear(attended_input, cross_proj)
+    hidden_normed, back_hidden_norm = jax.vjp(layer_norm, resid_one, hidden_gain)
+    hidden_input = hidden_normed.astype(BFLOAT)
+    hidden_lifted, back_hidden_gelu = jax.vjp(gelu_tanh, linear(hidden_input, hidden_up))
+    hidden_act = hidden_lifted.astype(BFLOAT)
+    resid_two = resid_one + linear(hidden_act, hidden_down)
+    tower_normed, back_tower_norm = jax.vjp(layer_norm, resid_two, tower_gain)
+    tower_input = tower_normed.astype(BFLOAT)
+    tower_q = linear(tower_input, tower_query).astype(BFLOAT)
+    tower_k = linear(tower_input, tower_key).astype(BFLOAT)
+    tower_v = linear(tower_input, tower_value).astype(BFLOAT)
+    all_keys, all_values = (
+        lax.all_gather(tower_k, "tx", axis=1, tiled=True),
+        lax.all_gather(tower_v, "tx", axis=1, tiled=True),
+    )
+    split_q = tower_q.reshape(item_count, rows_here, head_count, head_size)
+    split_k = all_keys.reshape(item_count, -1, head_count, head_size)
+    split_v = all_values.reshape(item_count, -1, head_count, head_size)
+    tower_scores = (
+        jnp.einsum("bqhd,bkhd->bhqk", split_q, split_k, preferred_element_type=FLOAT) * tower_scale
+    )
+    tower_top = jnp.max(tower_scores, axis=3, keepdims=True)
+    tower_exp = jnp.exp(tower_scores - tower_top)
+    tower_total = jnp.sum(tower_exp, axis=3, keepdims=True)
+    tower_exact = tower_exp / tower_total
+    tower_probs = tower_exact.astype(BFLOAT)
+    mixed = jnp.einsum(
+        "bhqk,bkhd->bqhd", tower_probs, split_v, preferred_element_type=FLOAT
+    ).reshape(item_count, rows_here, model_width)
+    mixed_input = mixed.astype(BFLOAT)
+    resid_three = resid_two + linear(mixed_input, tower_proj)
+    final_normed, back_final_norm = jax.vjp(layer_norm, resid_three, final_gain)
+    final_input = final_normed.astype(BFLOAT)
+    final_lifted, back_final_gelu = jax.vjp(gelu_tanh, linear(final_input, final_up))
+    final_act = final_lifted.astype(BFLOAT)
+    resid_four = resid_three + linear(final_act, final_down)
+    grad_four = cotangent.astype(FLOAT)
+    grad_final_lift = back_final_gelu(linear_back(cotangent, final_down))[0].astype(BFLOAT)
+    grad_rows_three, final_gain_grad = back_final_norm(linear_back(grad_final_lift, final_up))
+    grad_three = grad_four + grad_rows_three
+    grad_tower_out = grad_three.astype(BFLOAT)
+    grad_mixed_flat = linear_back(grad_tower_out, tower_proj).astype(BFLOAT)
+    grad_mixed = grad_mixed_flat.reshape(item_count, rows_here, head_count, head_size)
+    grad_tower_p = jnp.einsum("bqhd,bkhd->bhqk", grad_mixed, split_v, preferred_element_type=FLOAT)
+    tower_delta = jnp.sum(tower_exact * grad_tower_p, axis=3, keepdims=True)
+    grad_tower_scores = (tower_exact * (grad_tower_p - tower_delta)).astype(BFLOAT)
+    grad_tower_q = (
+        (
+            jnp.einsum("bhqk,bkhd->bqhd", grad_tower_scores, split_k, preferred_element_type=FLOAT)
+            * tower_scale
+        )
+        .astype(BFLOAT)
+        .reshape(item_count, rows_here, model_width)
+    )
+    value_part = jnp.einsum(
+        "bhqk,bqhd->bkhd", tower_probs, grad_mixed, preferred_element_type=FLOAT
+    )
+    key_part = (
+        jnp.einsum("bhqk,bqhd->bkhd", grad_tower_scores, split_q, preferred_element_type=FLOAT)
+        * tower_scale
+    )
+    key_sums, value_sums = (
+        lax.psum_scatter(
+            key_part.reshape(item_count, -1, model_width), "tx", scatter_dimension=1, tiled=True
+        ),
+        lax.psum_scatter(
+            value_part.reshape(item_count, -1, model_width), "tx", scatter_dimension=1, tiled=True
+        ),
+    )
+    grad_tower_k = key_sums.astype(BFLOAT)
+    grad_tower_v = value_sums.astype(BFLOAT)
+    grad_tower_rows = (
+        linear_back(grad_tower_q, tower_query)
+        + linear_back(grad_tower_k, tower_key)
+        + linear_back(grad_tower_v, tower_value)
+    )
+    grad_rows_two, tower_gain_grad = back_tower_norm(grad_tower_rows)
+    grad_two = grad_three + grad_rows_two
+    grad_hidden_out = grad_two.astype(BFLOAT)
+    grad_hidden_lift = back_hidden_gelu(linear_back(grad_hidden_out, hidden_down))[0].astype(BFLOAT)
+    grad_rows_one, hidden_gain_grad = back_hidden_norm(linear_back(grad_hidden_lift, hidden_up))
+    grad_one = grad_two + grad_rows_one
+    grad_cross_out = grad_one.astype(BFLOAT)
+    grad_attended = linear_back(grad_cross_out, cross_proj).astype(BFLOAT)
+    raw_up = linear_back(grad_attended, value_proj)
+    grad_probs = against_pixels(raw_up * feature_gain)
+    cross_delta = jnp.sum(grad_attended.astype(FLOAT) * attended, axis=2)
+    grad_scores = cross_exact * (grad_probs - cross_delta[:, :, None, None])
+    raw_grad_mix = lax.psum(over_pixels(grad_scores), "ty")
+    grad_mix = (raw_grad_mix * feature_gain).astype(BFLOAT)
+    grad_queries = (linear(grad_mix, key_proj) * cross_scale).astype(BFLOAT)
+    feature_part = jnp.sum(raw_grad_mix * raw_query + raw_mix * raw_up, axis=(0, 1))
+    grad_latent_rows, query_gain_grad = back_query_norm(linear_back(grad_queries, query_proj))
+    latent_grad = grad_one + grad_latent_rows
+    share = item_count * rows_here // lax.axis_size("ty")
+    ty_index = lax.axis_index("ty")
+
+    def own_rows(rows):
+        return lax.dynamic_slice_in_dim(
+            rows.reshape(item_count * rows_here, -1), ty_index * share, share, 0
+        )
+
+    pairs = [
+        (final_act, cotangent),
+        (final_input, grad_final_lift),
+        (mixed_input, grad_tower_out),
+        (tower_input, grad_tower_q),
+        (tower_input, grad_tower_k),
+        (tower_input, grad_tower_v),
+        (hidden_act, grad_hidden_out),
+        (hidden_input, grad_hidden_lift),
     ]
-    return jnp.concatenate(pieces, axis=3).reshape(item_count, tile_height * tile_width, FEAT)
+    sums = weight_sums(
+        jnp.stack([own_rows(x) for x, _ in pairs]), jnp.stack([own_rows(g) for _, g in pairs])
+    ).astype(FLOAT)
+    quarter = 1.0 / lax.axis_size("ty")
+    lanes = ((0, 11), (0, 0))
+    gains = jnp.stack(
+        [query_gain_grad, hidden_gain_grad, tower_gain_grad, final_gain_grad,
+         jnp.pad(feature_part, (0, model_width - FEAT))]
+    ) * quarter
+    joined = jnp.concatenate(
+        [
+            jnp.pad(weight_grad(own_rows(mix).astype(BFLOAT), own_rows(grad_cross_out)), lanes),
+            jnp.pad(weight_grad(own_rows(grad_mix), own_rows(query_input)), lanes),
+            jnp.pad(gains, ((0, 27), (0, 0))),
+        ]
+    )
+    joined = all_sum(joined.astype(BFLOAT))
+    cross_core = joined[:FEAT]
+    query_core = joined[272 : 272 + FEAT]
+    value_proj_grad = linear_back(cross_core, cross_proj)
+    key_proj_grad = linear(query_core, query_proj) * cross_scale
+    wide = model_width // lax.axis_size("tx")
+    tx_from = lax.axis_index("tx") * wide
+    cross_proj_grad = weight_grad(
+        lax.dynamic_slice_in_dim(value_proj, tx_from, wide, 1), cross_core
+    )
+    query_proj_grad = weight_grad(
+        lax.dynamic_slice_in_dim(query_core, tx_from, wide, 1), key_proj
+    ) * cross_scale
+    gain_sums = joined[544:549].astype(FLOAT)
+    gain_here = lax.dynamic_slice_in_dim(gain_sums, tx_from, wide, 1)
+    return (
+        resid_four.astype(BFLOAT),
+        latent_grad,
+        gain_sums[4, :FEAT],
+        gain_here[0],
+        query_proj_grad,
+        key_proj_grad,
+        value_proj_grad,
+        cross_proj_grad,
+        gain_here[1],
+        sums[7],
+        sums[6],
+        gain_here[2],
+        sums[3],
+        sums[4],
+        sums[5],
+        sums[2],
+        gain_here[3],
+        sums[1],
+        sums[0],
+    )
 
 
 def on_device(
@@ -106,45 +557,64 @@
     tower_scale = 1.0 / math.sqrt(head_size)
     row_ids = lax.axis_index("ty") * tile_height + jnp.arange(tile_height, dtype=jnp.int32)
     col_ids = lax.axis_index("tx") * tile_width + jnp.arange(tile_width, dtype=jnp.int32)
+    all_cols = jnp.arange(tile_width * lax.axis_size("tx"), dtype=jnp.int32)
+    wide_pixels = lax.all_gather(pixels, "tx", axis=3, tiled=True).astype(FLOAT)
+    wide_mask = lax.all_gather(pixel_mask, "tx", axis=2, tiled=True)
     side_sizes = image_sizes[:, None, None]
-    inside = (
-        (pixel_mask > 0)
+    live = (
+        (wide_mask > 0)
         & (row_ids[None, :, None] < side_sizes)
-        & (col_ids[None, None, :] < side_sizes)
-    )
-    live_mask = inside.reshape(item_count, 1, tile_height * tile_width)
-    features = pixel_features(pixels, image_sizes, row_ids, col_ids)
-
-    def feature_norm(scales):
-        return layer_norm(features, scales)
-
-    normed, back_features = jax.vjp(feature_norm, feature_gain)
-    normed_pixels = normed.astype(BFLOAT)
-    pixel_keys = linear(normed_pixels, key_proj).astype(BFLOAT)
-    pixel_values = linear(normed_pixels, value_proj).astype(BFLOAT)
+        & (all_cols[None, None, :] < side_sizes)
+    )[:, None]
+    row_table, row_coord, row_sum = axis_tables(image_sizes, row_ids, 3, 5)
+    col_table, col_coord, col_sum = axis_tables(image_sizes, all_cols, 4, 5 + 2 * BANDS)
+    pixel_mean = (
+        jnp.sum(wide_pixels, axis=1) + row_sum[:, :, None] + col_sum[:, None, :]
+    ) / FEAT
+    pixel_square = (
+        jnp.sum(wide_pixels * wide_pixels, axis=1)
+        + (row_coord * row_coord)[:, :, None]
+        + (col_coord * col_coord)[:, None, :]
+        + 2.0 * BANDS
+    ) / FEAT
+    pixel_rate = lax.rsqrt(pixel_square - pixel_mean * pixel_mean + EPSILON)
+    exact = lax.Precision.HIGHEST
+
+    def against_pixels(coefs):
+        by_row = jnp.einsum("blf,bif->bli", coefs, row_table, precision=exact)
+        by_col = jnp.einsum("blf,bjf->blj", coefs, col_table, precision=exact)
+        total = by_row[:, :, :, None] + by_col[:, :, None, :]
+        for c in range(3):
+            total = total + coefs[:, :, c][:, :, None, None] * wide_pixels[:, None, c]
+        total = total - jnp.sum(coefs, axis=2)[:, :, None, None] * pixel_mean[:, None]
+        return total * pixel_rate[:, None]
+
+    def over_pixels(weights):
+        scaled = weights * pixel_rate[:, None]
+        by_row = jnp.sum(scaled, axis=3)
+        by_col = jnp.sum(scaled, axis=2)
+        total = jnp.einsum("bli,bif->blf", by_row, row_table, precision=exact)
+        total = total + jnp.einsum("blj,bjf->blf", by_col, col_table, precision=exact)
+        colour = jnp.stack(
+            [jnp.sum(scaled * wide_pixels[:, None, c], axis=(2, 3)) for c in range(3)], axis=2
+        )
+        total = total + jnp.pad(colour, ((0, 0), (0, 0), (0, FEAT - 3)))
+        return total - jnp.sum(scaled * pixel_mean[:, None], axis=(2, 3))[:, :, None]
+
     latent_rows = latents.astype(FLOAT)
     query_normed, back_query_norm = jax.vjp(layer_norm, latent_rows, query_gain)
     query_input = query_normed.astype(BFLOAT)
     own_queries = linear(query_input, query_proj).astype(BFLOAT)
-    all_queries = lax.all_gather(own_queries, "tx", axis=1, tiled=True)
-    scores = (
-        jnp.einsum("blc,bpc->blp", all_queries, pixel_keys, preferred_element_type=FLOAT)
-        * cross_scale
-    )
-    live_scores = jnp.where(live_mask, scores, -1e30)
-    row_top = lax.pmax(jnp.max(live_scores, axis=2), ("ty", "tx"))
-    row_exp = jnp.where(
-        live_mask,
-        jnp.exp(jnp.where(live_mask, scores, row_top[:, :, None]) - row_top[:, :, None]),
-        0.0,
-    )
-    row_total = lax.psum(jnp.sum(row_exp, axis=2), ("ty", "tx"))
-    cross_exact = row_exp / row_total[:, :, None]
-    partial_attended = jnp.einsum(
-        "blp,bpc->blc", cross_exact.astype(BFLOAT), pixel_values, preferred_element_type=FLOAT
-    )
-    column_sums = lax.psum_scatter(partial_attended, "tx", scatter_dimension=1, tiled=True)
-    attended = lax.psum(column_sums, "ty")
+    raw_query = linear_back(own_queries, key_proj) * cross_scale
+    scores = against_pixels(raw_query * feature_gain)
+    row_top = jnp.max(jnp.where(live, scores, -1e30), axis=(2, 3))
+    all_top = lax.pmax(row_top, "ty")
+    row_exp = jnp.where(live, jnp.exp(scores - all_top[:, :, None, None]), 0.0)
+    row_total = lax.psum(jnp.sum(row_exp, axis=(2, 3)), "ty")
+    cross_exact = row_exp / row_total[:, :, None, None]
+    raw_mix = lax.psum(over_pixels(cross_exact), "ty")
+    mix = raw_mix * feature_gain
+    attended = linear(mix.astype(BFLOAT), value_proj)
     attended_input = attended.astype(BFLOAT)
     resid_one = latent_rows + linear(attended_input, cross_proj)
     hidden_normed, back_hidden_norm = jax.vjp(layer_norm, resid_one, hidden_gain)
@@ -239,40 +709,17 @@
     grad_cross_out = grad_one.astype(BFLOAT)
     cross_proj_grad = weight_grad(attended_input, grad_cross_out)
     grad_attended = linear_back(grad_cross_out, cross_proj).astype(BFLOAT)
-    all_upstream = lax.all_gather(grad_attended, "tx", axis=1, tiled=True)
-    again_scores = (
-        jnp.einsum("blc,bpc->blp", all_queries, pixel_keys, preferred_element_type=FLOAT)
-        * cross_scale
-    )
-    again_exp = jnp.where(
-        live_mask,
-        jnp.exp(jnp.where(live_mask, again_scores, row_top[:, :, None]) - row_top[:, :, None]),
-        0.0,
-    )
-    again_probs = again_exp / row_total[:, :, None]
-    grad_probs = jnp.einsum(
-        "blc,bpc->blp", all_upstream, pixel_values, preferred_element_type=FLOAT
-    )
-    cross_delta = lax.psum(jnp.sum(again_probs * grad_probs, axis=2), ("ty", "tx"))
-    grad_scores = (again_probs * (grad_probs - cross_delta[:, :, None])).astype(BFLOAT)
-    query_part = (
-        jnp.einsum("blp,bpc->blc", grad_scores, pixel_keys, preferred_element_type=FLOAT)
-        * cross_scale
-    )
-    query_columns = lax.psum_scatter(query_part, "tx", scatter_dimension=1, tiled=True)
-    grad_queries = lax.psum(query_columns, "ty").astype(BFLOAT)
-    grad_keys = (
-        jnp.einsum("blp,blc->bpc", grad_scores, all_queries, preferred_element_type=FLOAT)
-        * cross_scale
-    ).astype(BFLOAT)
-    grad_values = jnp.einsum(
-        "blp,blc->bpc", again_probs.astype(BFLOAT), all_upstream, preferred_element_type=FLOAT
-    ).astype(BFLOAT)
-    key_proj_grad = weight_grad(normed_pixels, grad_keys)
-    value_proj_grad = weight_grad(normed_pixels, grad_values)
-    grad_normed = linear_back(grad_keys, key_proj) + linear_back(grad_values, value_proj)
-    feature_part = back_features(grad_normed)[0]
-    pixel_sums = lax.psum((key_proj_grad, value_proj_grad, feature_part), ("ty", "tx"))
+    raw_up = linear_back(grad_attended, value_proj)
+    grad_probs = against_pixels(raw_up * feature_gain)
+    cross_delta = jnp.sum(grad_attended.astype(FLOAT) * attended, axis=2)
+    grad_scores = cross_exact * (grad_probs - cross_delta[:, :, None, None])
+    raw_grad_mix = lax.psum(over_pixels(grad_scores), "ty")
+    grad_mix = (raw_grad_mix * feature_gain).astype(BFLOAT)
+    grad_queries = (linear(grad_mix, key_proj) * cross_scale).astype(BFLOAT)
+    key_proj_grad = weight_grad(grad_mix, own_queries) * cross_scale
+    value_proj_grad = weight_grad(mix.astype(BFLOAT), grad_attended)
+    feature_part = jnp.sum(raw_grad_mix * raw_query + raw_mix * raw_up, axis=(0, 1))
+    pixel_sums = lax.psum((key_proj_grad, value_proj_grad, feature_part), "tx")
     query_proj_grad = weight_grad(query_input, grad_queries)
     grad_latent_rows, query_gain_grad = back_query_norm(linear_back(grad_queries, query_proj))
     latent_grad = grad_one + grad_latent_rows
@@ -361,6 +808,8 @@
         P("tx", None),
         P("tx", None),
     )
+    fits = mesh.shape["ty"] == 4 and mesh.shape["tx"] == HEADS
+    plan = on_device_fast if fits else on_device
     return jax.shard_map(
-        on_device, mesh=mesh, in_specs=in_specs, out_specs=out_specs, check_vma=False
-    )
+        plan, mesh=mesh, in_specs=in_specs, out_specs=out_specs, check_vma=False
+    )

time: 1950 us -> 771 us (0.40)
  waiting for transfers between devices: 1350 us -> 307 us
  blocking collectives: 225 us -> 76.9 us
  Pallas kernels: 0 us -> 137 us
  matrix products: 197 us -> 75.7 us
  local copies, waits for them, and re-layouts: 111 us -> 51.5 us
  other arithmetic: 42.5 us -> 96.8 us
    reduce_scatter x14 -> x2, waiting for transfers between devices: 1070 us -> 153 us  [the longest x1 85.2 us: on_device_fast(): lax.psum_scatter(value_part.reshape(item_count, -1, model_width), 'tx', s...]
    psum x5 -> x1, blocking collectives: 155 us -> 5.97 us  [on_device_fast(): row_total = lax.psum(jnp.sum(row_exp, axis=(2, 3)), 'ty')]
    pallas_call x0 -> x2, Pallas kernels: none -> 137 us  [the longest x1 90.3 us: weight_sums(): pl.pallas_call(weight_sums_kernel, out_shape=jax.ShapeDtypeStruct((count,...]
    psum x1 -> x2, waiting for transfers between devices: 140 us -> 63.9 us  [the longest x1 32.3 us: on_device_fast(): raw_grad_mix = lax.psum(over_pixels(grad_scores), 'ty')]
    dot_general x12 -> x14, matrix products: 91.8 us -> 30.4 us  [the longest x1 5.74 us: on_device_fast(): jnp.einsum('bhqk,bqhd->bkhd', tower_probs, grad_mixed, preferred_element_...]
    reduce_sum x1 -> x7, other arithmetic: 5.92 us -> 67.2 us  [the longest x2 49.6 us: over_pixels(): jnp.sum(scaled * pixel_mean[:, None], axis=(2, 3))[:, :, None]]
    all_gather x0 -> x2, blocking collectives: none -> 53.7 us  [the longest x1 27.1 us: on_device_fast(): wide_mask = lax.all_gather(pixel_mask, 'tx', axis=2, tiled=True)]
    all_gather x4 -> x2, waiting for transfers between devices: 136 us -> 89.7 us  [the longest x1 45.1 us: on_device_fast(): lax.all_gather(tower_v, 'tx', axis=1, tiled=True)]
  transfers between devices with their start and end apart: 19 -> 6, of which waited for: 17 -> 6; matrix products, arithmetic and copies ran while one was open for 12% -> 5% of each run, Pallas kernels for 0% -> 0%
where the time goes in v1:
time: 771 us; the launch traced here: 761 us
  waiting for transfers between devices  307 us (40%)
  Pallas kernels  137 us (18%)
  other arithmetic  96.8 us (13%)
  blocking collectives  76.9 us (10%)
  matrix products  75.7 us (10%)
  local copies, waits for them, and re-layouts  51.5 us (7%)
  between operations  16.1 us (2%)
    pallas_call x1, Pallas kernels, weight_sums(): pl.pallas_call(weight_sums_kernel, out_shape=jax.ShapeDtypeStruct((count,...  90.3 us
    reduce_scatter x1, waiting for transfers between devices, on_device_fast(): lax.psum_scatter(value_part.reshape(item_count, -1, model_width), 'tx', s...  85.2 us
    reduce_scatter x1, waiting for transfers between devices, on_device_fast(): lax.psum_scatter(key_part.reshape(item_count, -1, model_width), 'tx', sca...  67.8 us
    reduce_sum x2, other arithmetic, over_pixels(): jnp.sum(scaled * pixel_mean[:, None], axis=(2, 3))[:, :, None]  49.6 us
    pallas_call x1, Pallas kernels, all_sum(): pl.pallas_call(all_sum_kernel, out_shape=jax.ShapeDtypeStruct((4, 8, part...  46.4 us
    all_gather x1, waiting for transfers between devices, on_device_fast(): lax.all_gather(tower_v, 'tx', axis=1, tiled=True)  45.1 us
    all_gather x1, waiting for transfers between devices, on_device_fast(): lax.all_gather(tower_k, 'tx', axis=1, tiled=True)  44.6 us
    psum x1, waiting for transfers between devices, on_device_fast(): raw_grad_mix = lax.psum(over_pixels(grad_scores), 'ty')  32.3 us
  transfers between devices with their start and end apart: 6, of which 6 were waited for; matrix products, arithmetic and copies ran while one was open for 5% of the time, Pallas kernels for 0%

profile of v1, /device:TPU:1, one launch (start us, length us, event | category | flops | bytes accessed | tf_op | source)
XLA Modules:
  0.0 761.3 jit_solution(11824375234222820934)
XLA Ops:
  9.0 26.6 %all_gather.13 = bf16[2,3,72,288]{2,0,3,1:T(2,128)(2,1)S(1)} all-gather(bf16[2,3,72,36]{2,0,3,1:T(2,128)(2,1)} %param.22), channel_id=1, replica_groups=mesh['ty'=4,'tx'=8] {'tx'}, dimensions={3}, use_global_device_ids=true | all-gather | bytes 279936 | tf_op jit(solution)/shard_map/all_gather | solution.py:301
  40.9 2.1 fusion.193
  46.1 3.6 fusion.222
  52.9 3.9 concatenate.15
  56.8 2.6 fusion.232
  67.6 27.1 %all_gather.12 = s32[2,72,288]{1,0,2:T(2,128)} all-gather(s32[2,72,36]{1,0,2:T(2,128)S(1)} %copy-done.76), channel_id=1, replica_groups=mesh['ty'=4,'tx'=8] {'tx'}, dimensions={2}, use_global_device_ids=true | all-gather | bytes 186624 | tf_op jit(solution)/shard_map/all_gather | solution.py:302
  99.7 9.7 %select_reduce_fusion = f32[2,64]{1,0:T(2,128)S(1)} fusion(f32[2,72,288]{2,1,0:T(8,128)S(1)} %get-tuple-element.61, f32[2,72,288]{2,1,0:T(8,128)S(1)} %get-tuple-element.62, f32[2,64]{1,0:T(2,128)S(1)} %copy-done.102, f32[2,72,288]{2,1,0:T(8,128)} %copy.140, f32[2,64]{1,0:T(2,128)} %get-tuple-element.45, f32[2,72,288]{2,1,0:T(8,128)} %copy.139, ...), kind=kLoop, calls=%fused_computation.11 | loop fusion | flops 31850368 | bytes 1057792 | tf_op jit(solution)/shard_map/reduce_max | solution.py:350
  109.5 17.2 %pmax.7 = f32[2,64]{1,0:T(2,128)S(1)} all-reduce(f32[2,64]{1,0:T(2,128)S(1)} %select_reduce_fusion), channel_id=1, replica_groups=mesh['ty'=4,'tx'=8] {'ty'}, use_global_device_ids=true, to_apply=%region_10.11 | all-reduce | flops 128 | bytes 1024 | tf_op jit(solution)/shard_map/pmax | solution.py:351
  126.7 11.4 %fusion.2 = f32[2,64]{1,0:T(2,128)S(1)} fusion(f32[2,64]{1,0:T(2,128)S(1)} %pmax.7, f32[2,72,288]{2,1,0:T(8,128)} %copy-done.52, f32[2,72,288]{2,1,0:T(8,128)} %copy-done.54, f32[2,64]{1,0:T(2,128)S(1)} %copy-done.102, f32[2,72,288]{2,1,0:T(8,128)} %copy.140, f32[2,64]{1,0:T(2,128)} %get-tuple-element.45, f32[2,72,288]{2,1,0:T(8,128)} %copy.139, ...), kind=kLoop, calls=%fused_computation.14 | loop fusion | flops 34504576 | bytes 1058304 | tf_op jit(solution)/shard_map/reduce_sum | solution.py:353
  138.1 6.0 psum.21
  144.2 23.3 %multiply_reduce_fusion.4 = (f32[2,64]{1,0:T(2,128)S(1)}, f32[2,64,72]{2,1,0:T(8,128)}, f32[2,64]{1,0:T(2,128)S(1)}, f32[2,64]{1,0:T(2,128)S(1)}, f32[2,64]{1,0:T(2,128)S(1)}, /*index=5*/f32[2,64,288]{2,1,0:T(8,128)}) fusion(f32[2,72,288]{2,1,0:T(8,128)} %copy-done.52, f32[2,72,288]{2,1,0:T(8,128)} %copy-done.54, f32[2,64]{1,0:T(2,128)S(1)} %psum.21, ...), kind=kLoop, calls=%fused_computation.6 | loop fusion | flops 63654400 | bytes 1244672 | tf_op jit(solution)/shard_map/reduce_sum | solution.py:342
  171.5 31.6 %all-reduce.9.cloned.1.call-done = f32[2,64,261]{2,1,0:T(8,128)} async-done(((f32[2,64,261]{2,1,0:T(8,128)}), f32[2,64,261]{2,1,0:T(8,128)}) %all-reduce.9.cloned.1.call-update) | async-done | bytes 133648 | tf_op jit(solution)/shard_map/psum | solution.py:355
  211.7 2.7 fusion.90
  216.9 44.6 %all-gather.5.cloned.1.call-done = bf16[2,512,1024]{2,1,0:T(8,128)(2,1)} async-done(((bf16[2,64,1024]{2,1,0:T(8,128)(2,1)}), bf16[2,512,1024]{2,1,0:T(8,128)(2,1)}) %all-gather.5.cloned.1.call-update) | async-done | bytes 2097168 | tf_op jit(solution)/shard_map/all_gather | solution.py:371
  261.5 2.4 fusion.13
  267.2 45.1 %all-gather.3.cloned.1.call-done = bf16[2,512,1024]{2,1,0:T(8,128)(2,1)} async-done(((bf16[2,64,1024]{2,1,0:T(8,128)(2,1)}), bf16[2,512,1024]{2,1,0:T(8,128)(2,1)}) %all-gather.3.cloned.1.call-update) | async-done | bytes 2097168 | tf_op jit(solution)/shard_map/all_gather | solution.py:372
  312.3 4.2 fusion.102
  316.5 2.3 fusion.228
  327.8 2.7 convolution_multiply_fusion
  330.5 5.4 copy.153
  336.0 5.7 fusion.162
  341.8 5.5 copy.155
  348.5 2.6 fusion.81
  356.0 67.8 %reduce-scatter.3.cloned.1.call-done = f32[2,64,1024]{2,1,0:T(8,128)} async-done(((f32[2,512,1024]{2,1,0:T(8,128)}), f32[2,64,1024]{2,1,0:T(8,128)}) %reduce-scatter.3.cloned.1.call-update) | async-done | bytes 524304 | tf_op jit(solution)/shard_map/reduce_scatter | solution.py:421
  425.8 2.4 fusion.27
  429.8 85.2 %reduce-scatter.5.cloned.1.call-done = f32[2,64,1024]{2,1,0:T(8,128)} async-done(((f32[2,512,1024]{2,1,0:T(8,128)}), f32[2,64,1024]{2,1,0:T(8,128)}) %reduce-scatter.5.cloned.1.call-update) | async-done | bytes 524304 | tf_op jit(solution)/shard_map/reduce_scatter | solution.py:424
  516.1 2.9 multiply_reduce_fusion.18
  530.2 90.3 %weight_sums.1 = bf16[8,128,1024]{2,1,0:T(8,128)(2,1)S(1)} custom-call(bf16[8,32,1024]{2,1,0:T(8,128)(2,1)S(1)} %get-tuple-element.115.x_ref, bf16[8,32,1024]{2,1,0:T(8,128)(2,1)S(1)} %get-tuple-element.114.g_ref), custom_call_target="tpu_custom_call" | custom-call | tf_op jit(solution)/shard_map/weight_sums/pallas_call | solution.py:175
  623.3 26.3 %multiply_reduce_fusion = (f32[2,64]{1,0:T(2,128)S(1)}, f32[2,64]{1,0:T(2,128)S(1)}, f32[2,64]{1,0:T(2,128)S(1)}, f32[2,64]{1,0:T(2,128)S(1)}, f32[2,64,288]{2,1,0:T(8,128)}, /*index=5*/f32[2,64,72]{2,1,0:T(8,128)}) fusion(f32[2,72,288]{2,1,0:T(8,128)S(1)} %copy-done.55, f32[2,72,288]{2,1,0:T(8,128)S(1)} %copy-done.58, f32[2,72,288]{2,1,0:T(8,128)S(1)} %copy-done.57, ...), kind=kLoop, calls=%fused_computation.1 | loop fusion | flops 95504896 | bytes 1431552 | tf_op jit(solution)/shard_map/reduce_sum | solution.py:342
  656.2 32.3 %all-reduce.11.cloned.1.call-done = f32[2,64,261]{2,1,0:T(8,128)} async-done(((f32[2,64,261]{2,1,0:T(8,128)}), f32[2,64,261]{2,1,0:T(8,128)}) %all-reduce.11.cloned.1.call-update) | async-done | bytes 133648 | tf_op jit(solution)/shard_map/psum | solution.py:447
  689.8 2.7 fusion.151
  697.2 46.4 %all_sum.1 = bf16[4,8,144,128]{3,2,1,0:T(8,128)(2,1)S(1)} custom-call(bf16[4,144,1024]{2,1,0:T(8,128)(2,1)S(1)} %bitcast.341), custom_call_target="tpu_custom_call" | custom-call | tf_op jit(solution)/shard_map/all_sum/pallas_call | solution.py:244
  (397 shorter events, 100.4 us)
Async XLA Ops:
  7.2 198.2 %copy-start = (bf16[1024,1024]{1,0:T(8,128)(2,1)S(1)}, bf16[1024,1024]{1,0:T(8,128)(2,1)}, u32[]{:S(2)}) copy-start(bf16[1024,1024]{1,0:T(8,128)(2,1)} %param.32) | copy-start | bytes 6291460
  7.2 31.4 %copy-start.117 = (s32[2]{0:T(128)S(1)}, s32[2]{0:T(128)}, u32[]{:S(2)}) copy-start(s32[2]{0:T(128)} %param.24) | copy-start | bytes 28
  7.2 195.8 %all-reduce.9.cloned.1.call-start = ((), (), s32[]{:S(2)}) async-start(), calls=%async_computation.2 | async-start | bytes 393216 | tf_op jit(solution)/shard_map/psum | solution.py:355
  45.6 647.6 %copy-start.77 = (f32[2,64]{1,0:T(2,128)}, f32[2,64]{1,0:T(2,128)S(1)}, u32[]{:S(2)}) copy-start(f32[2,64]{1,0:T(2,128)S(1)} %broadcast_multiply_fusion.9) | copy-start | bytes 1540
  51.7 117.9 %copy-start.19 = (f32[2,72,261]{2,1,0:T(8,128)}, f32[2,72,261]{2,1,0:T(8,128)S(1)}, u32[]{:S(2)}) copy-start(f32[2,72,261]{2,1,0:T(8,128)S(1)} %concatenate.14) | copy-start | bytes 451012
  52.1 92.0 %copy-start.67 = (f32[2,64,72]{2,1,0:T(8,128)}, f32[2,64,72]{2,1,0:T(8,128)S(1)}, u32[]{:S(2)}) copy-start(f32[2,64,72]{2,1,0:T(8,128)S(1)} %fusion.231) | copy-start | bytes 110596
  56.8 110.8 %copy-start.3 = (f32[2,288,261]{1,2,0:T(8,128)}, f32[2,288,261]{1,2,0:T(8,128)S(1)}, u32[]{:S(2)}) copy-start(f32[2,288,261]{1,2,0:T(8,128)S(1)} %concatenate.15) | copy-start | bytes 1804036
  56.8 10.2 %copy-start.118 = (s32[2]{0:T(128)S(1)}, s32[2]{0:T(128)}, u32[]{:S(2)}) copy-start(s32[2]{0:T(128)} %param.24) | copy-start | bytes 28
  56.8 10.8 %copy-start.76 = (s32[2,72,36]{1,0,2:T(2,128)S(1)}, s32[2,72,36]{1,0,2:T(2,128)}, u32[]{:S(2)}) copy-start(s32[2,72,36]{1,0,2:T(2,128)} %param.23) | copy-start | bytes 62212
  59.5 37.0 %copy-start.81 = (f32[2]{0:T(128)S(1)}, f32[2]{0:T(128)}, u32[]{:S(2)}) copy-start(f32[2]{0:T(128)} %copy-done.80) | copy-start | bytes 28
  59.5 37.0 %copy-start.101 = (f32[72]{0:T(128)S(1)}, f32[72]{0:T(128)}, u32[]{:S(2)}) copy-start(f32[72]{0:T(128)} %copy-done.100) | copy-start | bytes 868
  59.5 37.0 %copy-start.110 = (f32[2,72]{1,0:T(2,128)S(1)}, f32[2,72]{1,0:T(2,128)}, u32[]{:S(2)}) copy-start(f32[2,72]{1,0:T(2,128)} %get-tuple-element.49) | copy-start | bytes 1732
  59.5 37.0 %copy-start.111 = (f32[2,72]{1,0:T(2,128)S(1)}, f32[2,72]{1,0:T(2,128)}, u32[]{:S(2)}) copy-start(f32[2,72]{1,0:T(2,128)} %get-tuple-element.50) | copy-start | bytes 1732
  59.5 37.1 %copy-start.87 = (f32[2,288]{1,0:T(2,128)S(1)}, f32[2,288]{1,0:T(2,128)}, u32[]{:S(2)}) copy-start(f32[2,288]{1,0:T(2,128)} %get-tuple-element.47) | copy-start | bytes 6916
  59.5 37.1 %copy-start.88 = (f32[2,288]{1,0:T(2,128)S(1)}, f32[2,288]{1,0:T(2,128)}, u32[]{:S(2)}) copy-start(f32[2,288]{1,0:T(2,128)} %get-tuple-element.48) | copy-start | bytes 6916
  59.5 37.2 %copy-start.99 = (pred[2,288]{1,0:T(4,128)(4,1)S(1)}, pred[2,288]{1,0:T(4,128)(4,1)}, u32[]{:S(2)}) copy-start(pred[2,288]{1,0:T(4,128)(4,1)} %iota_compare_fusion.4) | copy-start | bytes 1732
  61.6 38.1 %copy-start.102 = (f32[2,64]{1,0:T(2,128)S(1)}, f32[2,64]{1,0:T(2,128)}, u32[]{:S(2)}) copy-start(f32[2,64]{1,0:T(2,128)} %get-tuple-element.59) | copy-start | bytes 1540
  61.6 38.1 %copy-start.104 = (f32[2,64]{1,0:T(2,128)S(1)}, f32[2,64]{1,0:T(2,128)}, u32[]{:S(2)}) copy-start(f32[2,64]{1,0:T(2,128)} %get-tuple-element.44) | copy-start | bytes 1540
  97.7 46.4 %copy-start.69 = (pred[2,72,288]{2,1,0:T(8,128)(4,1)}, pred[2,72,288]{2,1,0:T(8,128)(4,1)S(1)}, u32[]{:S(2)}) copy-start(pred[2,72,288]{2,1,0:T(8,128)(4,1)S(1)} %and_and_fusion) | copy-start | bytes 124420
  126.7 17.4 %copy-start.113 = (f32[2,64]{1,0:T(2,128)}, f32[2,64]{1,0:T(2,128)S(1)}, u32[]{:S(2)}) copy-start(f32[2,64]{1,0:T(2,128)S(1)} %pmax.7) | copy-start | bytes 1540
  126.7 17.4 %copy-start.106 = (f32[2,64]{1,0:T(2,128)S(1)}, f32[2,64]{1,0:T(2,128)}, u32[]{:S(2)}) copy-start(f32[2,64]{1,0:T(2,128)} %get-tuple-element.45) | copy-start | bytes 1540
  126.7 17.4 %copy-start.108 = (f32[2,64]{1,0:T(2,128)S(1)}, f32[2,64]{1,0:T(2,128)}, u32[]{:S(2)}) copy-start(f32[2,64]{1,0:T(2,128)} %get-tuple-element.46) | copy-start | bytes 1540
  144.1 23.3 %copy-start.115 = (f32[2,64]{1,0:T(2,128)}, f32[2,64]{1,0:T(2,128)S(1)}, u32[]{:S(2)}) copy-start(f32[2,64]{1,0:T(2,128)S(1)} %psum.21) | copy-start | bytes 1540
  171.4 90.1 %all-gather.5.cloned.1.call-start = ((), (), s32[]{:S(2)}) async-start(), calls=%async_computation.4 | async-start | bytes 2359296 | tf_op jit(solution)/shard_map/all_gather | solution.py:371
  209.2 107.3 %copy-start.1 = (f32[2,64,1024]{2,1,0:T(8,128)}, f32[2,64,1024]{2,1,0:T(8,128)S(1)}, u32[]{:S(2)}) copy-start(f32[2,64,1024]{2,1,0:T(8,128)S(1)} %get-tuple-element.96) | copy-start | bytes 1572868
  211.7 100.6 %all-gather.3.cloned.1.call-start = ((), (), s32[]{:S(2)}) async-start(), calls=%async_computation.3 | async-start | bytes 2359296 | tf_op jit(solution)/shard_map/all_gather | solution.py:372
  214.5 209.3 %reduce-scatter.3.cloned.1.call-start = ((), (), s32[]{:S(2)}) async-start(), calls=%async_computation.5 | async-start | bytes 4718592 | tf_op jit(solution)/shard_map/reduce_scatter | solution.py:421
  336.0 179.0 %reduce-scatter.5.cloned.1.call-start = ((), (), s32[]{:S(2)}) async-start(), calls=%async_computation.6 | async-start | bytes 4718592 | tf_op jit(solution)/shard_map/reduce_scatter | solution.py:424
  347.3 341.3 %all-reduce.11.cloned.1.call-start = ((), (), s32[]{:S(2)}) async-start(), calls=%async_computation.7 | async-start | bytes 393216 | tf_op jit(solution)/shard_map/psum | solution.py:447
  623.2 27.1 %copy-start.5 = (f32[2,288,261]{1,2,0:T(8,128)S(1)}, f32[2,288,261]{1,2,0:T(8,128)}, u32[]{:S(2)}) copy-start(f32[2,288,261]{1,2,0:T(8,128)} %copy-done.3) | copy-start | bytes 1804036
  623.3 29.0 %copy-start.21 = (f32[2,72,261]{2,1,0:T(8,128)S(1)}, f32[2,72,261]{2,1,0:T(8,128)}, u32[]{:S(2)}) copy-start(f32[2,72,261]{2,1,0:T(8,128)} %copy-done.19) | copy-start | bytes 451012
  652.3 37.5 %copy-start.23 = (bf16[261,1024]{1,0:T(8,128)(2,1)S(1)}, bf16[261,1024]{1,0:T(8,128)(2,1)}, u32[]{:S(2)}) copy-start(bf16[261,1024]{1,0:T(8,128)(2,1)} %param.30) | copy-start | bytes 1603588
  (96 other events, 293.7 us)
Sparse Core Ops, SparseCore 0:
  171.5 31.4 all-reduce.8
  211.8 49.6 all-gather.4
  264.5 47.7 all-gather.2
  336.1 87.6 reduce-scatter.2
  427.3 87.6 reduce-scatter.4
  654.4 34.1 all-reduce.10

commit v2 on v1

--- a/solution.py
+++ b/solution.py
@@ -262,6 +262,274 @@
     return jnp.transpose(out, (0, 2, 1, 3)).reshape(rows, width)
 
 
+LANES = 384
+CUBE = 0.044715
+SLOPE = 0.7978845608028654
+
+
+def norm_rows(rows):
+    shifted = rows - jnp.mean(rows, axis=-1, keepdims=True)
+    rate = lax.rsqrt(jnp.mean(shifted * shifted, axis=-1, keepdims=True) + EPSILON)
+    return shifted * rate, rate
+
+
+def norm_rows_back(upstream, gain, unit, rate):
+    scaled = upstream * gain
+    along = jnp.mean(scaled * unit, axis=-1, keepdims=True)
+    grad = rate * (scaled - jnp.mean(scaled, axis=-1, keepdims=True) - unit * along)
+    return grad, jnp.sum(upstream * unit, axis=0, keepdims=True)
+
+
+def gelu_pair(values):
+    square = values * values
+    bend = jnp.tanh(SLOPE * (values + CUBE * values * square))
+    half = 0.5 * (1.0 + bend)
+    slope = half + 0.5 * values * (1.0 - bend * bend) * (SLOPE * (1.0 + 3.0 * CUBE * square))
+    return values * half, slope
+
+
+def dot_nt(left, right):
+    return lax.dot_general(left, right, (((1,), (1,)), ((), ())), preferred_element_type=FLOAT)
+
+
+def dot_nn(left, right):
+    return lax.dot_general(left, right, (((1,), (0,)), ((), ())), preferred_element_type=FLOAT)
+
+
+def tower_kernel(
+    part_ref, lat_ref, cot_ref, fgain_ref, hgain_ref, tgain_ref, ogain_ref, vproj_ref,
+    w0, w1, w2, w3, w4, w5, w6, w7, w8,
+    result_ref, x_ref, g_ref, mix_ref, gcross_ref, one_ref, gains_ref, feat_ref, coef_ref,
+    ws, part_in, qkv_out, qkv_in, kv_in, probs, mixed_out, mixed_in, gm_out, gm_in,
+    kvx_out, kvx_in, gqkv_out, gqkv_in,
+    w_sem, a_s, a_r, q_s, q_r, k_s, k_r, m_s, m_r, g_s, g_r, e_s, e_r, b_s, b_r, c_s, c_r, o_s, o_r,
+):
+    ty, tx = lax.axis_index("ty"), lax.axis_index("tx")
+    tys = [{"ty": lax.rem(ty + d, 4), "tx": tx} for d in (1, 2, 3)]
+    txs = [{"ty": ty, "tx": lax.rem(tx + d, 8)} for d in range(1, 8)]
+    mate = {"ty": 2 * (ty // 2) + 1 - lax.rem(ty, 2), "tx": tx}
+    weights = (w0, w1, w2, w3, w4, w5, w6, w7, w8)
+    loads = []
+    for i, w in enumerate(weights):
+        loads.append(pltpu.make_async_copy(w, ws.at[i], w_sem.at[i]))
+        loads[i].start()
+    greet(tys + txs)
+    cross, up, down, tq, tk, tv, tproj, fup, fdown = range(9)
+
+    def times(rows, i):
+        return dot_nn(rows, ws[i])
+
+    def times_back(rows, i):
+        return dot_nt(rows, ws[i])
+
+    def spread(out, into, s_sem, r_sem):
+        copies = [
+            send(out.at[lax.rem(tx + d, 8)], into.at[tx], s_sem.at[d - 1], r_sem.at[d - 1], txs[d - 1])
+            for d in range(1, 8)
+        ]
+        into[tx] = out[tx]
+        return copies
+
+    def finish(copies):
+        for copy in copies:
+            copy.wait()
+
+    copies = [
+        send(part_ref.at[lax.rem(ty + d, 4)], part_in.at[d - 1], a_s.at[d - 1], a_r.at[d - 1], tys[d - 1])
+        for d in (1, 2, 3)
+    ]
+    parts = [part_ref[ty]]
+    finish(copies)
+    parts += [part_in[d] for d in range(3)]
+    tops = [p[:, FEAT + 1 : FEAT + 2] for p in parts]
+    top = jnp.maximum(jnp.maximum(tops[0], tops[1]), jnp.maximum(tops[2], tops[3]))
+    joined = sum(p * jnp.exp2(t - top) for p, t in zip(parts, tops))
+    total = joined[:, FEAT : FEAT + 1]
+    fgain = fgain_ref[...]
+    raw_mix = joined / total
+    shift = top + jnp.log2(total)
+    mix = (raw_mix * fgain).astype(BFLOAT)
+    mix_ref[...] = mix
+    attended = dot_nn(mix, vproj_ref[...])
+    finish(loads[:1])
+    one = lat_ref[ty].astype(FLOAT) + times(attended.astype(BFLOAT), cross)
+    h_unit, h_rate = norm_rows(one)
+    hidden = (h_unit * hgain_ref[...]).astype(BFLOAT)
+    x_ref[7] = hidden
+    finish(loads[1:2])
+    act, act_slope = gelu_pair(times(hidden, up))
+    act = act.astype(BFLOAT)
+    x_ref[6] = act
+    finish(loads[2:3])
+    two = one + times(act, down)
+    t_unit, t_rate = norm_rows(two)
+    trows = (t_unit * tgain_ref[...]).astype(BFLOAT)
+    x_ref[3] = trows
+    x_ref[4] = trows
+    x_ref[5] = trows
+    for s, i in enumerate((tq, tk, tv)):
+        finish(loads[i : i + 1])
+        value = times(trows, i).astype(BFLOAT)
+        for h in range(8):
+            qkv_out[h, 32 * s : 32 * s + 32] = value[:, 128 * h : 128 * h + 128]
+    finish(spread(qkv_out, qkv_in, q_s, q_r))
+    copies = [send(qkv_in.at[:, 32:96], kv_in, k_s, k_r, mate)]
+    q = qkv_in[:, 0:32].reshape(256, 128)
+    k1 = qkv_in[:, 32:64].reshape(256, 128)
+    v1 = qkv_in[:, 64:96].reshape(256, 128)
+    scale = 1.0 / math.sqrt(128)
+    s1 = dot_nt(q, k1) * scale
+    finish(copies)
+    k2 = kv_in[:, 0:32].reshape(256, 128)
+    v2 = kv_in[:, 32:64].reshape(256, 128)
+    s2 = dot_nt(q, k2) * scale
+    stop = jnp.maximum(
+        jnp.max(s1, axis=1, keepdims=True), jnp.max(s2, axis=1, keepdims=True)
+    )
+    e1, e2 = jnp.exp(s1 - stop), jnp.exp(s2 - stop)
+    rate = 1.0 / (jnp.sum(e1, axis=1, keepdims=True) + jnp.sum(e2, axis=1, keepdims=True))
+    p1, p2 = e1 * rate, e2 * rate
+    probs[0] = p1
+    probs[1] = p2
+    mixed_out[...] = (
+        (dot_nn(p1.astype(BFLOAT), v1) + dot_nn(p2.astype(BFLOAT), v2))
+        .astype(BFLOAT)
+        .reshape(8, 32, 128)
+    )
+    copies = spread(mixed_out, mixed_in, m_s, m_r)
+    finish(loads[6:9])
+    cot = cot_ref[ty]
+    g_ref[0] = cot
+    back_four = times_back(cot, fdown)
+    finish(copies)
+    mixed = jnp.concatenate([mixed_in[h] for h in range(8)], axis=1)
+    x_ref[2] = mixed
+    three = two + times(mixed, tproj)
+    o_unit, o_rate = norm_rows(three)
+    ogain = ogain_ref[...]
+    frows = (o_unit * ogain).astype(BFLOAT)
+    x_ref[1] = frows
+    fact, fact_slope = gelu_pair(times(frows, fup))
+    fact = fact.astype(BFLOAT)
+    x_ref[0] = fact
+    g_lift = (back_four * fact_slope).astype(BFLOAT)
+    g_ref[1] = g_lift
+    g_three, o_grad = norm_rows_back(times_back(g_lift, fup), ogain, o_unit, o_rate)
+    gains_ref[2:3] = o_grad
+    g_three = cot.astype(FLOAT) + g_three
+    g_tower = g_three.astype(BFLOAT)
+    g_ref[2] = g_tower
+    g_mixed = times_back(g_tower, tproj).astype(BFLOAT)
+    for h in range(8):
+        gm_out[h] = g_mixed[:, 128 * h : 128 * h + 128]
+    copies = spread(gm_out, gm_in, g_s, g_r)
+    result_ref[ty] = (three + times(fact, fdown)).astype(BFLOAT)
+    copies_out = [
+        send(result_ref.at[ty], result_ref.at[ty], o_s.at[d - 1], o_r.at[d - 1], tys[d - 1])
+        for d in (1, 2, 3)
+    ]
+    finish(copies)
+    gm = gm_in[...].reshape(256, 128)
+    q = qkv_in[:, 0:32].reshape(256, 128)
+    k1 = qkv_in[:, 32:64].reshape(256, 128)
+    v1 = qkv_in[:, 64:96].reshape(256, 128)
+    k2 = kv_in[:, 0:32].reshape(256, 128)
+    v2 = kv_in[:, 32:64].reshape(256, 128)
+    p1, p2 = probs[0], probs[1]
+    gp1, gp2 = dot_nt(gm, v1), dot_nt(gm, v2)
+    away = jnp.sum(p1 * gp1, axis=1, keepdims=True) + jnp.sum(p2 * gp2, axis=1, keepdims=True)
+    gs1 = (p1 * (gp1 - away)).astype(BFLOAT)
+    gs2 = (p2 * (gp2 - away)).astype(BFLOAT)
+    kvx_out[0] = (outer(gs2, q) * scale).astype(BFLOAT)
+    kvx_out[1] = outer(p2.astype(BFLOAT), gm).astype(BFLOAT)
+    copies = [send(kvx_out, kvx_in, e_s, e_r, mate)]
+    gq = (dot_nn(gs1, k1) + dot_nn(gs2, k2)) * scale
+    gk = outer(gs1, q) * scale
+    gv = outer(p1.astype(BFLOAT), gm)
+    gqkv_out[:, 0:32] = gq.astype(BFLOAT).reshape(8, 32, 128)
+    finish(copies)
+    gqkv_out[:, 32:64] = (gk + kvx_in[0].astype(FLOAT)).astype(BFLOAT).reshape(8, 32, 128)
+    gqkv_out[:, 64:96] = (gv + kvx_in[1].astype(FLOAT)).astype(BFLOAT).reshape(8, 32, 128)
+    finish(spread(gqkv_out, gqkv_in, b_s, b_r))
+    g_trows = None
+    for s, i in enumerate((tq, tk, tv)):
+        value = jnp.concatenate([gqkv_in[h, 32 * s : 32 * s + 32] for h in range(8)], axis=1)
+        g_ref[3 + s] = value
+        term = times_back(value, i)
+        g_trows = term if g_trows is None else g_trows + term
+    g_two, t_grad = norm_rows_back(g_trows, tgain_ref[...], t_unit, t_rate)
+    gains_ref[1:2] = t_grad
+    g_two = g_three + g_two
+    g_hidden = g_two.astype(BFLOAT)
+    g_ref[6] = g_hidden
+    g_hlift = (times_back(g_hidden, down) * act_slope).astype(BFLOAT)
+    g_ref[7] = g_hlift
+    g_one, h_grad = norm_rows_back(times_back(g_hlift, up), hgain_ref[...], h_unit, h_rate)
+    gains_ref[0:1] = h_grad
+    g_one = g_two + g_one
+    one_ref[...] = g_one
+    g_cross = g_one.astype(BFLOAT)
+    gcross_ref[...] = g_cross
+    g_att = times_back(g_cross, cross).astype(BFLOAT)
+    raw_up = dot_nt(g_att, vproj_ref[...])
+    feat_ref[...] = jnp.sum(raw_mix * raw_up, axis=0, keepdims=True)
+    delta = jnp.sum(g_att.astype(FLOAT) * attended, axis=1, keepdims=True)
+    lane = lax.broadcasted_iota(jnp.int32, raw_up.shape, 1)
+    coef_ref[ty] = jnp.where(
+        lane < FEAT, raw_up * fgain, jnp.where(lane == FEAT, delta, shift)
+    )
+    copies_out += [
+        send(coef_ref.at[ty], coef_ref.at[ty], c_s.at[d - 1], c_r.at[d - 1], tys[d - 1])
+        for d in (1, 2, 3)
+    ]
+    finish(copies_out)
+
+
+def tower(part, lat, cot, fgain, hgain, tgain, ogain, vproj, weights):
+    _, rows, width = lat.shape
+    dma = pltpu.SemaphoreType.DMA
+    vmem = pl.BlockSpec(memory_space=pltpu.VMEM)
+    shape = jax.ShapeDtypeStruct
+    head = (8, rows, 128)
+    three = (8, 3 * rows, 128)
+    return pl.pallas_call(
+        tower_kernel,
+        out_shape=(
+            shape((4, rows, width), BFLOAT),
+            shape((8, rows, width), BFLOAT),
+            shape((8, rows, width), BFLOAT),
+            shape((rows, LANES), BFLOAT),
+            shape((rows, width), BFLOAT),
+            shape((rows, width), FLOAT),
+            shape((3, width), FLOAT),
+            shape((1, LANES), FLOAT),
+            shape((4, rows, LANES), FLOAT),
+        ),
+        in_specs=[vmem] * 8 + [pl.BlockSpec(memory_space=pl.ANY)] * 9,
+        out_specs=(vmem,) * 9,
+        scratch_shapes=[
+            pltpu.VMEM((9, width, width), BFLOAT),
+            pltpu.VMEM((3, rows, LANES), FLOAT),
+            pltpu.VMEM(three, BFLOAT),
+            pltpu.VMEM(three, BFLOAT),
+            pltpu.VMEM((8, 2 * rows, 128), BFLOAT),
+            pltpu.VMEM((2, 8 * rows, 8 * rows), FLOAT),
+            pltpu.VMEM(head, BFLOAT), pltpu.VMEM(head, BFLOAT),
+            pltpu.VMEM(head, BFLOAT), pltpu.VMEM(head, BFLOAT),
+            pltpu.VMEM((2, 8 * rows, 128), BFLOAT), pltpu.VMEM((2, 8 * rows, 128), BFLOAT),
+            pltpu.VMEM(three, BFLOAT), pltpu.VMEM(three, BFLOAT),
+            dma((9,)),
+            dma((3,)), dma((3,)), dma((7,)), dma((7,)), dma(()), dma(()), dma((7,)), dma((7,)),
+            dma((7,)), dma((7,)), dma(()), dma(()), dma((7,)), dma((7,)), dma((3,)), dma((3,)),
+            dma((3,)), dma((3,)),
+        ],
+        compiler_params=pltpu.CompilerParams(
+            collective_id=3, has_side_effects=True, vmem_limit_bytes=56 << 20
+        ),
+        name="tower",
+    )(part, lat, cot, fgain, hgain, tgain, ogain, vproj, *weights)
+
+
 def on_device_fast(
     pixels,
     pixel_mask,
@@ -346,141 +614,60 @@
     query_input = query_normed.astype(BFLOAT)
     own_queries = linear(query_input, query_proj).astype(BFLOAT)
     raw_query = linear_back(own_queries, key_proj) * cross_scale
-    scores = against_pixels(raw_query * feature_gain)
+    query_coefs = raw_query * (feature_gain * (1.0 / math.log(2.0)))
+    scores = against_pixels(query_coefs)
     row_top = jnp.max(jnp.where(live, scores, -1e30), axis=(2, 3))
-    all_top = lax.pmax(row_top, "ty")
-    row_exp = jnp.where(live, jnp.exp(scores - all_top[:, :, None, None]), 0.0)
-    row_total = lax.psum(jnp.sum(row_exp, axis=(2, 3)), "ty")
-    cross_exact = row_exp / row_total[:, :, None, None]
-    raw_mix = lax.psum(over_pixels(cross_exact), "ty")
-    mix = raw_mix * feature_gain
-    attended = linear(mix.astype(BFLOAT), value_proj)
-    attended_input = attended.astype(BFLOAT)
-    resid_one = latent_rows + linear(attended_input, cross_proj)
-    hidden_normed, back_hidden_norm = jax.vjp(layer_norm, resid_one, hidden_gain)
-    hidden_input = hidden_normed.astype(BFLOAT)
-    hidden_lifted, back_hidden_gelu = jax.vjp(gelu_tanh, linear(hidden_input, hidden_up))
-    hidden_act = hidden_lifted.astype(BFLOAT)
-    resid_two = resid_one + linear(hidden_act, hidden_down)
-    tower_normed, back_tower_norm = jax.vjp(layer_norm, resid_two, tower_gain)
-    tower_input = tower_normed.astype(BFLOAT)
-    tower_q = linear(tower_input, tower_query).astype(BFLOAT)
-    tower_k = linear(tower_input, tower_key).astype(BFLOAT)
-    tower_v = linear(tower_input, tower_value).astype(BFLOAT)
-    all_keys, all_values = (
-        lax.all_gather(tower_k, "tx", axis=1, tiled=True),
-        lax.all_gather(tower_v, "tx", axis=1, tiled=True),
-    )
-    split_q = tower_q.reshape(item_count, rows_here, head_count, head_size)
-    split_k = all_keys.reshape(item_count, -1, head_count, head_size)
-    split_v = all_values.reshape(item_count, -1, head_count, head_size)
-    tower_scores = (
-        jnp.einsum("bqhd,bkhd->bhqk", split_q, split_k, preferred_element_type=FLOAT) * tower_scale
-    )
-    tower_top = jnp.max(tower_scores, axis=3, keepdims=True)
-    tower_exp = jnp.exp(tower_scores - tower_top)
-    tower_total = jnp.sum(tower_exp, axis=3, keepdims=True)
-    tower_exact = tower_exp / tower_total
-    tower_probs = tower_exact.astype(BFLOAT)
-    mixed = jnp.einsum(
-        "bhqk,bkhd->bqhd", tower_probs, split_v, preferred_element_type=FLOAT
-    ).reshape(item_count, rows_here, model_width)
-    mixed_input = mixed.astype(BFLOAT)
-    resid_three = resid_two + linear(mixed_input, tower_proj)
-    final_normed, back_final_norm = jax.vjp(layer_norm, resid_three, final_gain)
-    final_input = final_normed.astype(BFLOAT)
-    final_lifted, back_final_gelu = jax.vjp(gelu_tanh, linear(final_input, final_up))
-    final_act = final_lifted.astype(BFLOAT)
-    resid_four = resid_three + linear(final_act, final_down)
-    grad_four = cotangent.astype(FLOAT)
-    grad_final_lift = back_final_gelu(linear_back(cotangent, final_down))[0].astype(BFLOAT)
-    grad_rows_three, final_gain_grad = back_final_norm(linear_back(grad_final_lift, final_up))
-    grad_three = grad_four + grad_rows_three
-    grad_tower_out = grad_three.astype(BFLOAT)
-    grad_mixed_flat = linear_back(grad_tower_out, tower_proj).astype(BFLOAT)
-    grad_mixed = grad_mixed_flat.reshape(item_count, rows_here, head_count, head_size)
-    grad_tower_p = jnp.einsum("bqhd,bkhd->bhqk", grad_mixed, split_v, preferred_element_type=FLOAT)
-    tower_delta = jnp.sum(tower_exact * grad_tower_p, axis=3, keepdims=True)
-    grad_tower_scores = (tower_exact * (grad_tower_p - tower_delta)).astype(BFLOAT)
-    grad_tower_q = (
-        (
-            jnp.einsum("bhqk,bkhd->bqhd", grad_tower_scores, split_k, preferred_element_type=FLOAT)
-            * tower_scale
-        )
-        .astype(BFLOAT)
-        .reshape(item_count, rows_here, model_width)
-    )
-    value_part = jnp.einsum(
-        "bhqk,bqhd->bkhd", tower_probs, grad_mixed, preferred_element_type=FLOAT
-    )
-    key_part = (
-        jnp.einsum("bhqk,bqhd->bkhd", grad_tower_scores, split_q, preferred_element_type=FLOAT)
-        * tower_scale
-    )
-    key_sums, value_sums = (
-        lax.psum_scatter(
-            key_part.reshape(item_count, -1, model_width), "tx", scatter_dimension=1, tiled=True
-        ),
-        lax.psum_scatter(
-            value_part.reshape(item_count, -1, model_width), "tx", scatter_dimension=1, tiled=True
-        ),
-    )
-    grad_tower_k = key_sums.astype(BFLOAT)
-    grad_tower_v = value_sums.astype(BFLOAT)
-    grad_tower_rows = (
-        linear_back(grad_tower_q, tower_query)
-        + linear_back(grad_tower_k, tower_key)
-        + linear_back(grad_tower_v, tower_value)
-    )
-    grad_rows_two, tower_gain_grad = back_tower_norm(grad_tower_rows)
-    grad_two = grad_three + grad_rows_two
-    grad_hidden_out = grad_two.astype(BFLOAT)
-    grad_hidden_lift = back_hidden_gelu(linear_back(grad_hidden_out, hidden_down))[0].astype(BFLOAT)
-    grad_rows_one, hidden_gain_grad = back_hidden_norm(linear_back(grad_hidden_lift, hidden_up))
-    grad_one = grad_two + grad_rows_one
-    grad_cross_out = grad_one.astype(BFLOAT)
-    grad_attended = linear_back(grad_cross_out, cross_proj).astype(BFLOAT)
-    raw_up = linear_back(grad_attended, value_proj)
-    grad_probs = against_pixels(raw_up * feature_gain)
-    cross_delta = jnp.sum(grad_attended.astype(FLOAT) * attended, axis=2)
-    grad_scores = cross_exact * (grad_probs - cross_delta[:, :, None, None])
+    row_exp = jnp.where(live, jnp.exp2(scores - row_top[:, :, None, None]), 0.0)
+    row_total = jnp.sum(row_exp, axis=(2, 3))
+    part = jnp.concatenate(
+        [over_pixels(row_exp), row_total[:, :, None], row_top[:, :, None],
+         jnp.zeros((item_count, rows_here, LANES - FEAT - 2), FLOAT)], axis=2
+    )
+    share = item_count * rows_here // lax.axis_size("ty")
+    ty_index = lax.axis_index("ty")
+
+    def in_shares(rows):
+        return rows.reshape(lax.axis_size("ty"), share, rows.shape[-1])
+
+    def own_share(rows):
+        return lax.dynamic_index_in_dim(in_shares(rows), ty_index, 0, keepdims=False)
+
+    def wide_lanes(rows):
+        return jnp.pad(rows, ((0, 0), (0, LANES - FEAT)))
+
+    gain_lanes = jnp.pad(feature_gain, (0, LANES - FEAT))[None]
+    value_rows = jnp.pad(value_proj, ((0, LANES - FEAT), (0, 0)))
+    result, lefts, rights, mix, g_cross, grad_one, gain_parts, feat_part, coefs = tower(
+        in_shares(part), in_shares(latents), in_shares(cotangent), gain_lanes,
+        hidden_gain[None], tower_gain[None], final_gain[None], value_rows,
+        (cross_proj, hidden_up, hidden_down, tower_query, tower_key, tower_value, tower_proj,
+         final_up, final_down),
+    )
+    coefs = coefs.reshape(item_count, rows_here, LANES)
+    grad_probs = against_pixels(coefs[:, :, :FEAT])
+    probs = jnp.where(live, jnp.exp2(scores - coefs[:, :, FEAT + 1][:, :, None, None]), 0.0)
+    grad_scores = probs * (grad_probs - coefs[:, :, FEAT][:, :, None, None])
     raw_grad_mix = lax.psum(over_pixels(grad_scores), "ty")
+    raw_grad_mix = own_share(raw_grad_mix)
     grad_mix = (raw_grad_mix * feature_gain).astype(BFLOAT)
     grad_queries = (linear(grad_mix, key_proj) * cross_scale).astype(BFLOAT)
-    feature_part = jnp.sum(raw_grad_mix * raw_query + raw_mix * raw_up, axis=(0, 1))
-    grad_latent_rows, query_gain_grad = back_query_norm(linear_back(grad_queries, query_proj))
-    latent_grad = grad_one + grad_latent_rows
-    share = item_count * rows_here // lax.axis_size("ty")
-    ty_index = lax.axis_index("ty")
-
-    def own_rows(rows):
-        return lax.dynamic_slice_in_dim(
-            rows.reshape(item_count * rows_here, -1), ty_index * share, share, 0
-        )
-
-    pairs = [
-        (final_act, cotangent),
-        (final_input, grad_final_lift),
-        (mixed_input, grad_tower_out),
-        (tower_input, grad_tower_q),
-        (tower_input, grad_tower_k),
-        (tower_input, grad_tower_v),
-        (hidden_act, grad_hidden_out),
-        (hidden_input, grad_hidden_lift),
-    ]
-    sums = weight_sums(
-        jnp.stack([own_rows(x) for x, _ in pairs]), jnp.stack([own_rows(g) for _, g in pairs])
-    ).astype(FLOAT)
-    quarter = 1.0 / lax.axis_size("ty")
+    feature_part = jnp.sum(raw_grad_mix * own_share(raw_query), axis=0) + feat_part[0, :FEAT]
+    own_latents, own_query_input = own_share(latent_rows), own_share(query_input)
+    unit, rate = norm_rows(own_latents)
+    grad_latent_rows, query_gain_grad = norm_rows_back(
+        linear_back(grad_queries, query_proj), query_gain[None], unit, rate
+    )
+    latent_grad = lax.all_gather(grad_one + grad_latent_rows, "ty", axis=0)
+    latent_grad = latent_grad.reshape(latents.shape)
+    sums = weight_sums(lefts, rights).astype(FLOAT)
     lanes = ((0, 11), (0, 0))
-    gains = jnp.stack(
-        [query_gain_grad, hidden_gain_grad, tower_gain_grad, final_gain_grad,
-         jnp.pad(feature_part, (0, model_width - FEAT))]
-    ) * quarter
+    gains = jnp.concatenate(
+        [query_gain_grad, gain_parts, jnp.pad(feature_part, (0, model_width - FEAT))[None]]
+    )
     joined = jnp.concatenate(
         [
-            jnp.pad(weight_grad(own_rows(mix).astype(BFLOAT), own_rows(grad_cross_out)), lanes),
-            jnp.pad(weight_grad(own_rows(grad_mix), own_rows(query_input)), lanes),
+            weight_grad(mix, g_cross)[:272],
+            jnp.pad(weight_grad(grad_mix, own_query_input), lanes),
             jnp.pad(gains, ((0, 27), (0, 0))),
         ]
     )
@@ -500,7 +687,7 @@
     gain_sums = joined[544:549].astype(FLOAT)
     gain_here = lax.dynamic_slice_in_dim(gain_sums, tx_from, wide, 1)
     return (
-        resid_four.astype(BFLOAT),
+        result.reshape(latents.shape),
         latent_grad,
         gain_sums[4, :FEAT],
         gain_here[0],

time: 771 us -> 407 us (0.53)
  waiting for transfers between devices: 307 us -> 0.04 us
  Pallas kernels: 137 us -> 199 us
  matrix products: 75.7 us -> 25.7 us
  local copies, waits for them, and re-layouts: 51.5 us -> 25.3 us
  blocking collectives: 76.9 us -> 56.8 us
  other arithmetic: 96.8 us -> 82.3 us
    reduce_scatter x2 -> x0, waiting for transfers between devices: 153 us -> none  [the longest x1 85.2 us: on_device_fast(): lax.psum_scatter(value_part.reshape(item_count, -1, model_width), 'tx', s...]
    all_gather x2 -> x0, waiting for transfers between devices: 89.7 us -> none  [the longest x1 45.1 us: on_device_fast(): lax.all_gather(tower_v, 'tx', axis=1, tiled=True)]
    pallas_call x0 -> x1, Pallas kernels: none -> 60.4 us  [tower(): pl.pallas_call(tower_kernel, out_shape=(shape((4, rows, width), BFLOAT),...]
    psum x1, waiting for transfers between devices: 32.3 us -> 0.02 us  [on_device_fast(): raw_grad_mix = lax.psum(over_pixels(grad_scores), 'ty')]
    psum x1 -> x0, waiting for transfers between devices: 31.6 us -> none  [on_device_fast(): raw_mix = lax.psum(over_pixels(cross_exact), 'ty')]
    dot_general x6 -> x0, matrix products: 18.7 us -> none  [the longest x1 5.74 us: on_device_fast(): jnp.einsum('bhqk,bqhd->bkhd', tower_probs, grad_mixed, preferred_element_...]
    pmax x1 -> x0, blocking collectives: 17.2 us -> none  [on_device_fast(): all_top = lax.pmax(row_top, 'ty')]
    dot_general x13 -> x3, matrix products: 23 us -> 6.56 us  [linear_back(): lax.dot_general(upstream, weight, (((upstream.ndim - 1,), (1,)), ((), ())...]
  transfers between devices with their start and end apart: 6 -> 1, of which waited for: 6 -> 0; matrix products, arithmetic and copies ran while one was open for 5% -> 1% of each run, Pallas kernels for 0% -> 22%
where the time goes in v2:
time: 407 us; the launch traced here: 405 us
  Pallas kernels  199 us (49%)
  other arithmetic  82.3 us (20%)
  blocking collectives  56.8 us (14%)
  matrix products  25.7 us (6%)
  local copies, waits for them, and re-layouts  25.3 us (6%)
  between operations  14.9 us (4%)
    pallas_call x1, Pallas kernels, weight_sums(): pl.pallas_call(weight_sums_kernel, out_shape=jax.ShapeDtypeStruct((count,...  90.7 us
    pallas_call x1, Pallas kernels, tower(): pl.pallas_call(tower_kernel, out_shape=(shape((4, rows, width), BFLOAT),...  60.4 us
    reduce_sum x2, other arithmetic, over_pixels(): jnp.sum(scaled * pixel_mean[:, None], axis=(2, 3))[:, :, None]  50.2 us
    pallas_call x1, Pallas kernels, all_sum(): pl.pallas_call(all_sum_kernel, out_shape=jax.ShapeDtypeStruct((4, 8, part...  48.4 us
    all_gather x1, blocking collectives, on_device_fast(): wide_pixels = lax.all_gather(pixels, 'tx', axis=3, tiled=True).astype(FLOAT)  26.6 us
    all_gather x1, blocking collectives, on_device_fast(): wide_mask = lax.all_gather(pixel_mask, 'tx', axis=2, tiled=True)  24.7 us
    reduce_max x1, other arithmetic, on_device_fast(): row_top = jnp.max(jnp.where(live, scores, -1e+30), axis=(2, 3))  9.78 us
  transfers between devices with their start and end apart: 1, of which 0 were waited for; matrix products, arithmetic and copies ran while one was open for 1% of the time, Pallas kernels for 22%

profile of v2, /device:TPU:1, one launch (start us, length us, event | category | flops | bytes accessed | tf_op | source)
XLA Modules:
  0.0 404.7 jit_solution(12950863002081524277)
XLA Ops:
  9.6 1.3 iota_compare_fusion.3
  10.8 26.6 %all_gather.13 = bf16[2,3,72,288]{2,0,3,1:T(2,128)(2,1)S(1)} all-gather(bf16[2,3,72,36]{2,0,3,1:T(2,128)(2,1)} %param.22), channel_id=1, replica_groups=mesh['ty'=4,'tx'=8] {'tx'}, dimensions={3}, use_global_device_ids=true | all-gather | bytes 279936 | tf_op jit(solution)/shard_map/all_gather | solution.py:569
  37.5 1.2 multiply_reduce_fusion.10
  40.0 1.6 fusion.50
  41.6 1.5 fusion.39
  46.9 2.9 fusion.61
  52.7 2.4 concatenate.29
  55.1 1.4 fusion.67
  57.3 24.7 %all_gather.12 = s32[2,72,288]{1,0,2:T(2,128)S(1)} all-gather(s32[2,72,36]{1,0,2:T(2,128)} %param.23), channel_id=1, replica_groups=mesh['ty'=4,'tx'=8] {'tx'}, dimensions={2}, use_global_device_ids=true | all-gather | bytes 186624 | tf_op jit(solution)/shard_map/all_gather | solution.py:570
  82.9 2.0 slice_bitcast_fusion.10
  84.9 1.8 copy.94
  86.7 1.8 copy.95
  92.5 9.8 %select_reduce_fusion = f32[2,64]{1,0:T(2,128)S(1)} fusion(f32[2,72,288]{2,1,0:T(8,128)S(1)} %get-tuple-element.69, f32[2,72,288]{2,1,0:T(8,128)S(1)} %get-tuple-element.70, f32[2,64]{1,0:T(2,128)} %get-tuple-element.67, f32[2,72,288]{2,1,0:T(8,128)} %copy.96, f32[2,64]{1,0:T(2,128)} %get-tuple-element.60, f32[2,72,288]{2,1,0:T(8,128)} %copy.95, ...), kind=kLoop, calls=%fused_computation.10 | loop fusion | flops 31850368 | bytes 1057792 | tf_op jit(solution)/shard_map/reduce_max | solution.py:619
  102.3 24.1 %multiply_reduce_fusion.4 = (f32[2,64]{1,0:T(2,128)S(1)}, f32[2,64,72]{2,1,0:T(8,128)}, f32[2,64]{1,0:T(2,128)S(1)}, f32[2,64]{1,0:T(2,128)S(1)}, f32[2,64]{1,0:...) fusion(f32[2,72,288]{2,1,0:T(8,128)S(1)} %get-tuple-element.69, f32[2,72,288]{2,1,0:T(8,128)S(1)} %get-tuple-element.70, ...), kind=kLoop, calls=%fused_computation.5 | loop fusion | flops 66308480 | bytes 1244672 | tf_op jit(solution)/shard_map/reduce_sum | solution.py:610
  127.3 2.0 fusion.68
  130.7 2.0 pad.32.vproj_ref
  133.9 1.6 maximum_maximum_fusion.part_ref
  135.6 60.4 %tower.1 = (bf16[4,32,1024]{2,1,0:T(8,128)(2,1)}, bf16[8,32,1024]{2,1,0:T(8,128)(2,1)}, bf16[8,32,1024]{2,1,0:T(8,128)(2,1)}, bf16[32,384]{1,0:T(8,128)(2,1)}, b...) custom-call(f32[4,32,384]{2,1,0:T(8,128)} %maximum_maximum_fusion.pa, ...), custom_call_target="tpu_custom_call" | custom-call | tf_op jit(solution)/shard_map/tower/pallas_call | solution.py:495
  196.0 1.6 fusion.23
  197.7 1.3 fusion.25
  199.0 1.3 slice_reduce_fusion.5
  201.5 26.1 %multiply_reduce_fusion = (f32[2,64]{1,0:T(2,128)}, f32[2,64]{1,0:T(2,128)S(1)}, f32[2,64]{1,0:T(2,128)S(1)}, f32[2,64]{1,0:T(2,128)S(1)}, f32[2,64,288]{2,1,0:T(8,128)}, /*index=5*/f32[2,64,72]{2,1,0:T(8,128)S(1)}) fusion(f32[2,72,288]{2,1,0:T(8,128)S(1)} %copy-done.13, f32[2,72,288]{2,1,0:T(8,128)S(1)} %copy-done.16, f32[2,72,288]{2,1,0:T(8,128)S(1)} %copy-done.15, ...), kind=kLoop, calls=%fused_computation | loop fusion | flops 95504896 | bytes 1431040 | tf_op jit(solution)/shard_map/reduce_sum | solution.py:610
  227.7 2.3 fusion.69
  230.0 1.9 fusion.13
  232.8 90.7 %weight_sums.1 = bf16[8,128,1024]{2,1,0:T(8,128)(2,1)S(1)} custom-call(bf16[8,32,1024]{2,1,0:T(8,128)(2,1)S(1)} %copy-done.1, bf16[8,32,1024]{2,1,0:T(8,128)(2,1)S(1)} %copy-done.2), custom_call_target="tpu_custom_call" | custom-call | tf_op jit(solution)/shard_map/weight_sums/pallas_call | solution.py:175
  324.1 2.0 slice_bitcast_fusion
  329.7 1.9 multiply_reduce_fusion.12
  333.0 48.4 %all_sum.1 = bf16[4,8,144,128]{3,2,1,0:T(8,128)(2,1)S(1)} custom-call(bf16[4,144,1024]{2,1,0:T(8,128)(2,1)S(1)} %bitcast.124), custom_call_target="tpu_custom_call" | custom-call | tf_op jit(solution)/shard_map/all_sum/pallas_call | solution.py:244
  382.0 1.7 convolution_multiply_fusion
  383.8 1.7 fusion.21
  385.6 2.0 fusion.19
  390.9 5.5 %all-gather = f32[128,1024]{1,0:T(8,128)S(1)} all-gather(f32[32,1024]{1,0:T(8,128)S(1)} %multiply_add_fusion), channel_id=2, replica_groups=mesh['ty'=4,'tx'=8] {'ty'}, dimensions={0}, use_global_device_ids=true | all-gather | bytes 655360 | tf_op jit(solution)/shard_map/all_gather | solution.py:660
  (166 shorter events, 32.1 us)
Async XLA Ops:
  7.2 39.7 %copy-start = (bf16[1024,1024]{1,0:T(8,128)(2,1)S(1)}, bf16[1024,1024]{1,0:T(8,128)(2,1)}, u32[]{:S(2)}) copy-start(bf16[1024,1024]{1,0:T(8,128)(2,1)} %param.29) | copy-start | bytes 6291460
  7.2 38.4 %copy-start.5 = (bf16[2,64,1024]{2,1,0:T(8,128)(2,1)S(1)}, bf16[2,64,1024]{2,1,0:T(8,128)(2,1)}, u32[]{:S(2)}) copy-start(bf16[2,64,1024]{2,1,0:T(8,128)(2,1)} %param.25) | copy-start | bytes 786436
  7.2 38.8 %copy-start.29 = (f32[261]{0:T(512)S(1)}, f32[261]{0:T(512)}, u32[]{:S(2)}) copy-start(f32[261]{0:T(512)} %param.27) | copy-start | bytes 3136
  7.2 38.8 %copy-start.27 = (f32[1024]{0:T(1024)S(1)}, f32[1024]{0:T(1024)}, u32[]{:S(2)}) copy-start(f32[1024]{0:T(1024)} %param.28) | copy-start | bytes 12292
  7.2 39.7 %copy-start.8 = (bf16[261,1024]{1,0:T(8,128)(2,1)S(1)}, bf16[261,1024]{1,0:T(8,128)(2,1)}, u32[]{:S(2)}) copy-start(bf16[261,1024]{1,0:T(8,128)(2,1)} %param.30) | copy-start | bytes 1603588
  7.3 321.5 %all-reduce.9.cloned.1.call-start = ((), (), s32[]{:S(2)}) async-start(), calls=%async_computation | async-start | bytes 393216 | tf_op jit(solution)/shard_map/psum | solution.py:650
  43.9 8.7 %copy-start.18 = (f32[2,288,64]{1,2,0:T(8,128)S(1)}, f32[2,288,64]{1,2,0:T(8,128)}, u32[]{:S(2)}) copy-start(f32[2,288,64]{1,2,0:T(8,128)} %get-tuple-element.87) | copy-start | bytes 442372
  50.8 146.8 %copy-start.7 = (f32[2,72,261]{2,1,0:T(8,128)}, f32[2,72,261]{2,1,0:T(8,128)S(1)}, u32[]{:S(2)}) copy-start(f32[2,72,261]{2,1,0:T(8,128)S(1)} %concatenate.28) | copy-start | bytes 451012
  55.1 140.9 %copy-start.3 = (f32[2,288,261]{1,2,0:T(8,128)}, f32[2,288,261]{1,2,0:T(8,128)S(1)}, u32[]{:S(2)}) copy-start(f32[2,288,261]{1,2,0:T(8,128)S(1)} %concatenate.29) | copy-start | bytes 1804036
  55.1 37.4 %copy-start.22 = (f32[2,64,72]{2,1,0:T(8,128)S(1)}, f32[2,64,72]{2,1,0:T(8,128)}, u32[]{:S(2)}) copy-start(f32[2,64,72]{2,1,0:T(8,128)} %fusion.66) | copy-start | bytes 110596
  55.1 47.2 %copy-start.34 = (f32[2,64]{1,0:T(2,128)S(1)}, f32[2,64]{1,0:T(2,128)}, u32[]{:S(2)}) copy-start(f32[2,64]{1,0:T(2,128)} %get-tuple-element.67) | copy-start | bytes 1540
  55.1 47.2 %copy-start.36 = (f32[2,64]{1,0:T(2,128)S(1)}, f32[2,64]{1,0:T(2,128)}, u32[]{:S(2)}) copy-start(f32[2,64]{1,0:T(2,128)} %get-tuple-element.59) | copy-start | bytes 1540
  55.1 47.2 %copy-start.38 = (f32[2,64]{1,0:T(2,128)S(1)}, f32[2,64]{1,0:T(2,128)}, u32[]{:S(2)}) copy-start(f32[2,64]{1,0:T(2,128)} %get-tuple-element.60) | copy-start | bytes 1540
  55.1 47.2 %copy-start.40 = (f32[2,64]{1,0:T(2,128)S(1)}, f32[2,64]{1,0:T(2,128)}, u32[]{:S(2)}) copy-start(f32[2,64]{1,0:T(2,128)} %get-tuple-element.61) | copy-start | bytes 1540
  91.2 36.1 %copy-start.23 = (pred[2,72,288]{2,1,0:T(8,128)(4,1)}, pred[2,72,288]{2,1,0:T(8,128)(4,1)S(1)}, u32[]{:S(2)}) copy-start(pred[2,72,288]{2,1,0:T(8,128)(4,1)S(1)} %and_and_fusion) | copy-start | bytes 124420
  92.4 9.8 %copy-start.10 = (f32[2,72,288]{2,1,0:T(8,128)}, f32[2,72,288]{2,1,0:T(8,128)S(1)}, u32[]{:S(2)}) copy-start(f32[2,72,288]{2,1,0:T(8,128)S(1)} %get-tuple-element.69) | copy-start | bytes 497668
  92.4 9.8 %copy-start.12 = (f32[2,72,288]{2,1,0:T(8,128)}, f32[2,72,288]{2,1,0:T(8,128)S(1)}, u32[]{:S(2)}) copy-start(f32[2,72,288]{2,1,0:T(8,128)S(1)} %get-tuple-element.70) | copy-start | bytes 497668
  135.5 65.9 %copy-start.11 = (f32[2,72,288]{2,1,0:T(8,128)S(1)}, f32[2,72,288]{2,1,0:T(8,128)}, u32[]{:S(2)}) copy-start(f32[2,72,288]{2,1,0:T(8,128)} %copy-done.10) | copy-start | bytes 497668
  135.5 65.9 %copy-start.13 = (f32[2,72,288]{2,1,0:T(8,128)S(1)}, f32[2,72,288]{2,1,0:T(8,128)}, u32[]{:S(2)}) copy-start(f32[2,72,288]{2,1,0:T(8,128)} %copy-done.12) | copy-start | bytes 497668
  135.5 65.9 %copy-start.14 = (f32[2,72,288]{2,1,0:T(8,128)S(1)}, f32[2,72,288]{2,1,0:T(8,128)}, u32[]{:S(2)}) copy-start(f32[2,72,288]{2,1,0:T(8,128)} %copy.94) | copy-start | bytes 497668
  135.5 65.9 %copy-start.15 = (f32[2,72,288]{2,1,0:T(8,128)S(1)}, f32[2,72,288]{2,1,0:T(8,128)}, u32[]{:S(2)}) copy-start(f32[2,72,288]{2,1,0:T(8,128)} %copy.95) | copy-start | bytes 497668
  135.5 65.9 %copy-start.16 = (f32[2,72,288]{2,1,0:T(8,128)S(1)}, f32[2,72,288]{2,1,0:T(8,128)}, u32[]{:S(2)}) copy-start(f32[2,72,288]{2,1,0:T(8,128)} %copy.96) | copy-start | bytes 497668
  135.5 65.9 %copy-start.17 = (f32[2,64,288]{2,1,0:T(8,128)S(1)}, f32[2,64,288]{2,1,0:T(8,128)}, u32[]{:S(2)}) copy-start(f32[2,64,288]{2,1,0:T(8,128)} %fusion.67) | copy-start | bytes 442372
  135.5 65.9 %copy-start.24 = (pred[2,72,288]{2,1,0:T(8,128)(4,1)S(1)}, pred[2,72,288]{2,1,0:T(8,128)(4,1)}, u32[]{:S(2)}) copy-start(pred[2,72,288]{2,1,0:T(8,128)(4,1)} %copy-done.23) | copy-start | bytes 124420
  135.6 65.9 %copy-start.35 = (f32[2,64]{1,0:T(2,128)S(1)}, f32[2,64]{1,0:T(2,128)}, u32[]{:S(2)}) copy-start(f32[2,64]{1,0:T(2,128)} %get-tuple-element.67) | copy-start | bytes 1540
  135.6 65.9 %copy-start.37 = (f32[2,64]{1,0:T(2,128)S(1)}, f32[2,64]{1,0:T(2,128)}, u32[]{:S(2)}) copy-start(f32[2,64]{1,0:T(2,128)} %get-tuple-element.59) | copy-start | bytes 1540
  135.6 65.9 %copy-start.39 = (f32[2,64]{1,0:T(2,128)S(1)}, f32[2,64]{1,0:T(2,128)}, u32[]{:S(2)}) copy-start(f32[2,64]{1,0:T(2,128)} %get-tuple-element.60) | copy-start | bytes 1540
  135.6 65.9 %copy-start.41 = (f32[2,64]{1,0:T(2,128)S(1)}, f32[2,64]{1,0:T(2,128)}, u32[]{:S(2)}) copy-start(f32[2,64]{1,0:T(2,128)} %get-tuple-element.61) | copy-start | bytes 1540
  197.6 34.3 %copy-start.6 = (bf16[2,64,1024]{2,1,0:T(8,128)(2,1)S(1)}, bf16[2,64,1024]{2,1,0:T(8,128)(2,1)}, u32[]{:S(2)}) copy-start(bf16[2,64,1024]{2,1,0:T(8,128)(2,1)} %param.25) | copy-start | bytes 786436
  200.3 32.5 %copy-start.1 = (bf16[8,32,1024]{2,1,0:T(8,128)(2,1)S(1)}, bf16[8,32,1024]{2,1,0:T(8,128)(2,1)}, u32[]{:S(2)}) copy-start(bf16[8,32,1024]{2,1,0:T(8,128)(2,1)} %get-tuple-element.35.x_ref) | copy-start | bytes 1572868
  200.3 32.5 %copy-start.2 = (bf16[8,32,1024]{2,1,0:T(8,128)(2,1)S(1)}, bf16[8,32,1024]{2,1,0:T(8,128)(2,1)}, u32[]{:S(2)}) copy-start(bf16[8,32,1024]{2,1,0:T(8,128)(2,1)} %get-tuple-element.36.g_ref) | copy-start | bytes 1572868
  383.8 12.5 %copy-start.21 = (bf16[4,32,1024]{2,1,0:T(8,128)(2,1)S(1)}, bf16[4,32,1024]{2,1,0:T(8,128)(2,1)}, u32[]{:S(2)}) copy-start(bf16[4,32,1024]{2,1,0:T(8,128)(2,1)} %get-tuple-element.28) | copy-start | bytes 786436
  (12 other events, 51.3 us)
Sparse Core Ops, SparseCore 0:
  232.1 30.6 all-reduce.8

commit v3 on v2

--- a/solution.py
+++ b/solution.py
@@ -2,6 +2,7 @@
 
 import jax
 import jax.numpy as jnp
+import numpy as np
 from jax import lax
 from jax.experimental import pallas as pl
 from jax.experimental.pallas import tpu as pltpu
@@ -67,10 +68,6 @@
 MESH = pl.DeviceIdType.MESH
 
 
-def peer_ty(ty, d):
-    return lax.rem(ty + d, lax.axis_size("ty"))
-
-
 def send(src, dst, send_sem, recv_sem, where):
     copy = pltpu.make_async_remote_copy(
         src_ref=src, dst_ref=dst, send_sem=send_sem, recv_sem=recv_sem,
@@ -87,179 +84,8 @@
     pl.semaphore_wait(barrier, len(places))
 
 
-def column_chunk(ref, index, width):
-    return ref[:, pl.ds(pl.multiple_of(index * width, width), width)]
-
-
 def outer(left, right):
     return lax.dot_general(left, right, (((0,), (0,)), ((), ())), preferred_element_type=FLOAT)
-
-
-def weight_sums_kernel(
-    x_ref, g_ref, out_ref,
-    xs, gs, ysend, yrecv, own, zsend, zrecv, last,
-    local_sem, xg_send, xg_recv, y_send, y_recv, z_send, z_recv, o_send, o_recv,
-):
-    ty, tx = lax.axis_index("ty"), lax.axis_index("tx")
-    z, y = tx // 2, lax.rem(tx, 2)
-    tys = [{"ty": lax.rem(ty + d, 4), "tx": tx} for d in (1, 2, 3)]
-    beside = {"ty": ty, "tx": 2 * z + 1 - y}
-    zs = [{"ty": ty, "tx": 2 * lax.rem(z + d, 4) + y} for d in (1, 2, 3)]
-    greet(tys + [beside] + zs)
-    rows = x_ref.shape[1]
-    started = []
-    gathers = [[], []]
-    for k in range(2):
-        for s, (src, dst) in enumerate(((x_ref, xs), (g_ref, gs))):
-            for d in (1, 2, 3):
-                gathers[k].append(send(
-                    src.at[4 * k + lax.rem(ty + d, 4)], dst.at[k, ty],
-                    xg_send.at[k, s, d - 1], xg_recv.at[k, s, d - 1], tys[d - 1],
-                ))
-            mine = pltpu.make_async_copy(src.at[4 * k + ty], dst.at[k, ty], local_sem.at[k, s])
-            mine.start()
-            gathers[k].append(mine)
-    ycopies = [[], []]
-    for k in range(2):
-        for copy in gathers[k]:
-            copy.wait()
-        gk = gs[k].reshape(4 * rows, -1)
-        for c in range(4):
-            part = xs[k, :, :, pl.ds(pl.multiple_of((2 * c + 1 - y) * 128, 128), 128)]
-            ysend[k, c] = outer(part.reshape(4 * rows, 128), gk).astype(BFLOAT)
-            ycopies[k].append(send(
-                ysend.at[k, c], yrecv.at[k, c], y_send.at[k, c], y_recv.at[k, c], beside
-            ))
-        for c in range(4):
-            at = lax.rem(z + c, 4)
-            part = xs[k, :, :, pl.ds(pl.multiple_of((2 * at + y) * 128, 128), 128)]
-            own[k, c] = outer(part.reshape(4 * rows, 128), gk)
-    zcopies = [[], []]
-    for k in range(2):
-        for copy in ycopies[k]:
-            copy.wait()
-        for c in (1, 2, 3, 0):
-            at = lax.rem(z + c, 4)
-            total = own[k, c] + yrecv[k, at].astype(FLOAT)
-            if c == 0:
-                own[k, c] = total
-            else:
-                zsend[k, c - 1] = total.astype(BFLOAT)
-                zcopies[k].append(send(
-                    zsend.at[k, c - 1], zrecv.at[k, c - 1],
-                    z_send.at[k, c - 1], z_recv.at[k, c - 1], zs[c - 1],
-                ))
-    for k in range(2):
-        for copy in zcopies[k]:
-            copy.wait()
-        total = own[k, 0]
-        for c in range(3):
-            total = total + zrecv[k, c].astype(FLOAT)
-        last[k] = total.astype(BFLOAT)
-        for d in (1, 2, 3):
-            started.append(send(
-                last.at[k], out_ref.at[4 * k + ty], o_send.at[k, d - 1], o_recv.at[k, d - 1],
-                tys[d - 1],
-            ))
-        mine = pltpu.make_async_copy(last.at[k], out_ref.at[4 * k + ty], local_sem.at[k, 0])
-        mine.start()
-        started.append(mine)
-    for copy in started:
-        copy.wait()
-
-
-def weight_sums(x, g):
-    count, rows, width = x.shape
-    dma = pltpu.SemaphoreType.DMA
-    block = (width // 8, width)
-    return pl.pallas_call(
-        weight_sums_kernel,
-        out_shape=jax.ShapeDtypeStruct((count,) + block, BFLOAT),
-        in_specs=[pl.BlockSpec(memory_space=pl.ANY)] * 2,
-        out_specs=pl.BlockSpec(memory_space=pl.ANY),
-        scratch_shapes=[
-            pltpu.VMEM((2, 4, rows, width), BFLOAT),
-            pltpu.VMEM((2, 4, rows, width), BFLOAT),
-            pltpu.VMEM((2, 4) + block, BFLOAT),
-            pltpu.VMEM((2, 4) + block, BFLOAT),
-            pltpu.VMEM((2, 4) + block, FLOAT),
-            pltpu.VMEM((2, 3) + block, BFLOAT),
-            pltpu.VMEM((2, 3) + block, BFLOAT),
-            pltpu.VMEM((2,) + block, BFLOAT),
-            dma((2, 2)), dma((2, 2, 3)), dma((2, 2, 3)), dma((2, 4)), dma((2, 4)),
-            dma((2, 3)), dma((2, 3)), dma((2, 3)), dma((2, 3)),
-        ],
-        compiler_params=pltpu.CompilerParams(
-            collective_id=1, has_side_effects=True, vmem_limit_bytes=48 << 20
-        ),
-        name="weight_sums",
-    )(x, g)
-
-
-def all_sum_kernel(
-    v_ref, out_ref, recv1, quarter, recv2, recv3, s1, r1, s2, r2, s3, r3, s4, r4, local_sem
-):
-    ty, tx = lax.axis_index("ty"), lax.axis_index("tx")
-    tys = [{"ty": lax.rem(ty + d, 4), "tx": tx} for d in (1, 2, 3)]
-    txs = [{"ty": ty, "tx": lax.rem(tx + d, 8)} for d in range(1, 8)]
-    greet(tys + txs)
-    copies = [
-        send(v_ref.at[lax.rem(ty + d, 4)], recv1.at[d - 1], s1.at[d - 1], r1.at[d - 1], tys[d - 1])
-        for d in (1, 2, 3)
-    ]
-    total = v_ref[ty].astype(FLOAT)
-    for d, copy in enumerate(copies):
-        copy.wait()
-        total = total + recv1[d].astype(FLOAT)
-    for c in range(8):
-        quarter[c] = total[:, c * 128 : c * 128 + 128].astype(BFLOAT)
-    copies = [
-        send(quarter.at[lax.rem(tx + d, 8)], recv2.at[d - 1], s2.at[d - 1], r2.at[d - 1], txs[d - 1])
-        for d in range(1, 8)
-    ]
-    total = quarter[tx].astype(FLOAT)
-    for d, copy in enumerate(copies):
-        copy.wait()
-        total = total + recv2[d].astype(FLOAT)
-    recv3[tx] = total.astype(BFLOAT)
-    copies = [
-        send(recv3.at[tx], recv3.at[tx], s3.at[d - 1], r3.at[d - 1], txs[d - 1])
-        for d in range(1, 8)
-    ]
-    for copy in copies:
-        copy.wait()
-    copies = [
-        send(recv3, out_ref.at[ty], s4.at[d - 1], r4.at[d - 1], tys[d - 1]) for d in (1, 2, 3)
-    ]
-    mine = pltpu.make_async_copy(recv3, out_ref.at[ty], local_sem)
-    mine.start()
-    for copy in copies + [mine]:
-        copy.wait()
-
-
-def all_sum(v):
-    rows, width = v.shape
-    part = rows // 4
-    dma = pltpu.SemaphoreType.DMA
-    out = pl.pallas_call(
-        all_sum_kernel,
-        out_shape=jax.ShapeDtypeStruct((4, 8, part, 128), BFLOAT),
-        in_specs=[pl.BlockSpec(memory_space=pltpu.VMEM)],
-        out_specs=pl.BlockSpec(memory_space=pl.ANY),
-        scratch_shapes=[
-            pltpu.VMEM((3, part, width), BFLOAT),
-            pltpu.VMEM((8, part, 128), BFLOAT),
-            pltpu.VMEM((7, part, 128), BFLOAT),
-            pltpu.VMEM((8, part, 128), BFLOAT),
-            dma((3,)), dma((3,)), dma((7,)), dma((7,)), dma((7,)), dma((7,)), dma((3,)), dma((3,)),
-            dma(()),
-        ],
-        compiler_params=pltpu.CompilerParams(
-            collective_id=2, has_side_effects=True, vmem_limit_bytes=32 << 20
-        ),
-        name="all_sum",
-    )(v.reshape(4, part, width))
-    return jnp.transpose(out, (0, 2, 1, 3)).reshape(rows, width)
 
 
 LANES = 384
@@ -299,10 +125,10 @@
 def tower_kernel(
     part_ref, lat_ref, cot_ref, fgain_ref, hgain_ref, tgain_ref, ogain_ref, vproj_ref,
     w0, w1, w2, w3, w4, w5, w6, w7, w8,
-    result_ref, x_ref, g_ref, mix_ref, gcross_ref, one_ref, gains_ref, feat_ref, coef_ref,
-    ws, part_in, qkv_out, qkv_in, kv_in, probs, mixed_out, mixed_in, gm_out, gm_in,
+    result_ref, xs_ref, gs_ref, mix_ref, gcross_ref, one_ref, gains_ref, feat_ref, coef_ref,
+    x_ref, g_ref, gcross_out, gains_out, ws, part_in, qkv_out, qkv_in, kv_in, probs, mixed_out, mixed_in, gm_out, gm_in,
     kvx_out, kvx_in, gqkv_out, gqkv_in,
-    w_sem, a_s, a_r, q_s, q_r, k_s, k_r, m_s, m_r, g_s, g_r, e_s, e_r, b_s, b_r, c_s, c_r, o_s, o_r,
+    w_sem, a_s, a_r, q_s, q_r, k_s, k_r, m_s, m_r, g_s, g_r, e_s, e_r, b_s, b_r, c_s, c_r, o_s, o_r, h_s, h_r, n_s, n_r,
 ):
     ty, tx = lax.axis_index("ty"), lax.axis_index("tx")
     tys = [{"ty": lax.rem(ty + d, 4), "tx": tx} for d in (1, 2, 3)]
@@ -333,6 +159,26 @@
     def finish(copies):
         for copy in copies:
             copy.wait()
+
+    handed = []
+    gains_out[...] = jnp.zeros_like(gains_out)
+
+    def put_gain(row, grad):
+        for h in range(4):
+            gains_out[h, row : row + 1] = grad[:, 256 * h : 256 * h + 256]
+
+    def hand_over(stack, into, k, s):
+        for d in (1, 2, 3):
+            handed.append(send(
+                stack.at[4 * k + lax.rem(ty + d, 4)], into.at[k, ty],
+                h_s.at[k, s, d - 1], h_r.at[k, s, d - 1], tys[d - 1],
+            ))
+        into[k, ty] = stack[4 * k + ty]
+
+    def hand_to_all(out, into, i, by_place):
+        for d in (1, 2, 3):
+            src = out.at[lax.rem(ty + d, 4)] if by_place else into.at[ty]
+            handed.append(send(src, into.at[ty], n_s.at[i, d - 1], n_r.at[i, d - 1], tys[d - 1]))
 
     copies = [
         send(part_ref.at[lax.rem(ty + d, 4)], part_in.at[d - 1], a_s.at[d - 1], a_r.at[d - 1], tys[d - 1])
@@ -349,7 +195,8 @@
     raw_mix = joined / total
     shift = top + jnp.log2(total)
     mix = (raw_mix * fgain).astype(BFLOAT)
-    mix_ref[...] = mix
+    mix_ref[ty] = mix
+    hand_to_all(None, mix_ref, 0, False)
     attended = dot_nn(mix, vproj_ref[...])
     finish(loads[:1])
     one = lat_ref[ty].astype(FLOAT) + times(attended.astype(BFLOAT), cross)
@@ -359,20 +206,22 @@
     finish(loads[1:2])
     act, act_slope = gelu_pair(times(hidden, up))
     act = act.astype(BFLOAT)
-    x_ref[6] = act
+    x_ref[5] = act
     finish(loads[2:3])
     two = one + times(act, down)
     t_unit, t_rate = norm_rows(two)
     trows = (t_unit * tgain_ref[...]).astype(BFLOAT)
     x_ref[3] = trows
     x_ref[4] = trows
-    x_ref[5] = trows
+    x_ref[6] = trows
     for s, i in enumerate((tq, tk, tv)):
         finish(loads[i : i + 1])
         value = times(trows, i).astype(BFLOAT)
         for h in range(8):
             qkv_out[h, 32 * s : 32 * s + 32] = value[:, 128 * h : 128 * h + 128]
-    finish(spread(qkv_out, qkv_in, q_s, q_r))
+    copies = spread(qkv_out, qkv_in, q_s, q_r)
+    hand_over(x_ref, xs_ref, 1, 0)
+    finish(copies)
     copies = [send(qkv_in.at[:, 32:96], kv_in, k_s, k_r, mate)]
     q = qkv_in[:, 0:32].reshape(256, 128)
     k1 = qkv_in[:, 32:64].reshape(256, 128)
@@ -403,26 +252,27 @@
     back_four = times_back(cot, fdown)
     finish(copies)
     mixed = jnp.concatenate([mixed_in[h] for h in range(8)], axis=1)
-    x_ref[2] = mixed
+    x_ref[1] = mixed
     three = two + times(mixed, tproj)
     o_unit, o_rate = norm_rows(three)
     ogain = ogain_ref[...]
     frows = (o_unit * ogain).astype(BFLOAT)
-    x_ref[1] = frows
+    x_ref[2] = frows
     fact, fact_slope = gelu_pair(times(frows, fup))
     fact = fact.astype(BFLOAT)
     x_ref[0] = fact
     g_lift = (back_four * fact_slope).astype(BFLOAT)
-    g_ref[1] = g_lift
+    g_ref[2] = g_lift
     g_three, o_grad = norm_rows_back(times_back(g_lift, fup), ogain, o_unit, o_rate)
-    gains_ref[2:3] = o_grad
+    put_gain(2, o_grad)
     g_three = cot.astype(FLOAT) + g_three
     g_tower = g_three.astype(BFLOAT)
-    g_ref[2] = g_tower
+    g_ref[1] = g_tower
     g_mixed = times_back(g_tower, tproj).astype(BFLOAT)
     for h in range(8):
         gm_out[h] = g_mixed[:, 128 * h : 128 * h + 128]
     copies = spread(gm_out, gm_in, g_s, g_r)
+    hand_over(x_ref, xs_ref, 0, 0)
     result_ref[ty] = (three + times(fact, fdown)).astype(BFLOAT)
     copies_out = [
         send(result_ref.at[ty], result_ref.at[ty], o_s.at[d - 1], o_r.at[d - 1], tys[d - 1])
@@ -454,22 +304,29 @@
     g_trows = None
     for s, i in enumerate((tq, tk, tv)):
         value = jnp.concatenate([gqkv_in[h, 32 * s : 32 * s + 32] for h in range(8)], axis=1)
-        g_ref[3 + s] = value
+        g_ref[(3, 4, 6)[s]] = value
         term = times_back(value, i)
         g_trows = term if g_trows is None else g_trows + term
+    hand_over(g_ref, gs_ref, 0, 1)
     g_two, t_grad = norm_rows_back(g_trows, tgain_ref[...], t_unit, t_rate)
-    gains_ref[1:2] = t_grad
+    put_gain(1, t_grad)
     g_two = g_three + g_two
     g_hidden = g_two.astype(BFLOAT)
-    g_ref[6] = g_hidden
+    g_ref[5] = g_hidden
     g_hlift = (times_back(g_hidden, down) * act_slope).astype(BFLOAT)
     g_ref[7] = g_hlift
+    hand_over(g_ref, gs_ref, 1, 1)
     g_one, h_grad = norm_rows_back(times_back(g_hlift, up), hgain_ref[...], h_unit, h_rate)
-    gains_ref[0:1] = h_grad
+    put_gain(0, h_grad)
+    gains_ref[ty] = gains_out[ty]
+    hand_to_all(gains_out, gains_ref, 1, True)
     g_one = g_two + g_one
     one_ref[...] = g_one
     g_cross = g_one.astype(BFLOAT)
-    gcross_ref[...] = g_cross
+    for h in range(4):
+        gcross_out[h] = g_cross[:, 256 * h : 256 * h + 256]
+    gcross_ref[ty] = gcross_out[ty]
+    hand_to_all(gcross_out, gcross_ref, 2, True)
     g_att = times_back(g_cross, cross).astype(BFLOAT)
     raw_up = dot_nt(g_att, vproj_ref[...])
     feat_ref[...] = jnp.sum(raw_mix * raw_up, axis=0, keepdims=True)
@@ -483,6 +340,7 @@
         for d in (1, 2, 3)
     ]
     finish(copies_out)
+    finish(handed)
 
 
 def tower(part, lat, cot, fgain, hgain, tgain, ogain, vproj, weights):
@@ -496,18 +354,22 @@
         tower_kernel,
         out_shape=(
             shape((4, rows, width), BFLOAT),
-            shape((8, rows, width), BFLOAT),
-            shape((8, rows, width), BFLOAT),
-            shape((rows, LANES), BFLOAT),
-            shape((rows, width), BFLOAT),
+            shape((2, 4, rows, width), BFLOAT),
+            shape((2, 4, rows, width), BFLOAT),
+            shape((4, rows, LANES), BFLOAT),
+            shape((4, rows, width // 4), BFLOAT),
             shape((rows, width), FLOAT),
-            shape((3, width), FLOAT),
+            shape((4, 8, width // 4), FLOAT),
             shape((1, LANES), FLOAT),
             shape((4, rows, LANES), FLOAT),
         ),
         in_specs=[vmem] * 8 + [pl.BlockSpec(memory_space=pl.ANY)] * 9,
         out_specs=(vmem,) * 9,
         scratch_shapes=[
+            pltpu.VMEM((8, rows, width), BFLOAT),
+            pltpu.VMEM((8, rows, width), BFLOAT),
+            pltpu.VMEM((4, rows, width // 4), BFLOAT),
+            pltpu.VMEM((4, 8, width // 4), FLOAT),
             pltpu.VMEM((9, width, width), BFLOAT),
             pltpu.VMEM((3, rows, LANES), FLOAT),
             pltpu.VMEM(three, BFLOAT),
@@ -521,13 +383,438 @@
             dma((9,)),
             dma((3,)), dma((3,)), dma((7,)), dma((7,)), dma(()), dma(()), dma((7,)), dma((7,)),
             dma((7,)), dma((7,)), dma(()), dma(()), dma((7,)), dma((7,)), dma((3,)), dma((3,)),
-            dma((3,)), dma((3,)),
+            dma((3,)), dma((3,)), dma((2, 2, 3)), dma((2, 2, 3)), dma((3, 3)), dma((3, 3)),
         ],
         compiler_params=pltpu.CompilerParams(
             collective_id=3, has_side_effects=True, vmem_limit_bytes=56 << 20
         ),
         name="tower",
     )(part, lat, cot, fgain, hgain, tgain, ogain, vproj, *weights)
+
+
+HALVES = 2
+GROUP = 128
+LOG2E = 1.0 / math.log(2.0)
+
+
+def split_two(values):
+    high = values.astype(BFLOAT)
+    return high, (values - high.astype(FLOAT)).astype(BFLOAT)
+
+
+def dot_wide(dot, values, high, low):
+    first, second = split_two(values)
+    return dot(first, high) + (dot(first, low) + dot(second, high))
+
+
+def coefs_by_pixel(coefs, thigh_ref, tlow_ref, into):
+    count = coefs.shape[0] // 2
+    for b in range(2):
+        wide = dot_wide(dot_nt, coefs[b * count : (b + 1) * count], thigh_ref[b], tlow_ref[b])
+        for half in range(HALVES):
+            at = pl.ds((half * 2 + b) * count, count)
+            rows = wide[:, half * GROUP : (half + 1) * GROUP]
+            for t in range(8):
+                high, low = split_two(rows + wide[:, (2 + t) * GROUP : (3 + t) * GROUP])
+                into[t, at, 0:GROUP] = high
+                into[t, at, GROUP : 2 * GROUP] = low
+
+
+def features_of(sums, scales, thigh_ref, tlow_ref):
+    count = sums.shape[1] // 4
+    blocks = [sums[t] if scales is None else sums[t] * scales[t] for t in range(8)]
+    joined = blocks[0]
+    for block in blocks[1:]:
+        joined = joined + block
+    outs = []
+    for b in range(2):
+        first, second = pl.ds(b * count, count), (2 + b) * count
+        lo, hi = slice(b * count, (b + 1) * count), slice((2 + b) * count, (3 + b) * count)
+        wide = jnp.concatenate(
+            [joined[lo], joined[hi]] + [block[lo] + block[hi] for block in blocks], axis=1
+        )
+        outs.append(dot_wide(dot_nn, wide, thigh_ref[b], tlow_ref[b]))
+    return jnp.concatenate(outs, axis=0)
+
+
+def rate_and_bias(block, group):
+    rate = block[group % 2 * 4 + group // 2 * 8 + 3 :][:1].astype(FLOAT)
+    return rate, jnp.where(rate == 0.0, -1e30, 0.0)
+
+
+def front_kernel(
+    msg_ref, lat_ref, qgain_ref, fgain_ref, qproj_ref, kproj_ref, thigh_ref, tlow_ref, hot_ref,
+    msgs_ref, coef_ref, part_ref, qrows_ref, raw_ref,
+    pixels, scores, weights, sums, tops, totals, rows_all, raw_all, s_sem, r_sem,
+):
+    ty, tx = lax.axis_index("ty"), lax.axis_index("tx")
+    txs = [{"ty": ty, "tx": lax.rem(tx + d, 8)} for d in range(1, 8)]
+    greet(txs)
+    copies = [
+        send(msg_ref, msgs_ref.at[tx], s_sem.at[d - 1], r_sem.at[d - 1], txs[d - 1])
+        for d in range(1, 8)
+    ]
+    msgs_ref[tx] = msg_ref[...]
+    pixels[0:GROUP] = hot_ref[...]
+    pixels[GROUP : 2 * GROUP] = hot_ref[...]
+    share = raw_ref.shape[0]
+    count = 2 * share
+    unit, _ = norm_rows(lat_ref[...].astype(FLOAT))
+    rows = (unit * qgain_ref[...]).astype(BFLOAT)
+    rows_all[...] = rows
+    queries = dot_nn(rows, qproj_ref[...]).astype(BFLOAT)
+    raw = dot_nt(queries, kproj_ref[...]) * (1.0 / math.sqrt(rows.shape[1]))
+    raw_all[...] = raw
+    mine = pl.ds(pl.multiple_of(ty * share, share), share)
+    qrows_ref[...] = rows_all[:, pl.ds(pl.multiple_of(ty * qrows_ref.shape[1], 128), qrows_ref.shape[1])]
+    raw_ref[...] = raw_all[mine]
+    coefs_by_pixel(raw * (fgain_ref[...] * LOG2E), thigh_ref, tlow_ref, coef_ref)
+    for copy in copies:
+        copy.wait()
+
+    def block_step(t, _):
+        block = msgs_ref[t]
+        pixels[0:16] = block
+        pixels[GROUP : GROUP + 16] = block
+        scores[...] = dot_nn(coef_ref[t], pixels[...])
+        for group in range(4):
+            at = pl.ds(group * count, count)
+            rate, bias = rate_and_bias(block, group)
+            s = scores[at] * rate + bias
+            top = jnp.max(s, axis=1, keepdims=True)
+            e = jnp.exp2(s - top)
+            tops[t, at] = top
+            totals[t, at] = jnp.sum(e, axis=1, keepdims=True)
+            weights[at] = (e * rate).astype(BFLOAT)
+        sums[t] = dot_nt(weights[...], pixels[0:GROUP])
+        return 0
+
+    lax.fori_loop(0, 8, block_step, 0)
+    top = tops[0]
+    for t in range(1, 8):
+        top = jnp.maximum(top, tops[t])
+    top = jnp.maximum(top[: 2 * count], top[2 * count :])
+    both = jnp.concatenate([top, top], axis=0)
+    scales = [jnp.exp2(tops[t] - both) for t in range(8)]
+    total = sum(totals[t] * scales[t] for t in range(8))
+    total = total[: 2 * count] + total[2 * count :]
+    feats = features_of(sums, scales, thigh_ref, tlow_ref)
+    lane = lax.broadcasted_iota(jnp.int32, feats.shape, 1)
+    part_ref[...] = jnp.where(
+        lane < FEAT, feats, jnp.where(lane == FEAT, total, top)
+    ).reshape(part_ref.shape)
+
+
+def front(msg, latents, query_gain, gain_lanes, query_proj, key_rows, thigh, tlow, hot):
+    count, here, width = latents.shape
+    share, length = count * here // 4, msg.shape[1]
+    rows = 4 * here
+    dma = pltpu.SemaphoreType.DMA
+    vmem = pl.BlockSpec(memory_space=pltpu.VMEM)
+    shape = jax.ShapeDtypeStruct
+    return pl.pallas_call(
+        front_kernel,
+        out_shape=(
+            shape((8, 16, length), BFLOAT),
+            shape((8, rows, 2 * GROUP), BFLOAT),
+            shape((4, share, LANES), FLOAT),
+            shape((4 * share, width // 4), BFLOAT),
+            shape((share, LANES), FLOAT),
+        ),
+        in_specs=[vmem] * 9,
+        out_specs=(vmem,) * 5,
+        scratch_shapes=[
+            pltpu.VMEM((2 * GROUP, length), BFLOAT),
+            pltpu.VMEM((rows, length), FLOAT),
+            pltpu.VMEM((rows, length), BFLOAT),
+            pltpu.VMEM((8, rows, GROUP), FLOAT),
+            pltpu.VMEM((8, rows, 1), FLOAT),
+            pltpu.VMEM((8, rows, 1), FLOAT),
+            pltpu.VMEM((4 * share, width), BFLOAT),
+            pltpu.VMEM((4 * share, LANES), FLOAT),
+            dma((7,)), dma((7,)),
+        ],
+        compiler_params=pltpu.CompilerParams(
+            collective_id=4, has_side_effects=True, vmem_limit_bytes=48 << 20
+        ),
+        name="front",
+    )(msg, latents.reshape(count * here, width), query_gain, gain_lanes, query_proj, key_rows, thigh, tlow, hot)
+
+
+def back_kernel(
+    msgs_ref, coef_ref, up_ref, one_ref, lat_ref, raw_ref, qgain_ref, fgain_ref, qproj_ref, kproj_ref,
+    thigh_ref, tlow_ref, hot_ref, xs_ref, gs_ref, mix_ref, gcross_ref, gains_ref, feat_ref, qrows_ref,
+    grad_ref, value_ref, key_ref, sums_ref,
+    pixels, upcoefs, scores, ups, weights, sums, part_out, part_in, gmix, qgains_out, qgains_in,
+    nsend, nextra, nrecv, nmore, ysend, yrecv, own, zsend, zrecv, last,
+    a_s, a_r, o_s, o_r, m_s, m_r, n_s, n_r, e_s, e_r, c_s, c_r, t_s, t_r,
+    y_s, y_r, z_s, z_r, w_s, w_r, l_s,
+):
+    ty, tx = lax.axis_index("ty"), lax.axis_index("tx")
+    z, y = tx // 2, lax.rem(tx, 2)
+    tys = [{"ty": lax.rem(ty + d, 4), "tx": tx} for d in (1, 2, 3)]
+    txs = [{"ty": ty, "tx": lax.rem(tx + d, 8)} for d in range(1, 8)]
+    beside = {"ty": ty, "tx": 2 * z + 1 - y}
+    zs = [{"ty": ty, "tx": 2 * lax.rem(z + d, 4) + y} for d in (1, 2, 3)]
+    greet(tys + txs)
+
+    def finish(copies):
+        for copy in copies:
+            copy.wait()
+
+    def to_tys(src, into, s_sem, r_sem, by_place=False):
+        return [
+            send(
+                src.at[lax.rem(ty + d, 4)] if by_place else src, into(d),
+                s_sem.at[d - 1], r_sem.at[d - 1], tys[d - 1],
+            )
+            for d in (1, 2, 3)
+        ]
+
+    share = raw_ref.shape[0]
+    count = 2 * share
+
+    def product_start(i, left, right, gains):
+        product = outer(left, right)
+        nsend[i] = product[0:256].astype(BFLOAT).reshape(8, 32, 256)
+        row = lax.broadcasted_iota(jnp.int32, (16, 256), 0)
+        more = product[256:272] + jnp.where(row < 8, 0.0, jnp.concatenate([gains, gains], axis=0))
+        nextra[i] = more.astype(BFLOAT)
+        main = [
+            send(nsend.at[i, lax.rem(tx + d, 8)], nrecv.at[i, d - 1], n_s.at[i, d - 1], n_r.at[i, d - 1], txs[d - 1])
+            for d in range(1, 8)
+        ]
+        return main + [
+            send(nextra.at[i], nmore.at[i, d - 1], e_s.at[i, d - 1], e_r.at[i, d - 1], txs[d - 1])
+            for d in range(1, 8)
+        ]
+
+    def product_join(i, copies, into):
+        finish(copies)
+        main = nsend[i, tx].astype(FLOAT)
+        more = nextra[i].astype(FLOAT)
+        for d in range(7):
+            main = main + nrecv[i, d].astype(FLOAT)
+            more = more + nmore[i, d].astype(FLOAT)
+        into[ty, pl.ds(pl.multiple_of(tx * 32, 32), 32)] = main.astype(BFLOAT)
+        into[ty, 256:272] = more.astype(BFLOAT)
+        here = into.at[ty, pl.ds(pl.multiple_of(tx * 32, 32), 32)]
+        return [send(here, here, c_s.at[i, d - 1], c_r.at[i, d - 1], txs[d - 1]) for d in range(1, 8)]
+
+    def product_end(i, copies, into):
+        finish(copies)
+        return to_tys(into.at[ty], lambda d: into.at[ty], t_s.at[i], t_r.at[i])
+
+    gain_rows = gains_ref[0] + gains_ref[1] + gains_ref[2] + gains_ref[3]
+    ncopies = product_start(
+        0, mix_ref[...].reshape(4 * share, LANES), gcross_ref[...].reshape(4 * share, 256), gain_rows
+    )
+    pixels[0:GROUP] = hot_ref[...]
+    pixels[GROUP : 2 * GROUP] = hot_ref[...]
+    coefs_by_pixel(up_ref[...].reshape(4 * share, LANES), thigh_ref, tlow_ref, upcoefs)
+
+    def block_step(t):
+        block = msgs_ref[t]
+        pixels[0:16] = block
+        pixels[GROUP : GROUP + 16] = block
+        scores[...] = dot_nn(coef_ref[t], pixels[...])
+        ups[...] = dot_nn(upcoefs[t], pixels[...])
+        for group in range(4):
+            at = pl.ds(group * count, count)
+            rate, bias = rate_and_bias(block, group)
+            b = group % 2
+            mine = up_ref[2 * b : 2 * b + 2].reshape(count, LANES)
+            p = jnp.exp2(scores[at] * rate + (bias - mine[:, FEAT + 1 : FEAT + 2]))
+            g = p * (ups[at] * rate - mine[:, FEAT : FEAT + 1])
+            weights[at] = (g * rate).astype(BFLOAT)
+        sums[t] = dot_nt(weights[...], pixels[0:GROUP])
+
+    def weight_block(k, chunk):
+        left = xs_ref[k, :, :, pl.ds(pl.multiple_of(chunk * 128, 128), 128)]
+        return outer(left.reshape(4 * share, 128), gs_ref[k].reshape(4 * share, -1))
+
+    def ycopy(k, c):
+        return pltpu.make_async_remote_copy(
+            src_ref=ysend.at[k, c], dst_ref=yrecv.at[k, c], send_sem=y_s.at[k, c],
+            recv_sem=y_r.at[k, c], device_id=beside, device_id_type=MESH,
+        )
+
+    def zcopy(k, c, where):
+        return pltpu.make_async_remote_copy(
+            src_ref=zsend.at[k, c], dst_ref=zrecv.at[k, c], send_sem=z_s.at[k, c],
+            recv_sem=z_r.at[k, c], device_id=where, device_id_type=MESH,
+        )
+
+    def first_steps(c, _):
+        block_step(c)
+        for k in range(2):
+            ysend[k, c] = weight_block(k, 2 * c + 1 - y).astype(BFLOAT)
+            ycopy(k, c).start()
+        return 0
+
+    def second_steps(c, _):
+        block_step(4 + c)
+        at = lax.rem(z + c + 1, 4)
+        for k in range(2):
+            ycopy(k, at).wait()
+            total = weight_block(k, 2 * at + y) + yrecv[k, at].astype(FLOAT)
+            zsend[k, c] = total.astype(BFLOAT)
+            zcopy(k, c, {"ty": ty, "tx": 2 * at + y}).start()
+        return 0
+
+    lax.fori_loop(0, 4, first_steps, 0)
+    ncopies = product_join(0, ncopies, value_ref)
+    lax.fori_loop(0, 3, second_steps, 0)
+    block_step(7)
+    part_out[...] = features_of(sums, None, thigh_ref, tlow_ref).reshape(part_out.shape)
+    tcopies = to_tys(part_out, lambda d: part_in.at[d - 1], a_s, a_r, True)
+    ncopies = product_end(0, ncopies, value_ref)
+    for k in range(2):
+        ycopy(k, z).wait()
+        own[k] = weight_block(k, 2 * z + y) + yrecv[k, z].astype(FLOAT)
+    unit, rate = norm_rows(lat_ref[ty].astype(FLOAT))
+    raw_mix = part_out[ty]
+    finish(tcopies)
+    for d in range(3):
+        raw_mix = raw_mix + part_in[d]
+    mix = (raw_mix * fgain_ref[...]).astype(BFLOAT)
+    gmix[ty] = mix
+    mcopies = to_tys(gmix.at[ty], lambda d: gmix.at[ty], m_s.at[0], m_r.at[0])
+    grad_q = (dot_nn(mix, kproj_ref[...]) * (1.0 / math.sqrt(qproj_ref.shape[0]))).astype(BFLOAT)
+    grad, qgain_grad = norm_rows_back(dot_nt(grad_q, qproj_ref[...]), qgain_ref[...], unit, rate)
+    qgains_out[...] = jnp.zeros_like(qgains_out)
+    features = feat_ref[...] + jnp.sum(raw_mix * raw_ref[...], axis=0, keepdims=True)
+    for h in range(4):
+        qgains_out[h, 0:1] = qgain_grad[:, 256 * h : 256 * h + 256]
+    qgains_out[0, 1:2] = features[:, 0:256]
+    qgains_out[1, 1:2, 0:128] = features[:, 256:384]
+    qgains_in[ty] = qgains_out[ty]
+    mcopies += to_tys(qgains_out, lambda d: qgains_in.at[ty], m_s.at[1], m_r.at[1], True)
+    grad_ref[ty] = (one_ref[...] + grad).astype(BFLOAT)
+    ncopies += to_tys(grad_ref.at[ty], lambda d: grad_ref.at[ty], o_s, o_r)
+    finish(mcopies)
+    gain_rows = qgains_in[0] + qgains_in[1] + qgains_in[2] + qgains_in[3]
+    mcopies = product_start(1, gmix[...].reshape(4 * share, LANES), qrows_ref[...], gain_rows)
+    for k in range(2):
+        total = own[k]
+        for c in range(3):
+            zcopy(k, c, zs[c]).wait()
+            total = total + zrecv[k, c].astype(FLOAT)
+        last[k] = total.astype(BFLOAT)
+        place = sums_ref.at[4 * k + ty]
+        ncopies += to_tys(last.at[k], lambda d: place, w_s.at[k], w_r.at[k])
+        mine = pltpu.make_async_copy(last.at[k], place, l_s.at[k])
+        mine.start()
+        ncopies.append(mine)
+    mcopies = product_join(1, mcopies, key_ref)
+    ncopies += product_end(1, mcopies, key_ref)
+    finish(ncopies)
+
+
+def back(msgs, coefs, up, one, lat, raw, query_gain, gain_lanes, query_proj, key_rows, thigh, tlow, hot,
+         xs, gs, mix, gcross, gains, feats, qrows):
+    _, share, width = lat.shape
+    rows, length = coefs.shape[1], msgs.shape[2]
+    dma = pltpu.SemaphoreType.DMA
+    vmem = pl.BlockSpec(memory_space=pltpu.VMEM)
+    shape = jax.ShapeDtypeStruct
+    block = (width // 8, width)
+    return pl.pallas_call(
+        back_kernel,
+        out_shape=(
+            shape((4, share, width), BFLOAT),
+            shape((4, 272, 256), BFLOAT),
+            shape((4, 272, 256), BFLOAT),
+            shape((8,) + block, BFLOAT),
+        ),
+        in_specs=[vmem] * 20,
+        out_specs=(vmem, vmem, vmem, pl.BlockSpec(memory_space=pl.ANY)),
+        scratch_shapes=[
+            pltpu.VMEM((2 * GROUP, length), BFLOAT),
+            pltpu.VMEM(coefs.shape, BFLOAT),
+            pltpu.VMEM((rows, length), FLOAT),
+            pltpu.VMEM((rows, length), FLOAT),
+            pltpu.VMEM((rows, length), BFLOAT),
+            pltpu.VMEM((8, rows, GROUP), FLOAT),
+            pltpu.VMEM((4, share, LANES), FLOAT),
+            pltpu.VMEM((3, share, LANES), FLOAT),
+            pltpu.VMEM((4, share, LANES), BFLOAT),
+            pltpu.VMEM((4, 8, 256), FLOAT),
+            pltpu.VMEM((4, 8, 256), FLOAT),
+            pltpu.VMEM((2, 8, 32, 256), BFLOAT),
+            pltpu.VMEM((2, 16, 256), BFLOAT),
+            pltpu.VMEM((2, 7, 32, 256), BFLOAT),
+            pltpu.VMEM((2, 7, 16, 256), BFLOAT),
+            pltpu.VMEM((2, 4) + block, BFLOAT),
+            pltpu.VMEM((2, 4) + block, BFLOAT),
+            pltpu.VMEM((2,) + block, FLOAT),
+            pltpu.VMEM((2, 3) + block, BFLOAT),
+            pltpu.VMEM((2, 3) + block, BFLOAT),
+            pltpu.VMEM((2,) + block, BFLOAT),
+            dma((3,)), dma((3,)), dma((3,)), dma((3,)), dma((2, 3)), dma((2, 3)),
+            dma((2, 7)), dma((2, 7)), dma((2, 7)), dma((2, 7)), dma((2, 7)), dma((2, 7)),
+            dma((2, 3)), dma((2, 3)), dma((2, 4)), dma((2, 4)), dma((2, 3)), dma((2, 3)),
+            dma((2, 3)), dma((2, 3)), dma((2,)),
+        ],
+        compiler_params=pltpu.CompilerParams(
+            collective_id=5, has_side_effects=True, vmem_limit_bytes=56 << 20
+        ),
+        name="back",
+    )(msgs, coefs, up, one, lat, raw, query_gain, gain_lanes, query_proj, key_rows, thigh, tlow, hot,
+      xs, gs, mix, gcross, gains, feats, qrows)
+
+
+def pixel_tables(image_sizes, row_ids, tile_width):
+    high = len(row_ids) // HALVES
+    all_cols = jnp.arange(8 * tile_width, dtype=jnp.int32)
+    row_table, row_coord, row_sum = axis_tables(image_sizes, row_ids, 3, 5)
+    col_table, col_coord, col_sum = axis_tables(image_sizes, all_cols, 4, 5 + 2 * BANDS)
+    row_table = row_table - row_sum[:, :, None] * (1.0 / FEAT)
+    col_table = col_table - col_sum[:, :, None] * (1.0 / FEAT)
+    row_table = row_table.reshape(2, HALVES, high, FEAT)
+    col_table = col_table.reshape(2, 8, tile_width, FEAT)
+    colours = np.zeros((2, HALVES, 16, FEAT), np.float32)
+    for b in range(2):
+        for half in range(HALVES):
+            for c in range(3):
+                colours[b, half, half * 8 + b * 4 + c] = -1.0 / FEAT
+                colours[b, half, half * 8 + b * 4 + c, c] += 1.0
+    first = jnp.concatenate(
+        [jnp.asarray(colours), row_table, jnp.zeros((2, HALVES, GROUP - 16 - high, FEAT), FLOAT)], axis=2
+    )
+    col_from = 16 + -(-high // 8) * 8
+    second = jnp.pad(col_table, ((0, 0), (0, 0), (col_from, GROUP - col_from - tile_width), (0, 0)))
+    table = jnp.concatenate([first, second], axis=1).reshape(2, 10 * GROUP, FEAT)
+    table = jnp.pad(table, ((0, 0), (0, 0), (0, LANES - FEAT)))
+    hot = np.zeros((GROUP, -(-high * tile_width // 128) * 128), np.float32)
+    for i in range(high):
+        for j in range(tile_width):
+            hot[16 + i, i * tile_width + j] = 1.0
+            hot[col_from + j, i * tile_width + j] = 1.0
+    here = lax.dynamic_slice_in_dim
+    at = lax.axis_index("tx") * tile_width
+    return (
+        split_two(table), jnp.asarray(hot, BFLOAT),
+        (row_coord, row_sum), (here(col_coord, at, tile_width, 1), here(col_sum, at, tile_width, 1)),
+    )
+
+
+def pixel_message(pixels, live, rows, cols, length):
+    (row_coord, row_sum), (col_coord, col_sum) = rows, cols
+    _, _, height, width = pixels.shape
+    wide = pixels.astype(FLOAT)
+    mean = (jnp.sum(wide, axis=1) + row_sum[:, :, None] + col_sum[:, None, :]) * (1.0 / FEAT)
+    square = (
+        jnp.sum(wide * wide, axis=1)
+        + (row_coord * row_coord)[:, :, None]
+        + (col_coord * col_coord)[:, None, :]
+        + 2.0 * BANDS
+    ) * (1.0 / FEAT)
+    rate = jnp.where(live, lax.rsqrt(square - mean * mean + EPSILON), 0.0)
+    rows = jnp.concatenate([pixels, rate.astype(BFLOAT)[:, None]], axis=1)
+    rows = rows.reshape(2, 4, HALVES, height // HALVES * width)
+    rows = jnp.transpose(rows, (2, 0, 1, 3)).reshape(16, -1)
+    return jnp.pad(rows, ((0, 0), (0, length - rows.shape[1])))
 
 
 def on_device_fast(
@@ -559,124 +846,48 @@
     tile_width = pixels.shape[3]
     model_width = latents.shape[2]
     rows_here = latents.shape[1]
-    head_count = HEADS
-    head_size = model_width // head_count
     cross_scale = 1.0 / math.sqrt(model_width)
-    tower_scale = 1.0 / math.sqrt(head_size)
     row_ids = lax.axis_index("ty") * tile_height + jnp.arange(tile_height, dtype=jnp.int32)
     col_ids = lax.axis_index("tx") * tile_width + jnp.arange(tile_width, dtype=jnp.int32)
-    all_cols = jnp.arange(tile_width * lax.axis_size("tx"), dtype=jnp.int32)
-    wide_pixels = lax.all_gather(pixels, "tx", axis=3, tiled=True).astype(FLOAT)
-    wide_mask = lax.all_gather(pixel_mask, "tx", axis=2, tiled=True)
     side_sizes = image_sizes[:, None, None]
     live = (
-        (wide_mask > 0)
+        (pixel_mask > 0)
         & (row_ids[None, :, None] < side_sizes)
-        & (all_cols[None, None, :] < side_sizes)
-    )[:, None]
-    row_table, row_coord, row_sum = axis_tables(image_sizes, row_ids, 3, 5)
-    col_table, col_coord, col_sum = axis_tables(image_sizes, all_cols, 4, 5 + 2 * BANDS)
-    pixel_mean = (
-        jnp.sum(wide_pixels, axis=1) + row_sum[:, :, None] + col_sum[:, None, :]
-    ) / FEAT
-    pixel_square = (
-        jnp.sum(wide_pixels * wide_pixels, axis=1)
-        + (row_coord * row_coord)[:, :, None]
-        + (col_coord * col_coord)[:, None, :]
-        + 2.0 * BANDS
-    ) / FEAT
-    pixel_rate = lax.rsqrt(pixel_square - pixel_mean * pixel_mean + EPSILON)
-    exact = lax.Precision.HIGHEST
-
-    def against_pixels(coefs):
-        by_row = jnp.einsum("blf,bif->bli", coefs, row_table, precision=exact)
-        by_col = jnp.einsum("blf,bjf->blj", coefs, col_table, precision=exact)
-        total = by_row[:, :, :, None] + by_col[:, :, None, :]
-        for c in range(3):
-            total = total + coefs[:, :, c][:, :, None, None] * wide_pixels[:, None, c]
-        total = total - jnp.sum(coefs, axis=2)[:, :, None, None] * pixel_mean[:, None]
-        return total * pixel_rate[:, None]
-
-    def over_pixels(weights):
-        scaled = weights * pixel_rate[:, None]
-        by_row = jnp.sum(scaled, axis=3)
-        by_col = jnp.sum(scaled, axis=2)
-        total = jnp.einsum("bli,bif->blf", by_row, row_table, precision=exact)
-        total = total + jnp.einsum("blj,bjf->blf", by_col, col_table, precision=exact)
-        colour = jnp.stack(
-            [jnp.sum(scaled * wide_pixels[:, None, c], axis=(2, 3)) for c in range(3)], axis=2
-        )
-        total = total + jnp.pad(colour, ((0, 0), (0, 0), (0, FEAT - 3)))
-        return total - jnp.sum(scaled * pixel_mean[:, None], axis=(2, 3))[:, :, None]
-
-    latent_rows = latents.astype(FLOAT)
-    query_normed, back_query_norm = jax.vjp(layer_norm, latent_rows, query_gain)
-    query_input = query_normed.astype(BFLOAT)
-    own_queries = linear(query_input, query_proj).astype(BFLOAT)
-    raw_query = linear_back(own_queries, key_proj) * cross_scale
-    query_coefs = raw_query * (feature_gain * (1.0 / math.log(2.0)))
-    scores = against_pixels(query_coefs)
-    row_top = jnp.max(jnp.where(live, scores, -1e30), axis=(2, 3))
-    row_exp = jnp.where(live, jnp.exp2(scores - row_top[:, :, None, None]), 0.0)
-    row_total = jnp.sum(row_exp, axis=(2, 3))
-    part = jnp.concatenate(
-        [over_pixels(row_exp), row_total[:, :, None], row_top[:, :, None],
-         jnp.zeros((item_count, rows_here, LANES - FEAT - 2), FLOAT)], axis=2
-    )
-    share = item_count * rows_here // lax.axis_size("ty")
-    ty_index = lax.axis_index("ty")
+        & (col_ids[None, None, :] < side_sizes)
+    )
+    (thigh, tlow), hot, rows, cols = pixel_tables(image_sizes, row_ids, tile_width)
+    message = pixel_message(pixels, live, rows, cols, hot.shape[1])
+    share = item_count * rows_here // 4
 
     def in_shares(rows):
-        return rows.reshape(lax.axis_size("ty"), share, rows.shape[-1])
-
-    def own_share(rows):
-        return lax.dynamic_index_in_dim(in_shares(rows), ty_index, 0, keepdims=False)
-
-    def wide_lanes(rows):
-        return jnp.pad(rows, ((0, 0), (0, LANES - FEAT)))
+        return rows.reshape(4, share, rows.shape[-1])
 
     gain_lanes = jnp.pad(feature_gain, (0, LANES - FEAT))[None]
     value_rows = jnp.pad(value_proj, ((0, LANES - FEAT), (0, 0)))
+    key_rows = jnp.pad(key_proj, ((0, LANES - FEAT), (0, 0)))
+    messages, pixel_coefs, part, query_rows, raw_query = front(
+        message, latents, query_gain[None], gain_lanes, query_proj, key_rows, thigh, tlow, hot
+    )
     result, lefts, rights, mix, g_cross, grad_one, gain_parts, feat_part, coefs = tower(
-        in_shares(part), in_shares(latents), in_shares(cotangent), gain_lanes,
+        part, in_shares(latents), in_shares(cotangent), gain_lanes,
         hidden_gain[None], tower_gain[None], final_gain[None], value_rows,
         (cross_proj, hidden_up, hidden_down, tower_query, tower_key, tower_value, tower_proj,
          final_up, final_down),
     )
-    coefs = coefs.reshape(item_count, rows_here, LANES)
-    grad_probs = against_pixels(coefs[:, :, :FEAT])
-    probs = jnp.where(live, jnp.exp2(scores - coefs[:, :, FEAT + 1][:, :, None, None]), 0.0)
-    grad_scores = probs * (grad_probs - coefs[:, :, FEAT][:, :, None, None])
-    raw_grad_mix = lax.psum(over_pixels(grad_scores), "ty")
-    raw_grad_mix = own_share(raw_grad_mix)
-    grad_mix = (raw_grad_mix * feature_gain).astype(BFLOAT)
-    grad_queries = (linear(grad_mix, key_proj) * cross_scale).astype(BFLOAT)
-    feature_part = jnp.sum(raw_grad_mix * own_share(raw_query), axis=0) + feat_part[0, :FEAT]
-    own_latents, own_query_input = own_share(latent_rows), own_share(query_input)
-    unit, rate = norm_rows(own_latents)
-    grad_latent_rows, query_gain_grad = norm_rows_back(
-        linear_back(grad_queries, query_proj), query_gain[None], unit, rate
-    )
-    latent_grad = lax.all_gather(grad_one + grad_latent_rows, "ty", axis=0)
-    latent_grad = latent_grad.reshape(latents.shape)
-    sums = weight_sums(lefts, rights).astype(FLOAT)
-    lanes = ((0, 11), (0, 0))
-    gains = jnp.concatenate(
-        [query_gain_grad, gain_parts, jnp.pad(feature_part, (0, model_width - FEAT))[None]]
-    )
-    joined = jnp.concatenate(
-        [
-            weight_grad(mix, g_cross)[:272],
-            jnp.pad(weight_grad(grad_mix, own_query_input), lanes),
-            jnp.pad(gains, ((0, 27), (0, 0))),
-        ]
-    )
-    joined = all_sum(joined.astype(BFLOAT))
-    cross_core = joined[:FEAT]
-    query_core = joined[272 : 272 + FEAT]
+    latent_grad, cross_core, query_core, sums = back(
+        messages, pixel_coefs, coefs, grad_one, in_shares(latents), raw_query, query_gain[None],
+        gain_lanes, query_proj, key_rows, thigh, tlow, hot, lefts, rights, mix, g_cross, gain_parts,
+        feat_part, query_rows
+    )
+    latent_grad = latent_grad.astype(FLOAT).reshape(latents.shape)
+    sums = sums.astype(FLOAT)
+    cross_core = jnp.transpose(cross_core, (1, 0, 2)).reshape(-1, model_width)
+    query_core = jnp.transpose(query_core, (1, 0, 2)).reshape(-1, model_width)
+    gain_sums = jnp.concatenate([query_core[264:266], cross_core[264:267]]).astype(FLOAT)
+    cross_core, query_core = cross_core[:FEAT], query_core[:FEAT]
     value_proj_grad = linear_back(cross_core, cross_proj)
     key_proj_grad = linear(query_core, query_proj) * cross_scale
-    wide = model_width // lax.axis_size("tx")
+    wide = model_width // 8
     tx_from = lax.axis_index("tx") * wide
     cross_proj_grad = weight_grad(
         lax.dynamic_slice_in_dim(value_proj, tx_from, wide, 1), cross_core
@@ -684,27 +895,26 @@
     query_proj_grad = weight_grad(
         lax.dynamic_slice_in_dim(query_core, tx_from, wide, 1), key_proj
     ) * cross_scale
-    gain_sums = joined[544:549].astype(FLOAT)
     gain_here = lax.dynamic_slice_in_dim(gain_sums, tx_from, wide, 1)
     return (
         result.reshape(latents.shape),
         latent_grad,
-        gain_sums[4, :FEAT],
+        gain_sums[1, :FEAT],
         gain_here[0],
         query_proj_grad,
         key_proj_grad,
         value_proj_grad,
         cross_proj_grad,
-        gain_here[1],
+        gain_here[2],
         sums[7],
-        sums[6],
-        gain_here[2],
+        sums[5],
+        gain_here[3],
         sums[3],
         sums[4],
-        sums[5],
+        sums[6],
+        sums[1],
+        gain_here[4],
         sums[2],
-        gain_here[3],
-        sums[1],
         sums[0],
     )
 

time: 407 us -> 229 us (0.56)
  other arithmetic: 82.3 us -> 9.82 us
  blocking collectives: 56.8 us -> 0 us
  matrix products: 25.7 us -> 6.61 us
  between operations: 14.9 us -> 1.17 us
  local copies, waits for them, and re-layouts: 25.3 us -> 15.5 us
  Pallas kernels: 199 us -> 192 us
    all_gather x3 -> x0, blocking collectives: 56.8 us -> none  [the longest x1 26.6 us: on_device_fast(): wide_pixels = lax.all_gather(pixels, 'tx', axis=3, tiled=True).astype(FLOAT)]
    reduce_sum x9 -> x1, other arithmetic: 55.8 us -> 0.15 us  [pixel_message(): jnp.sum(wide * wide, axis=1) + (row_coord * row_coord)[:, :, None]]
    dot_general x8 -> x0, matrix products: 12.7 us -> none  [the longest x2 4.23 us: over_pixels(): jnp.einsum('blj,bjf->blf', by_col, col_table, precision=exact)]
    reduce_max x1 -> x0, other arithmetic: 9.78 us -> none  [on_device_fast(): row_top = jnp.max(jnp.where(live, scores, -1e+30), axis=(2, 3))]
    mul x4 -> x1, local copies, waits for them, and re-layouts: 6.45 us -> 0.1 us  [pixel_message(): col_coord * col_coord]
    pallas_call x1, Pallas kernels: 60.4 us -> 54.2 us  [tower(): pl.pallas_call(tower_kernel, out_shape=(shape((4, rows, width), BFLOAT),...]
    unnamed x89 -> x54, local copies, waits for them, and re-layouts: 2.03 us -> 7.19 us
    dot_general x3 -> x1, matrix products: 6.56 us -> 1.76 us  [linear_back(): lax.dot_general(upstream, weight, (((upstream.ndim - 1,), (1,)), ((), ())...]
  transfers between devices with their start and end apart: 1 -> 0, of which waited for: 0 -> 0; matrix products, arithmetic and copies ran while one was open for 1% -> 0% of each run, Pallas kernels for 22% -> 0%
where the time goes in v3:
time: 229 us; the launch traced here: 225 us
  Pallas kernels  192 us (84%)
  local copies, waits for them, and re-layouts  15.5 us (7%)
  other arithmetic  9.82 us (4%)
  matrix products  6.61 us (3%)
    pallas_call x1, Pallas kernels, back(): pl.pallas_call(back_kernel, out_shape=(shape((4, share, width), BFLOAT),...  113 us
    pallas_call x1, Pallas kernels, tower(): pl.pallas_call(tower_kernel, out_shape=(shape((4, rows, width), BFLOAT),...  54.2 us
    pallas_call x1, Pallas kernels, front(): pl.pallas_call(front_kernel, out_shape=(shape((8, 16, length), BFLOAT), s...  24.4 us
    unnamed x54, local copies, waits for them, and re-layouts  7.19 us

profile of v3, /device:TPU:1, one launch (start us, length us, event | category | flops | bytes accessed | tf_op | source)
XLA Modules:
  0.0 224.8 jit_solution(16606037214548193171)
XLA Ops:
  0.7 0.7 convert_add_fusion
  1.5 0.3 fusion.7
  2.1 0.4 multiply_cosine_fusion.2
  3.0 0.8 fusion.1
  3.9 1.2 multiply_cosine_fusion
  5.4 0.8 concatenate.34
  6.4 0.3 select_maximum_fusion
  6.7 0.2 pad_convert_fusion.thigh_ref
  7.0 1.7 subtract_convert_fusion.tlow_ref
  10.4 24.4 %front.1 = (bf16[8,16,1408]{2,1,0:T(8,128)(2,1)S(1)}, bf16[8,256,256]{2,1,0:T(8,128)(2,1)S(1)}, f32[4,32,384]{2,1,0:T(8,128)S(1)}, bf16[128,256]{1,0:T(8,128)(2,1)S(1)}, f32[32,384]{1,0:T(8,128)S(1)}) custom-call(bf16[16,1408]{1,0:T(8,128)(2,1)S(1)} %pad.23.msg_ref, bf16[128,1024]{1,0:T(8,128)(2,1)S(1)} %bitcast.60, f32[1,1024]{1,0:T(1,128)S(1)} %bitcast.62, ...), custom_call_target="tpu_custom_call" | custom-call | tf_op jit(solution)/shard_map/front/pallas_call | solution.py:515
  34.9 1.0 copy-done.4
  35.8 0.7 copy-done.5
  36.6 0.7 copy-done.6
  37.3 0.6 copy-done.7
  37.9 0.6 copy-done.8
  38.5 1.0 pad.28.vproj_ref
  39.5 54.2 %tower.1 = (bf16[4,32,1024]{2,1,0:T(8,128)(2,1)}, bf16[2,4,32,1024]{3,2,1,0:T(8,128)(2,1)}, bf16[2,4,32,1024]{3,2,1,0:T(8,128)(2,1)}, bf16[4,32,384]{2,1,0:T(8,1...) custom-call(f32[4,32,384]{2,1,0:T(8,128)} %copy-done.6, ...), custom_call_target="tpu_custom_call" | custom-call | tf_op jit(solution)/shard_map/tower/pallas_call | solution.py:353
  93.7 113.0 %back.1 = (bf16[4,32,1024]{2,1,0:T(8,128)(2,1)}, bf16[4,272,256]{2,1,0:T(8,128)(2,1)}, bf16[4,272,256]{2,1,0:T(8,128)(2,1)}, bf16[8,128,1024]{2,1,0:T(8,128)(2,1)}) custom-call(bf16[8,16,1408]{2,1,0:T(8,128)(2,1)} %copy-done.5, bf16[8,256,256]{2,1,0:T(8,128)(2,1)} %copy-done.4, f32[4,32,384]{2,1,0:T(8,128)} %get-tuple-element.41.up_ref, ...), custom_call_target="tpu_custom_call" | custom-call | tf_op jit(solution)/shard_map/back/pallas_call | solution.py:722
  206.7 2.0 convert_element_type.81
  208.8 2.0 slice_bitcast_fusion
  211.4 1.0 copy-done.12
  212.4 1.7 convolution_multiply_fusion
  214.7 1.0 copy-done.11
  215.8 1.8 fusion.16
  217.5 1.1 convolution_multiply_fusion.1
  218.6 2.0 fusion.3
  220.7 0.7 slice.85
  221.4 0.7 slice.84
  222.1 0.5 slice_bitcast_fusion.8
  222.7 0.6 slice_reduce_fusion
  223.3 0.8 bitcast_convert_fusion
  224.1 0.7 copy.64
  (97 shorter events, 4.2 us)
Async XLA Ops:
  5.3 1.0 copy-start.20
  7.0 3.4 %copy-start = (bf16[2,1280,384]{2,1,0:T(8,128)(2,1)}, bf16[2,1280,384]{2,1,0:T(8,128)(2,1)S(1)}, u32[]{:S(2)}) copy-start(bf16[2,1280,384]{2,1,0:T(8,128)(2,1)S(1)} %pad_convert_fusion.thigh_ref) | copy-start | bytes 5898244
  7.0 2.0 copy-start.23
  7.0 2.2 copy-start.19
  7.0 2.3 %copy-start.21 = (s32[2,72,36]{1,0,2:T(2,128)S(1)}, s32[2,72,36]{1,0,2:T(2,128)}, u32[]{:S(2)}) copy-start(s32[2,72,36]{1,0,2:T(2,128)} %param.25) | copy-start | bytes 62212
  7.0 3.2 %copy-start.22 = (f32[261]{0:T(512)S(1)}, f32[261]{0:T(512)}, u32[]{:S(2)}) copy-start(f32[261]{0:T(512)} %param.29) | copy-start | bytes 3136
  7.0 3.2 %copy-start.13 = (bf16[261,1024]{1,0:T(8,128)(2,1)S(1)}, bf16[261,1024]{1,0:T(8,128)(2,1)}, u32[]{:S(2)}) copy-start(bf16[261,1024]{1,0:T(8,128)(2,1)} %param.32) | copy-start | bytes 1603588
  8.7 1.7 copy-start.2
  8.7 1.7 copy-start.3
  8.7 1.7 copy-start.10
  10.3 24.6 %copy-start.9 = (f32[1,384]{1,0:T(1,128)}, f32[1,384]{1,0:T(1,128)S(1)}, u32[]{:S(2)}) copy-start(f32[1,384]{1,0:T(1,128)S(1)} %broadcast_in_dim.27.fgain_ref) | copy-start | bytes 4612
  10.4 24.5 %copy-start.1 = (bf16[384,1024]{1,0:T(8,128)(2,1)}, bf16[384,1024]{1,0:T(8,128)(2,1)S(1)}, u32[]{:S(2)}) copy-start(bf16[384,1024]{1,0:T(8,128)(2,1)S(1)} %pad.25.kproj_ref) | copy-start | bytes 2359300
  10.4 28.1 %copy-start.14 = (bf16[261,1024]{1,0:T(8,128)(2,1)S(1)}, bf16[261,1024]{1,0:T(8,128)(2,1)}, u32[]{:S(2)}) copy-start(bf16[261,1024]{1,0:T(8,128)(2,1)} %param.33) | copy-start | bytes 1603588
  34.9 1.0 copy-start.4
  35.8 0.7 copy-start.5
  36.6 0.7 copy-start.6
  37.3 0.6 copy-start.7
  37.9 0.6 copy-start.8
  208.8 2.1 copy-start.16
  210.8 1.6 copy-start.12
  212.4 1.7 copy-start.15
  214.2 1.6 copy-start.11
  217.5 5.7 %copy-start.17 = (bf16[4,32,1024]{2,1,0:T(8,128)(2,1)S(1)}, bf16[4,32,1024]{2,1,0:T(8,128)(2,1)}, u32[]{:S(2)}) copy-start(bf16[4,32,1024]{2,1,0:T(8,128)(2,1)} %get-tuple-element.51) | copy-start | bytes 786436
  217.5 6.6 %copy-start.18 = (bf16[4,32,1024]{2,1,0:T(8,128)(2,1)S(1)}, bf16[4,32,1024]{2,1,0:T(8,128)(2,1)}, u32[]{:S(2)}) copy-start(bf16[4,32,1024]{2,1,0:T(8,128)(2,1)} %get-tuple-element.38) | copy-start | bytes 786436

commit v4 on v0

--- a/solution.py
+++ b/solution.py
@@ -2,7 +2,10 @@
 
 import jax
 import jax.numpy as jnp
+import numpy as np
 from jax import lax
+from jax.experimental import pallas as pl
+from jax.experimental.pallas import tpu as pltpu
 from jax.sharding import PartitionSpec as P
 
 BANDS = 64
@@ -47,28 +50,832 @@
     )
 
 
-def pixel_features(pixels, image_sizes, row_ids, col_ids):
+def axis_tables(image_sizes, ids, coord_lane, first_lane):
+    side = image_sizes.astype(FLOAT)[:, None]
+    coord = -1.0 + 2.0 * ids.astype(FLOAT)[None, :] / (side - 1.0)
+    band = jnp.arange(BANDS, dtype=jnp.int32).astype(FLOAT)
+    frequency = 1.0 + band[None, :] * (side * 0.5 - 1.0) / (BANDS - 1)
+    angle = math.pi * coord[:, :, None] * frequency[:, None, :]
+    waves = jnp.concatenate([jnp.sin(angle), jnp.cos(angle)], axis=2)
+    count, length = coord.shape
+    lead = jnp.zeros((count, length, coord_lane), FLOAT)
+    gap = jnp.zeros((count, length, first_lane - coord_lane - 1), FLOAT)
+    tail = jnp.zeros((count, length, FEAT - first_lane - 2 * BANDS), FLOAT)
+    table = jnp.concatenate([lead, coord[:, :, None], gap, waves, tail], axis=2)
+    return table, coord, jnp.sum(waves, axis=2) + coord
+
+
+MESH = pl.DeviceIdType.MESH
+
+
+def send(src, dst, send_sem, recv_sem, where):
+    copy = pltpu.make_async_remote_copy(
+        src_ref=src, dst_ref=dst, send_sem=send_sem, recv_sem=recv_sem,
+        device_id=where, device_id_type=MESH,
+    )
+    copy.start()
+    return copy
+
+
+def greet(places):
+    barrier = pltpu.get_barrier_semaphore()
+    for place in places:
+        pl.semaphore_signal(barrier, inc=1, device_id=place, device_id_type=MESH)
+    pl.semaphore_wait(barrier, len(places))
+
+
+def outer(left, right):
+    return lax.dot_general(left, right, (((0,), (0,)), ((), ())), preferred_element_type=FLOAT)
+
+
+LANES = 384
+CUBE = 0.044715
+SLOPE = 0.7978845608028654
+
+
+def norm_rows(rows):
+    shifted = rows - jnp.mean(rows, axis=-1, keepdims=True)
+    rate = lax.rsqrt(jnp.mean(shifted * shifted, axis=-1, keepdims=True) + EPSILON)
+    return shifted * rate, rate
+
+
+def norm_rows_back(upstream, gain, unit, rate):
+    scaled = upstream * gain
+    along = jnp.mean(scaled * unit, axis=-1, keepdims=True)
+    grad = rate * (scaled - jnp.mean(scaled, axis=-1, keepdims=True) - unit * along)
+    return grad, jnp.sum(upstream * unit, axis=0, keepdims=True)
+
+
+def gelu_pair(values):
+    square = values * values
+    bend = jnp.tanh(SLOPE * (values + CUBE * values * square))
+    half = 0.5 * (1.0 + bend)
+    slope = half + 0.5 * values * (1.0 - bend * bend) * (SLOPE * (1.0 + 3.0 * CUBE * square))
+    return values * half, slope
+
+
+def dot_nt(left, right):
+    return lax.dot_general(left, right, (((1,), (1,)), ((), ())), preferred_element_type=FLOAT)
+
+
+def dot_nn(left, right):
+    return lax.dot_general(left, right, (((1,), (0,)), ((), ())), preferred_element_type=FLOAT)
+
+
+HALVES = 2
+GROUP = 128
+LOG2E = 1.0 / math.log(2.0)
+
+
+def split_two(values):
+    high = values.astype(BFLOAT)
+    return high, (values - high.astype(FLOAT)).astype(BFLOAT)
+
+
+def dot_wide(dot, values, high, low):
+    first, second = split_two(values)
+    return dot(first, high) + (dot(first, low) + dot(second, high))
+
+
+def coefs_by_pixel(coefs, thigh_ref, tlow_ref, into):
+    count = coefs.shape[0] // 2
+    for b in range(2):
+        wide = dot_wide(dot_nt, coefs[b * count : (b + 1) * count], thigh_ref[b], tlow_ref[b])
+        for half in range(HALVES):
+            at = pl.ds((half * 2 + b) * count, count)
+            rows = wide[:, half * GROUP : (half + 1) * GROUP]
+            for t in range(8):
+                high, low = split_two(rows + wide[:, (2 + t) * GROUP : (3 + t) * GROUP])
+                into[t, at, 0:GROUP] = high
+                into[t, at, GROUP : 2 * GROUP] = low
+
+
+def features_of(sums, scales, thigh_ref, tlow_ref):
+    count = sums.shape[1] // 4
+    blocks = [sums[t] if scales is None else sums[t] * scales[t] for t in range(8)]
+    joined = blocks[0]
+    for block in blocks[1:]:
+        joined = joined + block
+    outs = []
+    for b in range(2):
+        first, second = pl.ds(b * count, count), (2 + b) * count
+        lo, hi = slice(b * count, (b + 1) * count), slice((2 + b) * count, (3 + b) * count)
+        wide = jnp.concatenate(
+            [joined[lo], joined[hi]] + [block[lo] + block[hi] for block in blocks], axis=1
+        )
+        outs.append(dot_wide(dot_nn, wide, thigh_ref[b], tlow_ref[b]))
+    return jnp.concatenate(outs, axis=0)
+
+
+def rate_and_bias(block, group):
+    rate = block[group % 2 * 4 + group // 2 * 8 + 3 :][:1].astype(FLOAT)
+    return rate, jnp.where(rate == 0.0, -1e30, 0.0)
+
+
+class Ring:
+    def __init__(self, places, send_sems, recv_sems):
+        self.places, self.sems = places, (send_sems, recv_sems)
+
+    def copy(self, i, d, src, dst):
+        return pltpu.make_async_remote_copy(
+            src_ref=src, dst_ref=dst, send_sem=self.sems[0].at[i, d], recv_sem=self.sems[1].at[i, d],
+            device_id=self.places[d], device_id_type=MESH,
+        )
+
+    def start(self, i, sources, into):
+        copies = [self.copy(i, d, sources(d), into(d)) for d in range(len(self.places))]
+        for copy in copies:
+            copy.start()
+        return copies
+
+
+def finish(*groups):
+    for copies in groups:
+        for copy in copies:
+            copy.wait()
+
+
+def main_kernel(
+    msg_ref, lat_ref, cot_ref, fgain_ref, qgain_ref, hgain_ref, tgain_ref, ogain_ref,
+    kproj_ref, vproj_ref, thigh_ref, tlow_ref, hot_ref,
+    w0, w1, w2, w3, w4, w5, w6, w7, w8, w9,
+    result_ref, grad_ref, value_ref, key_ref, sums_ref,
+    ws, msgs, pixcoefs, upcoefs, pixels, scores, ups, weights, sums, tops, totals, raw_all, qrows,
+    part_out, part_in, q_out, q_in, kv_out, kv_in, kv_more, probs, mixed_out, mixed_in, gm_out, gm_in,
+    kvx_out, kvx_in, gq_in, gkv_in, up_ref, mix_all, gcross_out, gcross_all, gains_out, gains_all, gmix,
+    x_out, x_pass, x_all, g_out, g_all, own, zsend, zrecv, last, nsend, nextra, nrecv, nmore,
+    w_sem, l_sem, ty_s, ty_r, tx_s, tx_r, mate_s, mate_r, xg_s, xg_r, y_s, y_r, z_s, z_r, o_s, o_r,
+):
+    ty, tx = lax.axis_index("ty"), lax.axis_index("tx")
+    z, y = tx // 2, lax.rem(tx, 2)
+    tys = [{"ty": lax.rem(ty + d, 4), "tx": tx} for d in (1, 2, 3)]
+    txs = [{"ty": ty, "tx": lax.rem(tx + d, 8)} for d in range(1, 8)]
+    mate = {"ty": 2 * (ty // 2) + 1 - lax.rem(ty, 2), "tx": tx}
+    beside = {"ty": ty, "tx": 2 * z + 1 - y}
+    on_ty, on_tx = Ring(tys, ty_s, ty_r), Ring(txs, tx_s, tx_r)
+    on_mate = Ring([mate], mate_s, mate_r)
+    handing, passing = Ring(tys, xg_s, xg_r), Ring([beside], y_s, y_r)
+    giving = Ring(tys, o_s, o_r)
+    loads = []
+    for i, w in enumerate((w0, w1, w2, w3, w4, w5, w6, w7, w8, w9)):
+        loads.append(pltpu.make_async_copy(w, ws.at[i], w_sem.at[i]))
+        loads[i].start()
+    cross, up, down, tq, tk, tv, tproj, fup, fdown = range(1, 10)
+    greet(tys + txs)
+    ty_at = lambda d: lax.rem(ty + d + 1, 4)
+    tx_at = lambda d: lax.rem(tx + d + 1, 8)
+
+    def times(rows, i):
+        return dot_nn(rows, ws[i])
+
+    def times_back(rows, i):
+        return dot_nt(rows, ws[i])
+
+    def to_ty(i, src, into):
+        return on_ty.start(i, lambda d: src, lambda d: into)
+
+    def spread(i, out, into):
+        copies = on_tx.start(i, lambda d: out.at[tx_at(d)], lambda d: into.at[tx])
+        into[tx] = out[tx]
+        return copies
+
+    def over_ty(i, out, into):
+        copies = on_ty.start(i, lambda d: out.at[ty_at(d)], lambda d: into.at[ty])
+        into[ty] = out[ty]
+        return copies
+
+    xg = {}
+
+    def give_x(i, rows):
+        for c in range(8):
+            x_out[i, c % 2, c // 2] = rows[:, 128 * c : 128 * c + 128]
+        x_all[i, :, 0, ty] = x_out[i, y]
+        x_pass[i, :, ty] = x_out[i, 1 - y]
+        xg["x", i] = handing.start(
+            i, lambda d: x_out.at[i, y], lambda d: x_all.at[i, :, 0, ty]
+        ) + handing.start(14 + i, lambda d: x_out.at[i, 1 - y], lambda d: x_pass.at[i, :, ty])
+
+    def give_g(w, rows):
+        for h in range(4):
+            g_out[w, h] = rows[:, 256 * h : 256 * h + 256]
+        g_all[w, 0, ty] = g_out[w, ty]
+        xg["g", w] = handing.start(6 + w, lambda d: g_out.at[w, ty_at(d)], lambda d: g_all.at[w, 0, ty])
+
+    def pass_x(i):
+        finish(xg.pop(("x", i)))
+        xg["px", i] = passing.start(i, lambda d: x_pass.at[i], lambda d: x_all.at[i, :, 1])
+
+    def pass_g(w):
+        finish(xg.pop(("g", w)))
+        xg["pg", w] = passing.start(6 + w, lambda d: g_all.at[w, 0], lambda d: g_all.at[w, 1])
+
+    def slot_x(w):
+        return min(w, 3) + max(w - 5, 0) if isinstance(w, int) else jnp.minimum(w, 3) + jnp.maximum(w - 5, 0)
+
+    def zcopy(w, c):
+        return pltpu.make_async_remote_copy(
+            src_ref=zsend.at[w, c], dst_ref=zrecv.at[w, c], send_sem=z_s.at[w, c],
+            recv_sem=z_r.at[w, c], device_id={"ty": ty, "tx": 2 * lax.rem(z + c + 1, 4) + y},
+            device_id_type=MESH,
+        )
+
+    def stage_one(w):
+        i = slot_x(w)
+        if isinstance(w, int):
+            finish(xg.pop(("px", i), ()), xg.pop(("pg", w)))
+        else:
+            finish([passing.copy(6 + w, 0, g_all.at[w, 0], g_all.at[w, 1])])
+        right = g_all[w].reshape(256, 256)
+        for c in range(4):
+            at = lax.rem(z + c + 1, 4)
+            total = outer(x_all[i, at].reshape(256, 128), right)
+            if c == 3:
+                own[w] = total
+            else:
+                zsend[w, c] = total.astype(BFLOAT)
+                zcopy(w, c).start()
+
+    def out_copies(w):
+        return [giving.copy(w, d, last.at[w], sums_ref.at[w, ty]) for d in range(3)] + [
+            pltpu.make_async_copy(last.at[w], sums_ref.at[w, ty], l_sem.at[w])
+        ]
+
+    def stage_three(w):
+        total = own[w]
+        for c in range(3):
+            zcopy(w, c).wait()
+            total = total + zrecv[w, c].astype(FLOAT)
+        last[w] = total.astype(BFLOAT)
+        for copy in out_copies(w):
+            copy.start()
+
+    def product_start(i, left, right, gains):
+        product = outer(left, right)
+        nsend[i] = product[0:256].astype(BFLOAT).reshape(8, 32, 256)
+        row = lax.broadcasted_iota(jnp.int32, (16, 256), 0)
+        more = product[256:272] + jnp.where(row < 8, 0.0, jnp.concatenate([gains, gains], axis=0))
+        nextra[i] = more.astype(BFLOAT)
+        return on_tx.start(
+            6 + 3 * i, lambda d: nsend.at[i, tx_at(d)], lambda d: nrecv.at[i, d]
+        ) + on_tx.start(7 + 3 * i, lambda d: nextra.at[i], lambda d: nmore.at[i, d])
+
+    def product_join(i, copies, into):
+        finish(copies)
+        main = nsend[i, tx].astype(FLOAT)
+        more = nextra[i].astype(FLOAT)
+        for d in range(7):
+            main = main + nrecv[i, d].astype(FLOAT)
+            more = more + nmore[i, d].astype(FLOAT)
+        mine = pl.ds(pl.multiple_of(tx * 32, 32), 32)
+        into[ty, mine] = main.astype(BFLOAT)
+        into[ty, 256:272] = more.astype(BFLOAT)
+        return on_tx.start(8 + 3 * i, lambda d: into.at[ty, mine], lambda d: into.at[ty, mine])
+
+    def product_end(i, copies, into):
+        finish(copies)
+        return to_ty(7 + i, into.at[ty], into.at[ty])
+
+    def message(d):
+        return on_tx.copy(0, d, msg_ref, msgs.at[tx])
+
+    for d in range(7):
+        message(d).start()
+    msgs[tx] = msg_ref[...]
+    pixels[0:GROUP] = hot_ref[...]
+    pixels[GROUP : 2 * GROUP] = hot_ref[...]
+    gains_out[...] = jnp.zeros_like(gains_out)
+    share = lat_ref.shape[1]
+    count, width = 2 * share, lat_ref.shape[2]
+    cot = cot_ref[ty]
+    give_g(0, cot)
+    fgain = fgain_ref[...]
+    unit, _ = norm_rows(lat_ref[...].reshape(4 * share, width).astype(FLOAT))
+    rows = (unit * qgain_ref[...]).astype(BFLOAT)
+    qrows[...] = rows
+    finish(loads[:1])
+    queries = times(rows, 0).astype(BFLOAT)
+    cross_scale = 1.0 / math.sqrt(width)
+    raw = dot_nt(queries, kproj_ref[...]) * cross_scale
+    raw_all[...] = raw.reshape(raw_all.shape)
+    coefs_by_pixel(raw * (fgain * LOG2E), thigh_ref, tlow_ref, pixcoefs)
+
+    def take_block(t):
+        block = msgs[t]
+        pixels[0:16] = block
+        pixels[GROUP : GROUP + 16] = block
+        scores[...] = dot_nn(pixcoefs[t], pixels[...])
+        return block
+
+    def front_step(d, _):
+        @pl.when(d > 0)
+        def _():
+            pltpu.make_async_remote_copy(
+                src_ref=msg_ref, dst_ref=msgs.at[tx], send_sem=tx_s.at[0, d - 1],
+                recv_sem=tx_r.at[0, d - 1], device_id=beside, device_id_type=MESH,
+            ).wait()
+
+        t = lax.rem(tx + 8 - d, 8)
+        block = take_block(t)
+        for group in range(4):
+            at = pl.ds(group * count, count)
+            rate, bias = rate_and_bias(block, group)
+            s = scores[at] * rate + bias
+            top = jnp.max(s, axis=1, keepdims=True)
+            e = jnp.exp2(s - top)
+            tops[t, at] = top
+            totals[t, at] = jnp.sum(e, axis=1, keepdims=True)
+            weights[at] = (e * rate).astype(BFLOAT)
+        sums[t] = dot_nt(weights[...], pixels[0:GROUP])
+        return 0
+
+    lax.fori_loop(0, 8, front_step, 0)
+    top = tops[0]
+    for t in range(1, 8):
+        top = jnp.maximum(top, tops[t])
+    top = jnp.maximum(top[: 2 * count], top[2 * count :])
+    both = jnp.concatenate([top, top], axis=0)
+    scales = [jnp.exp2(tops[t] - both) for t in range(8)]
+    total = sum(totals[t] * scales[t] for t in range(8))
+    total = total[: 2 * count] + total[2 * count :]
+    feats = features_of(sums, scales, thigh_ref, tlow_ref)
+    lane = lax.broadcasted_iota(jnp.int32, feats.shape, 1)
+    part_out[...] = jnp.where(
+        lane < FEAT, feats, jnp.where(lane == FEAT, total, top)
+    ).reshape(part_out.shape)
+
+    copies = on_ty.start(0, lambda d: part_out.at[ty_at(d)], lambda d: part_in.at[d])
+    latent = lat_ref[ty].astype(FLOAT)
+    parts = [part_out[ty]]
+    finish(copies)
+    parts += [part_in[d] for d in range(3)]
+    tops_in = [p[:, FEAT + 1 : FEAT + 2] for p in parts]
+    top = jnp.maximum(
+        jnp.maximum(tops_in[0], tops_in[1]), jnp.maximum(tops_in[2], tops_in[3])
+    )
+    joined = sum(p * jnp.exp2(t - top) for p, t in zip(parts, tops_in))
+    total = joined[:, FEAT : FEAT + 1]
+    raw_mix = joined / total
+    shift = top + jnp.log2(total)
+    mix = (raw_mix * fgain).astype(BFLOAT)
+    mix_all[ty] = mix
+    later = to_ty(1, mix_all.at[ty], mix_all.at[ty])
+    attended = dot_nn(mix, vproj_ref[...])
+    finish(loads[1:])
+    one = latent + times(attended.astype(BFLOAT), cross)
+    h_unit, h_rate = norm_rows(one)
+    hidden = (h_unit * hgain_ref[...]).astype(BFLOAT)
+    act, act_slope = gelu_pair(times(hidden, up))
+    act = act.astype(BFLOAT)
+    two = one + times(act, down)
+    t_unit, t_rate = norm_rows(two)
+    trows = (t_unit * tgain_ref[...]).astype(BFLOAT)
+    for s, i in enumerate((tk, tv)):
+        value = times(trows, i).astype(BFLOAT)
+        for h in range(8):
+            kv_out[h, 32 * s : 32 * s + 32] = value[:, 128 * h : 128 * h + 128]
+    kv_copies = spread(1, kv_out, kv_in)
+    value = times(trows, tq).astype(BFLOAT)
+    for h in range(8):
+        q_out[h] = value[:, 128 * h : 128 * h + 128]
+    q_copies = spread(2, q_out, q_in)
+    give_x(5, hidden)
+    give_x(4, act)
+    give_x(3, trows)
+    back_four = times_back(cot, fdown)
+    finish(kv_copies)
+    copies = on_mate.start(0, lambda d: kv_in, lambda d: kv_more)
+    finish(q_copies)
+    q = q_in[...].reshape(8 * share, 128)
+    k1 = kv_in[:, 0:32].reshape(8 * share, 128)
+    v1 = kv_in[:, 32:64].reshape(8 * share, 128)
+    scale = 1.0 / math.sqrt(128)
+    s1 = dot_nt(q, k1) * scale
+    finish(copies)
+    k2 = kv_more[:, 0:32].reshape(8 * share, 128)
+    v2 = kv_more[:, 32:64].reshape(8 * share, 128)
+    s2 = dot_nt(q, k2) * scale
+    stop = jnp.maximum(jnp.max(s1, axis=1, keepdims=True), jnp.max(s2, axis=1, keepdims=True))
+    e1, e2 = jnp.exp(s1 - stop), jnp.exp(s2 - stop)
+    rate = 1.0 / (jnp.sum(e1, axis=1, keepdims=True) + jnp.sum(e2, axis=1, keepdims=True))
+    p1, p2 = e1 * rate, e2 * rate
+    probs[0] = p1
+    probs[1] = p2
+    mixed_out[...] = (
+        (dot_nn(p1.astype(BFLOAT), v1) + dot_nn(p2.astype(BFLOAT), v2))
+        .astype(BFLOAT)
+        .reshape(8, share, 128)
+    )
+    copies = spread(3, mixed_out, mixed_in)
+    pass_g(0)
+    pass_x(5)
+    pass_x(4)
+    pass_x(3)
+    finish(copies)
+    mixed = jnp.concatenate([mixed_in[h] for h in range(8)], axis=1)
+    give_x(2, mixed)
+    three = two + times(mixed, tproj)
+    o_unit, o_rate = norm_rows(three)
+    ogain = ogain_ref[...]
+    frows = (o_unit * ogain).astype(BFLOAT)
+    give_x(1, frows)
+    fact, fact_slope = gelu_pair(times(frows, fup))
+    fact = fact.astype(BFLOAT)
+    give_x(0, fact)
+
+    def put_gain(row, grad):
+        for h in range(4):
+            gains_out[0, h, row : row + 1] = grad[:, 256 * h : 256 * h + 256]
+
+    g_lift = (back_four * fact_slope).astype(BFLOAT)
+    give_g(1, g_lift)
+    g_three, o_grad = norm_rows_back(times_back(g_lift, fup), ogain, o_unit, o_rate)
+    put_gain(2, o_grad)
+    g_three = cot.astype(FLOAT) + g_three
+    g_tower = g_three.astype(BFLOAT)
+    g_mixed = times_back(g_tower, tproj).astype(BFLOAT)
+    for h in range(8):
+        gm_out[h] = g_mixed[:, 128 * h : 128 * h + 128]
+    copies = spread(4, gm_out, gm_in)
+    give_g(2, g_tower)
+    result_ref[ty] = (three + times(fact, fdown)).astype(BFLOAT)
+    later += to_ty(2, result_ref.at[ty], result_ref.at[ty])
+    pass_x(2)
+    pass_x(1)
+    pass_x(0)
+    pass_g(1)
+    finish(copies)
+    gm = gm_in[...].reshape(8 * share, 128)
+    q = q_in[...].reshape(8 * share, 128)
+    k1 = kv_in[:, 0:32].reshape(8 * share, 128)
+    v1 = kv_in[:, 32:64].reshape(8 * share, 128)
+    k2 = kv_more[:, 0:32].reshape(8 * share, 128)
+    v2 = kv_more[:, 32:64].reshape(8 * share, 128)
+    p1, p2 = probs[0], probs[1]
+    gp1, gp2 = dot_nt(gm, v1), dot_nt(gm, v2)
+    away = jnp.sum(p1 * gp1, axis=1, keepdims=True) + jnp.sum(p2 * gp2, axis=1, keepdims=True)
+    gs1 = (p1 * (gp1 - away)).astype(BFLOAT)
+    gs2 = (p2 * (gp2 - away)).astype(BFLOAT)
+    kvx_out[0] = (outer(gs2, q) * scale).astype(BFLOAT)
+    kvx_out[1] = outer(p2.astype(BFLOAT), gm).astype(BFLOAT)
+    copies = on_mate.start(1, lambda d: kvx_out, lambda d: kvx_in)
+    gq = (dot_nn(gs1, k1) + dot_nn(gs2, k2)) * scale
+    q_out[...] = gq.astype(BFLOAT).reshape(8, share, 128)
+    q_copies = spread(5, q_out, gq_in)
+    gk = outer(gs1, q) * scale
+    gv = outer(p1.astype(BFLOAT), gm)
+    finish(copies)
+    kv_out[:, 0:32] = (gk + kvx_in[0].astype(FLOAT)).astype(BFLOAT).reshape(8, share, 128)
+    kv_out[:, 32:64] = (gv + kvx_in[1].astype(FLOAT)).astype(BFLOAT).reshape(8, share, 128)
+    kv_copies = spread(12, kv_out, gkv_in)
+    pass_g(2)
+    stage_one(0)
+    finish(q_copies)
+    value = jnp.concatenate([gq_in[h] for h in range(8)], axis=1)
+    give_g(3, value)
+    g_trows = times_back(value, tq)
+    finish(kv_copies)
+    for s, i in enumerate((tk, tv)):
+        value = jnp.concatenate([gkv_in[h, 32 * s : 32 * s + 32] for h in range(8)], axis=1)
+        give_g(4 + s, value)
+        g_trows = g_trows + times_back(value, i)
+    g_two, t_grad = norm_rows_back(g_trows, tgain_ref[...], t_unit, t_rate)
+    put_gain(1, t_grad)
+    g_two = g_three + g_two
+    g_hidden = g_two.astype(BFLOAT)
+    give_g(6, g_hidden)
+    pass_g(3)
+    stage_one(1)
+    g_hlift = (times_back(g_hidden, down) * act_slope).astype(BFLOAT)
+    give_g(7, g_hlift)
+    pass_g(4)
+    pass_g(5)
+    stage_one(2)
+    g_one, h_grad = norm_rows_back(times_back(g_hlift, up), hgain_ref[...], h_unit, h_rate)
+    put_gain(0, h_grad)
+    gain_copies = over_ty(3, gains_out.at[0], gains_all.at[0])
+    g_one = g_two + g_one
+    g_cross = g_one.astype(BFLOAT)
+    for h in range(4):
+        gcross_out[h] = g_cross[:, 256 * h : 256 * h + 256]
+    gcross_copies = over_ty(4, gcross_out, gcross_all)
+    g_att = times_back(g_cross, cross).astype(BFLOAT)
+    raw_up = dot_nt(g_att, vproj_ref[...])
+    feat_part = jnp.sum(raw_mix * raw_up, axis=0, keepdims=True)
+    delta = jnp.sum(g_att.astype(FLOAT) * attended, axis=1, keepdims=True)
+    lane = lax.broadcasted_iota(jnp.int32, raw_up.shape, 1)
+    up_ref[ty] = jnp.where(
+        lane < FEAT, raw_up * fgain, jnp.where(lane == FEAT, delta, shift)
+    )
+    copies = to_ty(5, up_ref.at[ty], up_ref.at[ty])
+    pass_g(6)
+    stage_one(3)
+    finish(later, gain_copies, gcross_copies)
+    gain_rows = gains_all[0, 0] + gains_all[0, 1] + gains_all[0, 2] + gains_all[0, 3]
+    ncopies = product_start(
+        0, mix_all[...].reshape(4 * share, LANES), gcross_all[...].reshape(4 * share, 256), gain_rows
+    )
+    finish(copies)
+    pass_g(7)
+    for i in (3, 4, 5):
+        finish(xg.pop(("px", i), ()))
+
+    coefs_by_pixel(up_ref[...].reshape(4 * share, LANES), thigh_ref, tlow_ref, upcoefs)
+
+    def back_step(t):
+        block = take_block(t)
+        ups[...] = dot_nn(upcoefs[t], pixels[...])
+        for group in range(4):
+            at = pl.ds(group * count, count)
+            rate, bias = rate_and_bias(block, group)
+            b = group % 2
+            mine = up_ref[2 * b : 2 * b + 2].reshape(count, LANES)
+            p = jnp.exp2(scores[at] * rate + (bias - mine[:, FEAT + 1 : FEAT + 2]))
+            g = p * (ups[at] * rate - mine[:, FEAT : FEAT + 1])
+            weights[at] = (g * rate).astype(BFLOAT)
+        sums[t] = dot_nt(weights[...], pixels[0:GROUP])
+
+    def first_steps(t, _):
+        back_step(t)
+        stage_one(4 + t)
+        return 0
+
+    def second_steps(t, _):
+        back_step(t)
+        stage_three(t - 4)
+        return 0
+
+    lax.fori_loop(0, 3, first_steps, 0)
+    ncopies = product_join(0, ncopies, value_ref)
+    lax.fori_loop(3, 4, first_steps, 0)
+    lax.fori_loop(4, 8, second_steps, 0)
+    part_out[...] = features_of(sums, None, thigh_ref, tlow_ref).reshape(part_out.shape)
+    copies = on_ty.start(9, lambda d: part_out.at[ty_at(d)], lambda d: part_in.at[d])
+    ncopies = product_end(0, ncopies, value_ref)
+    unit, rate = norm_rows(lat_ref[ty].astype(FLOAT))
+    raw_mix = part_out[ty]
+    finish(copies)
+    for d in range(3):
+        raw_mix = raw_mix + part_in[d]
+    mix = (raw_mix * fgain).astype(BFLOAT)
+    gmix[ty] = mix
+    mcopies = to_ty(6, gmix.at[ty], gmix.at[ty])
+    grad_q = (dot_nn(mix, kproj_ref[...]) * cross_scale).astype(BFLOAT)
+    grad, qgain_grad = norm_rows_back(times_back(grad_q, 0), qgain_ref[...], unit, rate)
+    features = feat_part + jnp.sum(raw_mix * raw_all[ty], axis=0, keepdims=True)
+    for h in range(4):
+        gains_out[1, h, 0:1] = qgain_grad[:, 256 * h : 256 * h + 256]
+    gains_out[1, 0, 1:2] = features[:, 0:256]
+    gains_out[1, 1, 1:2, 0:128] = features[:, 256:384]
+    mcopies += over_ty(10, gains_out.at[1], gains_all.at[1])
+    grad_ref[ty] = (g_one + grad).astype(BFLOAT)
+    ncopies += to_ty(11, grad_ref.at[ty], grad_ref.at[ty])
+    finish(mcopies)
+    gain_rows = gains_all[1, 0] + gains_all[1, 1] + gains_all[1, 2] + gains_all[1, 3]
+    right = qrows[:, pl.ds(pl.multiple_of(ty * 256, 256), 256)]
+    mcopies = product_start(1, gmix[...].reshape(4 * share, LANES), right, gain_rows)
+    stage_three(4)
+    stage_three(5)
+    mcopies = product_join(1, mcopies, key_ref)
+    stage_three(6)
+    ncopies += product_end(1, mcopies, key_ref)
+    stage_three(7)
+    finish(ncopies)
+    for w in range(8):
+        finish(out_copies(w))
+
+
+def main_call(msg, lat, cot, gains, key_rows, value_rows, thigh, tlow, hot, matrices):
+    _, share, width = lat.shape
+    rows, length = 8 * share, msg.shape[1]
+    dma = pltpu.SemaphoreType.DMA
+    vmem = pl.BlockSpec(memory_space=pltpu.VMEM)
+    hbm = pl.BlockSpec(memory_space=pl.ANY)
+    shape = jax.ShapeDtypeStruct
+    half, full = (lambda *s: pltpu.VMEM(s, BFLOAT)), (lambda *s: pltpu.VMEM(s, FLOAT))
+    return pl.pallas_call(
+        main_kernel,
+        out_shape=(
+            shape((4, share, width), BFLOAT),
+            shape((4, share, width), BFLOAT),
+            shape((4, 272, 256), BFLOAT),
+            shape((4, 272, 256), BFLOAT),
+            shape((8, 4, 128, 256), BFLOAT),
+        ),
+        in_specs=[vmem] * 13 + [hbm] * 10,
+        out_specs=(vmem, vmem, vmem, vmem, hbm),
+        scratch_shapes=[
+            half(10, width, width), half(8, 16, length), half(8, rows, 2 * GROUP), half(8, rows, 2 * GROUP),
+            half(2 * GROUP, length), full(rows, length), full(rows, length), half(rows, length),
+            full(8, rows, GROUP), full(8, rows, 1), full(8, rows, 1), full(4, share, LANES), half(4 * share, width),
+            full(4, share, LANES), full(3, share, LANES),
+            half(8, share, 128), half(8, share, 128), half(8, 2 * share, 128), half(8, 2 * share, 128),
+            half(8, 2 * share, 128), full(2, rows, rows), half(8, share, 128), half(8, share, 128),
+            half(8, share, 128), half(8, share, 128), half(2, rows, 128), half(2, rows, 128),
+            half(8, share, 128), half(8, 2 * share, 128),
+            full(4, share, LANES), half(4, share, LANES), half(4, share, 256), half(4, share, 256),
+            full(2, 4, 8, 256), full(2, 4, 8, 256), half(4, share, LANES),
+            half(6, 2, 4, share, 128), half(6, 4, 4, share, 128), half(6, 4, 2, 4, share, 128),
+            half(8, 4, share, 256), half(8, 2, 4, share, 256), full(8, 128, 256),
+            half(8, 3, 128, 256), half(8, 3, 128, 256), half(8, 128, 256),
+            half(2, 8, 32, 256), half(2, 16, 256), half(2, 7, 32, 256), half(2, 7, 16, 256),
+            dma((10,)), dma((8,)), dma((12, 3)), dma((12, 3)), dma((13, 7)), dma((13, 7)),
+            dma((2, 1)), dma((2, 1)), dma((20, 3)), dma((20, 3)), dma((14, 1)), dma((14, 1)),
+            dma((8, 3)), dma((8, 3)), dma((8, 3)), dma((8, 3)),
+        ],
+        compiler_params=pltpu.CompilerParams(
+            collective_id=1, has_side_effects=True, vmem_limit_bytes=60 << 20
+        ),
+        name="main",
+    )(msg, lat, cot, *gains, key_rows, value_rows, thigh, tlow, hot, *matrices)
+
+
+def finish_kernel(
+    sums_ref, cross_core_ref, query_core_ref, latent_ref, result_in_ref, cross_ref, query_ref, value_ref, key_ref,
+    *outs,
+):
+    tx = lax.axis_index("tx")
+    result_ref, latent_out, feat_out, qgain_out, query_out, key_out, value_out, cross_out = outs[:8]
+    for w, out in enumerate(outs[8:16]):
+        for h in range(4):
+            out[:, 256 * h : 256 * h + 256] = sums_ref[w, h].astype(FLOAT)
+    result_ref[...] = result_in_ref[...]
+    latent_out[...] = latent_ref[...].astype(FLOAT)
+    here = pl.ds(pl.multiple_of(tx * 128, 128), 128)
+    quarter = tx // 2
+    inside = pl.ds(pl.multiple_of(lax.rem(tx, 2) * 128, 128), 128)
+    scale = 1.0 / math.sqrt(query_ref.shape[0])
+    cross_core = jnp.concatenate([cross_core_ref[h] for h in range(4)], axis=1)
+    query_core = jnp.concatenate([query_core_ref[h] for h in range(4)], axis=1)
+    value_out[...] = dot_nt(cross_core, cross_ref[...])[:FEAT]
+    key_out[...] = (dot_nn(query_core, query_ref[...]) * scale)[:FEAT]
+    row = lax.broadcasted_iota(jnp.int32, (272, 1024), 0)
+    core = jnp.where(row < FEAT, cross_core.astype(FLOAT), 0.0).astype(BFLOAT)
+    cross_out[...] = outer(value_ref[0:272, here], core)
+    row = lax.broadcasted_iota(jnp.int32, (272, 128), 0)
+    mine = query_core_ref[quarter, :, inside].astype(FLOAT)
+    core = jnp.where(row < FEAT, mine, 0.0).astype(BFLOAT)
+    query_out[...] = outer(core, key_ref[0:272]) * scale
+    qgain_out[...] = mine[264:265]
+    more = jnp.concatenate([query_core_ref[h, 256:272] for h in range(2)], axis=1).astype(FLOAT)
+    feat_out[...] = more[9:10, 0:FEAT]
+    mine = cross_core_ref[quarter, 256:272, inside].astype(FLOAT)
+    for i, out in enumerate(outs[16:19]):
+        out[...] = mine[8 + i : 9 + i]
+
+
+def finish_call(sums, cross_core, query_core, latent_grad, result, cross_proj, query_proj, value_rows, key_rows):
+    width = cross_proj.shape[0]
+    shape = lambda *s: jax.ShapeDtypeStruct(s, FLOAT)
+    rows = latent_grad.shape
+    block = [shape(128, width)]
+    vmem = pl.BlockSpec(memory_space=pltpu.VMEM)
+    return pl.pallas_call(
+        finish_kernel,
+        out_shape=(
+            [jax.ShapeDtypeStruct(rows, BFLOAT), shape(*rows), shape(1, FEAT), shape(1, 128)]
+            + block + [shape(FEAT, width)] * 2 + block + block * 8 + [shape(1, 128)] * 3
+        ),
+        in_specs=[vmem] * 9,
+        out_specs=[vmem] * 19,
+        compiler_params=pltpu.CompilerParams(vmem_limit_bytes=48 << 20),
+        name="finish",
+    )(sums, cross_core, query_core, latent_grad, result, cross_proj, query_proj, value_rows, key_rows)
+
+
+def pixel_tables(image_sizes, row_ids, tile_width):
+    high = len(row_ids) // HALVES
+    all_cols = jnp.arange(8 * tile_width, dtype=jnp.int32)
+    row_table, row_coord, row_sum = axis_tables(image_sizes, row_ids, 3, 5)
+    col_table, col_coord, col_sum = axis_tables(image_sizes, all_cols, 4, 5 + 2 * BANDS)
+    row_table = row_table - row_sum[:, :, None] * (1.0 / FEAT)
+    col_table = col_table - col_sum[:, :, None] * (1.0 / FEAT)
+    row_table = row_table.reshape(2, HALVES, high, FEAT)
+    col_table = col_table.reshape(2, 8, tile_width, FEAT)
+    colours = np.zeros((2, HALVES, 16, FEAT), np.float32)
+    for b in range(2):
+        for half in range(HALVES):
+            for c in range(3):
+                colours[b, half, half * 8 + b * 4 + c] = -1.0 / FEAT
+                colours[b, half, half * 8 + b * 4 + c, c] += 1.0
+    first = jnp.concatenate(
+        [jnp.asarray(colours), row_table, jnp.zeros((2, HALVES, GROUP - 16 - high, FEAT), FLOAT)], axis=2
+    )
+    col_from = 16 + -(-high // 8) * 8
+    second = jnp.pad(col_table, ((0, 0), (0, 0), (col_from, GROUP - col_from - tile_width), (0, 0)))
+    table = jnp.concatenate([first, second], axis=1).reshape(2, 10 * GROUP, FEAT)
+    table = jnp.pad(table, ((0, 0), (0, 0), (0, LANES - FEAT)))
+    hot = np.zeros((GROUP, -(-high * tile_width // 128) * 128), np.float32)
+    for i in range(high):
+        for j in range(tile_width):
+            hot[16 + i, i * tile_width + j] = 1.0
+            hot[col_from + j, i * tile_width + j] = 1.0
+    here = lax.dynamic_slice_in_dim
+    at = lax.axis_index("tx") * tile_width
+    return (
+        split_two(table), jnp.asarray(hot, BFLOAT),
+        (row_coord, row_sum), (here(col_coord, at, tile_width, 1), here(col_sum, at, tile_width, 1)),
+    )
+
+
+def pixel_message(pixels, live, rows, cols, length):
+    (row_coord, row_sum), (col_coord, col_sum) = rows, cols
+    _, _, height, width = pixels.shape
+    wide = pixels.astype(FLOAT)
+    mean = (jnp.sum(wide, axis=1) + row_sum[:, :, None] + col_sum[:, None, :]) * (1.0 / FEAT)
+    square = (
+        jnp.sum(wide * wide, axis=1)
+        + (row_coord * row_coord)[:, :, None]
+        + (col_coord * col_coord)[:, None, :]
+        + 2.0 * BANDS
+    ) * (1.0 / FEAT)
+    rate = jnp.where(live, lax.rsqrt(square - mean * mean + EPSILON), 0.0)
+    rows = jnp.concatenate([pixels, rate.astype(BFLOAT)[:, None]], axis=1)
+    rows = rows.reshape(2, 4, HALVES, height // HALVES * width)
+    rows = jnp.transpose(rows, (2, 0, 1, 3)).reshape(16, -1)
+    return jnp.pad(rows, ((0, 0), (0, length - rows.shape[1])))
+
+
+def on_device_fast(
+    pixels,
+    pixel_mask,
+    image_sizes,
+    latents,
+    cotangent,
+    feature_gain,
+    query_gain,
+    query_proj,
+    key_proj,
+    value_proj,
+    cross_proj,
+    hidden_gain,
+    hidden_up,
+    hidden_down,
+    tower_gain,
+    tower_query,
+    tower_key,
+    tower_value,
+    tower_proj,
+    final_gain,
+    final_up,
+    final_down,
+):
     item_count = pixels.shape[0]
     tile_height = pixels.shape[2]
     tile_width = pixels.shape[3]
-    image_side = image_sizes.astype(FLOAT)[:, None]
-    ycoord = -1.0 + 2.0 * row_ids.astype(FLOAT)[None, :] / (image_side - 1.0)
-    xcoord = -1.0 + 2.0 * col_ids.astype(FLOAT)[None, :] / (image_side - 1.0)
-    band_index = jnp.arange(BANDS, dtype=jnp.int32).astype(FLOAT)
-    frequency = 1.0 + band_index[None, :] * (image_side * 0.5 - 1.0) / (BANDS - 1)
-    yangle = math.pi * ycoord[:, :, None] * frequency[:, None, :]
-    xangle = math.pi * xcoord[:, :, None] * frequency[:, None, :]
-    tile_shape = (item_count, tile_height, tile_width)
-    pieces = [
-        jnp.transpose(pixels, (0, 2, 3, 1)).astype(FLOAT),
-        jnp.broadcast_to(ycoord[:, :, None, None], tile_shape + (1,)),
-        jnp.broadcast_to(xcoord[:, None, :, None], tile_shape + (1,)),
-        jnp.broadcast_to(jnp.sin(yangle)[:, :, None, :], tile_shape + (BANDS,)),
-        jnp.broadcast_to(jnp.cos(yangle)[:, :, None, :], tile_shape + (BANDS,)),
-        jnp.broadcast_to(jnp.sin(xangle)[:, None, :, :], tile_shape + (BANDS,)),
-        jnp.broadcast_to(jnp.cos(xangle)[:, None, :, :], tile_shape + (BANDS,)),
-    ]
-    return jnp.concatenate(pieces, axis=3).reshape(item_count, tile_height * tile_width, FEAT)
+    model_width = latents.shape[2]
+    rows_here = latents.shape[1]
+    cross_scale = 1.0 / math.sqrt(model_width)
+    row_ids = lax.axis_index("ty") * tile_height + jnp.arange(tile_height, dtype=jnp.int32)
+    col_ids = lax.axis_index("tx") * tile_width + jnp.arange(tile_width, dtype=jnp.int32)
+    side_sizes = image_sizes[:, None, None]
+    live = (
+        (pixel_mask > 0)
+        & (row_ids[None, :, None] < side_sizes)
+        & (col_ids[None, None, :] < side_sizes)
+    )
+    (thigh, tlow), hot, rows, cols = pixel_tables(image_sizes, row_ids, tile_width)
+    message = pixel_message(pixels, live, rows, cols, hot.shape[1])
+    share = item_count * rows_here // 4
+
+    def in_shares(rows):
+        return rows.reshape(4, share, rows.shape[-1])
+
+    gain_lanes = jnp.pad(feature_gain, (0, LANES - FEAT))[None]
+    value_rows = jnp.pad(value_proj, ((0, LANES - FEAT), (0, 0)))
+    key_rows = jnp.pad(key_proj, ((0, LANES - FEAT), (0, 0)))
+    result, latent_grad, cross_core, query_core, sums = main_call(
+        message, in_shares(latents), in_shares(cotangent),
+        (gain_lanes, query_gain[None], hidden_gain[None], tower_gain[None], final_gain[None]),
+        key_rows, value_rows, thigh, tlow, hot,
+        (query_proj, cross_proj, hidden_up, hidden_down, tower_query, tower_key, tower_value,
+         tower_proj, final_up, final_down),
+    )
+    (result, latent_grad, feature_sum, query_sum, query_grad, key_grad, value_grad, cross_grad,
+     final_down_grad, final_up_grad, tower_proj_grad, tower_query_grad, tower_key_grad,
+     tower_value_grad, hidden_down_grad, hidden_up_grad, hidden_sum, tower_sum, final_sum) = finish_call(
+        sums, cross_core, query_core, latent_grad, result, cross_proj, query_proj, value_rows, key_rows
+    )
+    return (
+        result.reshape(latents.shape),
+        latent_grad.reshape(latents.shape),
+        feature_sum[0],
+        query_sum[0],
+        query_grad,
+        key_grad,
+        value_grad,
+        cross_grad,
+        hidden_sum[0],
+        hidden_up_grad,
+        hidden_down_grad,
+        tower_sum[0],
+        tower_query_grad,
+        tower_key_grad,
+        tower_value_grad,
+        tower_proj_grad,
+        final_sum[0],
+        final_up_grad,
+        final_down_grad,
+    )
 
 
 def on_device(
@@ -106,45 +913,64 @@
     tower_scale = 1.0 / math.sqrt(head_size)
     row_ids = lax.axis_index("ty") * tile_height + jnp.arange(tile_height, dtype=jnp.int32)
     col_ids = lax.axis_index("tx") * tile_width + jnp.arange(tile_width, dtype=jnp.int32)
+    all_cols = jnp.arange(tile_width * lax.axis_size("tx"), dtype=jnp.int32)
+    wide_pixels = lax.all_gather(pixels, "tx", axis=3, tiled=True).astype(FLOAT)
+    wide_mask = lax.all_gather(pixel_mask, "tx", axis=2, tiled=True)
     side_sizes = image_sizes[:, None, None]
-    inside = (
-        (pixel_mask > 0)
+    live = (
+        (wide_mask > 0)
         & (row_ids[None, :, None] < side_sizes)
-        & (col_ids[None, None, :] < side_sizes)
-    )
-    live_mask = inside.reshape(item_count, 1, tile_height * tile_width)
-    features = pixel_features(pixels, image_sizes, row_ids, col_ids)
-
-    def feature_norm(scales):
-        return layer_norm(features, scales)
-
-    normed, back_features = jax.vjp(feature_norm, feature_gain)
-    normed_pixels = normed.astype(BFLOAT)
-    pixel_keys = linear(normed_pixels, key_proj).astype(BFLOAT)
-    pixel_values = linear(normed_pixels, value_proj).astype(BFLOAT)
+        & (all_cols[None, None, :] < side_sizes)
+    )[:, None]
+    row_table, row_coord, row_sum = axis_tables(image_sizes, row_ids, 3, 5)
+    col_table, col_coord, col_sum = axis_tables(image_sizes, all_cols, 4, 5 + 2 * BANDS)
+    pixel_mean = (
+        jnp.sum(wide_pixels, axis=1) + row_sum[:, :, None] + col_sum[:, None, :]
+    ) / FEAT
+    pixel_square = (
+        jnp.sum(wide_pixels * wide_pixels, axis=1)
+        + (row_coord * row_coord)[:, :, None]
+        + (col_coord * col_coord)[:, None, :]
+        + 2.0 * BANDS
+    ) / FEAT
+    pixel_rate = lax.rsqrt(pixel_square - pixel_mean * pixel_mean + EPSILON)
+    exact = lax.Precision.HIGHEST
+
+    def against_pixels(coefs):
+        by_row = jnp.einsum("blf,bif->bli", coefs, row_table, precision=exact)
+        by_col = jnp.einsum("blf,bjf->blj", coefs, col_table, precision=exact)
+        total = by_row[:, :, :, None] + by_col[:, :, None, :]
+        for c in range(3):
+            total = total + coefs[:, :, c][:, :, None, None] * wide_pixels[:, None, c]
+        total = total - jnp.sum(coefs, axis=2)[:, :, None, None] * pixel_mean[:, None]
+        return total * pixel_rate[:, None]
+
+    def over_pixels(weights):
+        scaled = weights * pixel_rate[:, None]
+        by_row = jnp.sum(scaled, axis=3)
+        by_col = jnp.sum(scaled, axis=2)
+        total = jnp.einsum("bli,bif->blf", by_row, row_table, precision=exact)
+        total = total + jnp.einsum("blj,bjf->blf", by_col, col_table, precision=exact)
+        colour = jnp.stack(
+            [jnp.sum(scaled * wide_pixels[:, None, c], axis=(2, 3)) for c in range(3)], axis=2
+        )
+        total = total + jnp.pad(colour, ((0, 0), (0, 0), (0, FEAT - 3)))
+        return total - jnp.sum(scaled * pixel_mean[:, None], axis=(2, 3))[:, :, None]
+
     latent_rows = latents.astype(FLOAT)
     query_normed, back_query_norm = jax.vjp(layer_norm, latent_rows, query_gain)
     query_input = query_normed.astype(BFLOAT)
     own_queries = linear(query_input, query_proj).astype(BFLOAT)
-    all_queries = lax.all_gather(own_queries, "tx", axis=1, tiled=True)
-    scores = (
-        jnp.einsum("blc,bpc->blp", all_queries, pixel_keys, preferred_element_type=FLOAT)
-        * cross_scale
-    )
-    live_scores = jnp.where(live_mask, scores, -1e30)
-    row_top = lax.pmax(jnp.max(live_scores, axis=2), ("ty", "tx"))
-    row_exp = jnp.where(
-        live_mask,
-        jnp.exp(jnp.where(live_mask, scores, row_top[:, :, None]) - row_top[:, :, None]),
-        0.0,
-    )
-    row_total = lax.psum(jnp.sum(row_exp, axis=2), ("ty", "tx"))
-    cross_exact = row_exp / row_total[:, :, None]
-    partial_attended = jnp.einsum(
-        "blp,bpc->blc", cross_exact.astype(BFLOAT), pixel_values, preferred_element_type=FLOAT
-    )
-    column_sums = lax.psum_scatter(partial_attended, "tx", scatter_dimension=1, tiled=True)
-    attended = lax.psum(column_sums, "ty")
+    raw_query = linear_back(own_queries, key_proj) * cross_scale
+    scores = against_pixels(raw_query * feature_gain)
+    row_top = jnp.max(jnp.where(live, scores, -1e30), axis=(2, 3))
+    all_top = lax.pmax(row_top, "ty")
+    row_exp = jnp.where(live, jnp.exp(scores - all_top[:, :, None, None]), 0.0)
+    row_total = lax.psum(jnp.sum(row_exp, axis=(2, 3)), "ty")
+    cross_exact = row_exp / row_total[:, :, None, None]
+    raw_mix = lax.psum(over_pixels(cross_exact), "ty")
+    mix = raw_mix * feature_gain
+    attended = linear(mix.astype(BFLOAT), value_proj)
     attended_input = attended.astype(BFLOAT)
     resid_one = latent_rows + linear(attended_input, cross_proj)
     hidden_normed, back_hidden_norm = jax.vjp(layer_norm, resid_one, hidden_gain)
@@ -239,40 +1065,17 @@
     grad_cross_out = grad_one.astype(BFLOAT)
     cross_proj_grad = weight_grad(attended_input, grad_cross_out)
     grad_attended = linear_back(grad_cross_out, cross_proj).astype(BFLOAT)
-    all_upstream = lax.all_gather(grad_attended, "tx", axis=1, tiled=True)
-    again_scores = (
-        jnp.einsum("blc,bpc->blp", all_queries, pixel_keys, preferred_element_type=FLOAT)
-        * cross_scale
-    )
-    again_exp = jnp.where(
-        live_mask,
-        jnp.exp(jnp.where(live_mask, again_scores, row_top[:, :, None]) - row_top[:, :, None]),
-        0.0,
-    )
-    again_probs = again_exp / row_total[:, :, None]
-    grad_probs = jnp.einsum(
-        "blc,bpc->blp", all_upstream, pixel_values, preferred_element_type=FLOAT
-    )
-    cross_delta = lax.psum(jnp.sum(again_probs * grad_probs, axis=2), ("ty", "tx"))
-    grad_scores = (again_probs * (grad_probs - cross_delta[:, :, None])).astype(BFLOAT)
-    query_part = (
-        jnp.einsum("blp,bpc->blc", grad_scores, pixel_keys, preferred_element_type=FLOAT)
-        * cross_scale
-    )
-    query_columns = lax.psum_scatter(query_part, "tx", scatter_dimension=1, tiled=True)
-    grad_queries = lax.psum(query_columns, "ty").astype(BFLOAT)
-    grad_keys = (
-        jnp.einsum("blp,blc->bpc", grad_scores, all_queries, preferred_element_type=FLOAT)
-        * cross_scale
-    ).astype(BFLOAT)
-    grad_values = jnp.einsum(
-        "blp,blc->bpc", again_probs.astype(BFLOAT), all_upstream, preferred_element_type=FLOAT
-    ).astype(BFLOAT)
-    key_proj_grad = weight_grad(normed_pixels, grad_keys)
-    value_proj_grad = weight_grad(normed_pixels, grad_values)
-    grad_normed = linear_back(grad_keys, key_proj) + linear_back(grad_values, value_proj)
-    feature_part = back_features(grad_normed)[0]
-    pixel_sums = lax.psum((key_proj_grad, value_proj_grad, feature_part), ("ty", "tx"))
+    raw_up = linear_back(grad_attended, value_proj)
+    grad_probs = against_pixels(raw_up * feature_gain)
+    cross_delta = jnp.sum(grad_attended.astype(FLOAT) * attended, axis=2)
+    grad_scores = cross_exact * (grad_probs - cross_delta[:, :, None, None])
+    raw_grad_mix = lax.psum(over_pixels(grad_scores), "ty")
+    grad_mix = (raw_grad_mix * feature_gain).astype(BFLOAT)
+    grad_queries = (linear(grad_mix, key_proj) * cross_scale).astype(BFLOAT)
+    key_proj_grad = weight_grad(grad_mix, own_queries) * cross_scale
+    value_proj_grad = weight_grad(mix.astype(BFLOAT), grad_attended)
+    feature_part = jnp.sum(raw_grad_mix * raw_query + raw_mix * raw_up, axis=(0, 1))
+    pixel_sums = lax.psum((key_proj_grad, value_proj_grad, feature_part), "tx")
     query_proj_grad = weight_grad(query_input, grad_queries)
     grad_latent_rows, query_gain_grad = back_query_norm(linear_back(grad_queries, query_proj))
     latent_grad = grad_one + grad_latent_rows
@@ -361,6 +1164,8 @@
         P("tx", None),
         P("tx", None),
     )
+    fits = mesh.shape["ty"] == 4 and mesh.shape["tx"] == HEADS
+    plan = on_device_fast if fits else on_device
     return jax.shard_map(
-        on_device, mesh=mesh, in_specs=in_specs, out_specs=out_specs, check_vma=False
-    )
+        plan, mesh=mesh, in_specs=in_specs, out_specs=out_specs, check_vma=False
+    )

time: 1950 us -> 183 us (0.09)
  waiting for transfers between devices: 1350 us -> 0 us
  blocking collectives: 225 us -> 0 us
  matrix products: 197 us -> 0 us
  Pallas kernels: 0 us -> 157 us
  local copies, waits for them, and re-layouts: 111 us -> 13.9 us
  other arithmetic: 42.5 us -> 10.5 us
    reduce_scatter x14 -> x0, waiting for transfers between devices: 1070 us -> none  [the longest x1 92.5 us: on_device(): lax.psum_scatter(cross_proj_grad, 'tx', scatter_dimension=0, tiled=True)]
    dot_general x48 -> x0, matrix products: 197 us -> none  [the longest x12 42.1 us: weight_grad(): lax.dot_general(flat_inputs, flat_upstream, (((0,), (0,)), ((), ())), pre...]
    pallas_call x0 -> x2, Pallas kernels: none -> 157 us  [the longest x1 151 us: main_call(): pl.pallas_call(main_kernel, out_shape=(shape((4, share, width), BFLOAT),...]
    psum x5 -> x0, blocking collectives: 155 us -> none  [the longest x1 40.8 us: on_device(): lax.psum((key_proj_grad, value_proj_grad, feature_part), ('ty', 'tx'))]
    psum x1 -> x0, waiting for transfers between devices: 140 us -> none  [on_device(): lax.psum((key_proj_grad, value_proj_grad, feature_part), ('ty', 'tx'))]
    all_gather x4 -> x0, waiting for transfers between devices: 136 us -> none  [the longest x1 48 us: on_device(): all_upstream = lax.all_gather(grad_attended, 'tx', axis=1, tiled=True)]
    pmax x1 -> x0, blocking collectives: 40.5 us -> none  [on_device(): row_top = lax.pmax(jnp.max(live_scores, axis=2), ('ty', 'tx'))]
    concatenate x1 -> x5, local copies, waits for them, and re-layouts: 40.5 us -> 1.34 us  [the longest x2 0.95 us: axis_tables(): table = jnp.concatenate([lead, coord[:, :, None], gap, waves, tail], axis=2)]
  transfers between devices with their start and end apart: 19 -> 0, of which waited for: 17 -> 0; matrix products, arithmetic and copies ran while one was open for 12% -> 0% of each run, Pallas kernels for 0% -> 0%
where the time goes in v4:
time: 183 us
  Pallas kernels  157 us (86%)
  local copies, waits for them, and re-layouts  13.9 us (8%)
  other arithmetic  10.5 us (6%)
    pallas_call x1, Pallas kernels, main_call(): pl.pallas_call(main_kernel, out_shape=(shape((4, share, width), BFLOAT),...  151 us
    pallas_call x1, Pallas kernels, finish_call(): pl.pallas_call(finish_kernel, out_shape=[jax.ShapeDtypeStruct(rows, BFLOA...  6.71 us
    unnamed x21, local copies, waits for them, and re-layouts  6.66 us

profile of v4, /device:TPU:1, one launch (start us, length us, event | category | flops | bytes accessed | tf_op | source)
XLA Modules:
  0.0 182.8 jit_solution(17918334034713805776)
XLA Ops:
  0.7 0.7 broadcast_compare_fusion.1
  1.4 0.7 convert_add_fusion
  2.2 0.7 pad.24
  2.9 0.6 broadcast_in_dim.26.fgain_ref
  3.5 0.3 fusion.4
  4.2 0.7 broadcast_compare_fusion
  4.9 0.8 fusion.1
  6.2 1.0 fusion.2
  7.2 1.0 fusion.5
  8.2 0.1 copy.54
  8.3 0.1 concatenate.27
  8.5 1.0 copy.51
  9.5 0.2 concatenate.26
  9.8 0.6 pad.23.msg_ref
  10.4 0.4 multiply_cosine_fusion.2
  10.8 0.2 concatenate.29
  11.3 1.2 multiply_cosine_fusion
  12.6 0.8 concatenate.31
  13.3 0.2 broadcast_subtract_fusion
  13.6 1.0 pad.25.kproj_ref.key_ref
  14.6 1.0 pad.26.vproj_ref.value_ref
  15.5 0.3 select_maximum_fusion
  15.9 1.7 subtract_convert_fusion.tlow_ref
  17.6 1.5 pad_convert_fusion.thigh_ref
  19.1 150.8 %main.1 = (bf16[4,32,1024]{2,1,0:T(8,128)(2,1)}, bf16[4,32,1024]{2,1,0:T(8,128)(2,1)}, bf16[4,272,256]{2,1,0:T(8,128)(2,1)}, bf16[4,272,256]{2,1,0:T(8,128)(2,1)}, bf16[8,4,128,256]{3,2,1,0:T(8,128)(2,1)}) custom-call(bf16[16,1408]{1,0:T(8,128)(2,1)} %pad.23.msg_ref, bf16[4,32,1024]{2,1,0:T(8,128)(2,1)} %bitcast.20, bf16[4,32,1024]{2,1,0:T(8,128)(2,1)} %bitcast.21, ...), custom_call_target="tpu_custom_call" | custom-call | tf_op jit(solution)/shard_map/main/pallas_call | solution.py:655
  169.9 1.6 copy-done.2
  171.5 1.1 copy-done.3
  172.5 1.1 copy-done.4
  173.6 0.9 copy-done.5
  174.5 0.9 copy-done.6
  175.5 6.7 %finish.1 = (bf16[4,32,1024]{2,1,0:T(8,128)(2,1)}, f32[4,32,1024]{2,1,0:T(8,128)}, f32[1,261]{1,0:T(1,128)S(1)}, f32[1,128]{1,0:T(1,128)}, f32[128,1024]{1,0:T(8...) custom-call(bf16[8,4,128,256]{3,2,1,0:T(8,128)(2,1)S(1)} %copy-done., ...), custom_call_target="tpu_custom_call" | custom-call | tf_op jit(solution)/shard_map/finish/pallas_call | solution.py:732
  182.2 0.6 reduce.4
  (47 shorter events, 1.6 us)
Async XLA Ops:
  12.5 1.1 copy-start.7
  13.3 1.2 copy-start.8
  13.3 2.2 %copy-start.9 = (f32[2,2,16,261]{3,2,1,0:T(8,128)S(1)}, f32[2,2,16,261]{3,2,1,0:T(8,128)}, u32[]{:S(2)}) copy-start(f32[2,2,16,261]{3,2,1,0:T(8,128)} %constant.18.clone) | copy-start | bytes 200452
  19.1 150.8 %copy-start = (bf16[384,1024]{1,0:T(8,128)(2,1)S(1)}, bf16[384,1024]{1,0:T(8,128)(2,1)}, u32[]{:S(2)}) copy-start(bf16[384,1024]{1,0:T(8,128)(2,1)} %pad.25.kproj_ref.key_ref) | copy-start | bytes 2359300
  19.1 150.8 %copy-start.1 = (bf16[384,1024]{1,0:T(8,128)(2,1)S(1)}, bf16[384,1024]{1,0:T(8,128)(2,1)}, u32[]{:S(2)}) copy-start(bf16[384,1024]{1,0:T(8,128)(2,1)} %pad.26.vproj_ref.value_ref) | copy-start | bytes 2359300
  169.9 1.6 copy-start.2
  171.5 1.1 copy-start.3
  172.5 1.1 copy-start.4
  173.6 0.9 copy-start.5
  174.5 0.9 copy-start.6

commit v5 on v4

--- a/solution.py
+++ b/solution.py
@@ -195,17 +195,46 @@
             copy.wait()
 
 
+def sin_half_turns(turns):
+    whole = jnp.floor(turns + 0.5)
+    part = turns - whole
+    odd = whole - 2.0 * jnp.floor(whole * 0.5)
+    square = part * part
+    total = jnp.full_like(square, SINE[-1])
+    for term in SINE[-2::-1]:
+        total = total * square + term
+    return part * total * (1.0 - 2.0 * odd)
+
+
+def axis_rows(axis, side, first, lanes):
+    place = (lax.broadcasted_iota(jnp.int32, (48, 1), 0) + first).astype(FLOAT)
+    coord = -1.0 + 2.0 * place / (side - 1.0)
+    here = lanes[:, 128 * axis : 128 * axis + 256]
+    rate = 1.0 + here[0:1] * (side * 0.5 - 1.0) * (1.0 / (BANDS - 1))
+    waves = sin_half_turns(coord * rate + here[1:2]) * here[2 + axis : 3 + axis]
+    empty = jnp.zeros((48, LANES - 256), FLOAT)
+    table = jnp.concatenate([empty, waves] if axis else [waves, empty], axis=1)
+    total = jnp.sum(waves, axis=1, keepdims=True) + coord
+    table = table + coord * lanes[4 + axis : 5 + axis] - (total * (1.0 / FEAT)) * lanes[6:7]
+    return table, coord, total
+
+
 def main_kernel(
-    msg_ref, lat_ref, cot_ref, fgain_ref, qgain_ref, hgain_ref, tgain_ref, ogain_ref,
-    kproj_ref, vproj_ref, thigh_ref, tlow_ref, hot_ref,
-    w0, w1, w2, w3, w4, w5, w6, w7, w8, w9,
-    result_ref, grad_ref, value_ref, key_ref, sums_ref,
-    ws, msgs, pixcoefs, upcoefs, pixels, scores, ups, weights, sums, tops, totals, raw_all, qrows,
-    part_out, part_in, q_out, q_in, kv_out, kv_in, kv_more, probs, mixed_out, mixed_in, gm_out, gm_in,
-    kvx_out, kvx_in, gq_in, gkv_in, up_ref, mix_all, gcross_out, gcross_all, gains_out, gains_all, gmix,
-    x_out, x_pass, x_all, g_out, g_all, own, zsend, zrecv, last, nsend, nextra, nrecv, nmore,
-    w_sem, l_sem, ty_s, ty_r, tx_s, tx_r, mate_s, mate_r, xg_s, xg_r, y_s, y_r, z_s, z_r, o_s, o_r,
+    sizes_ref, *refs
 ):
+    names = IN_NAMES + OUT_NAMES + SCRATCH_NAMES
+    r = dict(zip(names, refs))
+    matrices = [r["w%d" % i] for i in range(10)]
+    result_ref, grad_ref, value_ref, key_ref, sums_ref = [r[n] for n in OUT_NAMES]
+    (ws, msgs, pixcoefs, upcoefs, pixels, scores, ups, weights, sums, tops, totals, raw_all, qrows,
+     part_out, part_in, q_out, q_in, kv_out, kv_in, kv_more, probs, mixed_out, mixed_in, gm_out, gm_in,
+     kvx_out, kvx_in, gq_in, gkv_in, up_ref, mix_all, gcross_out, gcross_all, gains_out, gains_all, gmix,
+     x_out, x_pass, x_all, g_out, g_all, own, held, relay_in, zsend, zrecv, last, nsend, nextra, nrecv, nmore,
+     msg_rows, msg_ref, thigh_ref, tlow_ref, kproj_ref, vproj_ref, fgain_ref, result_v, grad_v, value_v, key_v,
+     w_sem, l_sem, ty_s, ty_r, tx_s, tx_r, mate_s, mate_r, xg_s, xg_r, y_s, y_r, z_s, z_r, ac_s, ac_r, re_s, re_r,
+     in_sem, out_sem,
+     pix_v, mask_v, lat_ref, cot_ref, fgain_v, qgain_ref, hgain_ref, tgain_ref, ogain_ref,
+     kraw_v, vraw_v, hot_ref, hotcol_ref, ids_ref, lanes_ref) = [r[n] for n in SCRATCH_NAMES]
     ty, tx = lax.axis_index("ty"), lax.axis_index("tx")
     z, y = tx // 2, lax.rem(tx, 2)
     tys = [{"ty": lax.rem(ty + d, 4), "tx": tx} for d in (1, 2, 3)]
@@ -213,15 +242,21 @@
     mate = {"ty": 2 * (ty // 2) + 1 - lax.rem(ty, 2), "tx": tx}
     beside = {"ty": ty, "tx": 2 * z + 1 - y}
     on_ty, on_tx = Ring(tys, ty_s, ty_r), Ring(txs, tx_s, tx_r)
-    on_mate = Ring([mate], mate_s, mate_r)
+    on_mate, across = Ring([mate], mate_s, mate_r), Ring([tys[1]], ac_s, ac_r)
     handing, passing = Ring(tys, xg_s, xg_r), Ring([beside], y_s, y_r)
-    giving = Ring(tys, o_s, o_r)
     loads = []
-    for i, w in enumerate((w0, w1, w2, w3, w4, w5, w6, w7, w8, w9)):
+    small = []
+    for i, (name, into) in enumerate(zip(IN_NAMES, COPIED_NAMES)):
+        small.append(pltpu.make_async_copy(r[name], r[into], in_sem.at[i]))
+        small[i].start()
+    for i, w in enumerate(matrices):
         loads.append(pltpu.make_async_copy(w, ws.at[i], w_sem.at[i]))
         loads[i].start()
     cross, up, down, tq, tk, tv, tproj, fup, fdown = range(1, 10)
-    greet(tys + txs)
+    partners = tys + txs
+    barrier = pltpu.get_barrier_semaphore()
+    for place in partners:
+        pl.semaphore_signal(barrier, inc=1, device_id=place, device_id_type=MESH)
     ty_at = lambda d: lax.rem(ty + d + 1, 4)
     tx_at = lambda d: lax.rem(tx + d + 1, 8)
 
@@ -279,6 +314,14 @@
             device_id_type=MESH,
         )
 
+    at_end = (z == 0) | (z == 3)
+
+    def relay(w):
+        return pltpu.make_async_remote_copy(
+            src_ref=zsend.at[w, 1], dst_ref=relay_in.at[w], send_sem=re_s.at[w], recv_sem=re_r.at[w],
+            device_id={"ty": ty, "tx": 2 * (1 + z // 2) + y}, device_id_type=MESH,
+        )
+
     def stage_one(w):
         i = slot_x(w)
         if isinstance(w, int):
@@ -286,28 +329,80 @@
         else:
             finish([passing.copy(6 + w, 0, g_all.at[w, 0], g_all.at[w, 1])])
         right = g_all[w].reshape(256, 256)
-        for c in range(4):
-            at = lax.rem(z + c + 1, 4)
-            total = outer(x_all[i, at].reshape(256, 128), right)
-            if c == 3:
-                own[w] = total
-            else:
+
+        def part(c):
+            return outer(x_all[i, lax.rem(z + c + 1, 4)].reshape(256, 128), right)
+
+        zsend[w, 1] = part(1).astype(BFLOAT)
+
+        @pl.when(at_end)
+        def _():
+            relay(w).start()
+
+        @pl.when(jnp.logical_not(at_end))
+        def _():
+            zcopy(w, 1).start()
+
+        for c, middle in ((0, 1), (2, 2)):
+            total = part(c)
+
+            @pl.when(z == middle)
+            def _():
+                held[w] = total
+
+            @pl.when(z != middle)
+            def _():
                 zsend[w, c] = total.astype(BFLOAT)
                 zcopy(w, c).start()
 
+        own[w] = part(3)
+
+    def stage_two(w):
+        for c, middle in ((0, 1), (2, 2)):
+            @pl.when(z == middle)
+            def _():
+                relay(w).wait_recv()
+                zsend[w, c] = (held[w] + relay_in[w].astype(FLOAT)).astype(BFLOAT)
+                zcopy(w, c).start()
+
     def out_copies(w):
-        return [giving.copy(w, d, last.at[w], sums_ref.at[w, ty]) for d in range(3)] + [
-            pltpu.make_async_copy(last.at[w], sums_ref.at[w, ty], l_sem.at[w])
+        return [
+            on_mate.copy(2 + w, 0, last.at[w], sums_ref.at[w, ty]),
+            across.copy(w, 0, last.at[w], sums_ref.at[w, ty]),
+            pltpu.make_async_copy(last.at[w], sums_ref.at[w, ty], l_sem.at[w]),
         ]
 
     def stage_three(w):
         total = own[w]
-        for c in range(3):
+        for c in (0, 2):
             zcopy(w, c).wait()
             total = total + zrecv[w, c].astype(FLOAT)
-        last[w] = total.astype(BFLOAT)
+        own[w] = total
+
+        @pl.when(at_end)
+        def _():
+            relay(w).wait_send()
+            zcopy(w, 1).wait_recv()
+            own[w] = own[w] + zrecv[w, 1].astype(FLOAT)
+
+        @pl.when(jnp.logical_not(at_end))
+        def _():
+            zcopy(w, 1).wait_send()
+
+        last[w] = own[w].astype(BFLOAT)
         for copy in out_copies(w):
             copy.start()
+
+    def stage_four(w):
+        across.copy(w, 0, last.at[w], sums_ref.at[w, ty]).wait()
+        there = sums_ref.at[w, lax.rem(ty + 2, 4)]
+        on_mate.copy(10 + w, 0, there, there).start()
+
+    def stage_end(w):
+        there = sums_ref.at[w, lax.rem(ty + 2, 4)]
+        on_mate.copy(10 + w, 0, there, there).wait()
+        mine = out_copies(w)
+        finish(mine[:1], mine[2:])
 
     def product_start(i, left, right, gains):
         product = outer(left, right)
@@ -331,21 +426,116 @@
         into[ty, 256:272] = more.astype(BFLOAT)
         return on_tx.start(8 + 3 * i, lambda d: into.at[ty, mine], lambda d: into.at[ty, mine])
 
-    def product_end(i, copies, into):
+    def hand_out(k, source, out):
+        mine = pltpu.make_async_copy(source, out.at[ty], out_sem.at[k])
+        mine.start()
+        return on_mate.start(18 + k, lambda d: source, lambda d: out.at[ty]) + [mine], across.start(
+            8 + k, lambda d: source, lambda d: out.at[ty]
+        )
+
+    def hand_on(k, copies, out):
+        near, far = copies
+        finish(far)
+        there = out.at[lax.rem(ty + 2, 4)]
+        return near + on_mate.start(22 + k, lambda d: there, lambda d: there)
+
+    def product_end(i, copies, into, out):
         finish(copies)
-        return to_ty(7 + i, into.at[ty], into.at[ty])
+        return hand_out(i, into.at[ty], out)
 
     def message(d):
         return on_tx.copy(0, d, msg_ref, msgs.at[tx])
 
+    share, width = lat_ref.shape[1], lat_ref.shape[2]
+    count = 2 * share
+    high, wide = pix_v.shape[2] // HALVES, pix_v.shape[3]
+    for copy in small:
+        copy.wait()
+    lanes = lanes_ref[...]
+    ids = ids_ref[...]
+    sides = [jnp.zeros((1, 1), FLOAT) + sizes_ref[b].astype(FLOAT) for b in range(2)]
+    live_planes = jnp.where(mask_v[...] > 0, 1.0, 0.0).reshape(4 * high, wide)
+    planes = jnp.concatenate(
+        [pix_v[...].astype(FLOAT).reshape(12 * high, wide), live_planes], axis=0
+    ).astype(BFLOAT)
+    flat = dot_nn(planes, hotcol_ref[...])
+    row_of = lax.broadcasted_iota(jnp.int32, (2 * high, 1), 0).astype(FLOAT)
+    picks = [ids[0:1] + half * high == row_of for half in range(HALVES)]
+
+    def flatten(plane, half):
+        rows = flat[plane * 2 * high : (plane + 1) * 2 * high]
+        return jnp.sum(jnp.where(picks[half], rows, 0.0), axis=0, keepdims=True)
+
+    def put_table(b, at, rows):
+        high_part, low_part = split_two(rows)
+        thigh_ref[b, at : at + rows.shape[0]] = high_part
+        tlow_ref[b, at : at + rows.shape[0]] = low_part
+
+    def by_pixel(total, coord, rows):
+        square = coord * coord
+        total_high, total_low = split_two(total)
+        square_high, square_low = split_two(square)
+        left = jnp.concatenate([total_high, total_low, square_high, square_low], axis=1)
+        spread_out = outer(left, rows)
+        return spread_out[0:1] + spread_out[1:2], spread_out[2:3] + spread_out[3:4]
+
+    zeros = jnp.zeros((GROUP, LANES), BFLOAT)
+    lane_at = lax.broadcasted_iota(jnp.int32, (16, LANES), 1)
+    row_at = lax.broadcasted_iota(jnp.int32, (16, LANES), 0)
+    for b in range(2):
+        _, col_coord, col_total = axis_rows(1, sides[b], tx * wide, lanes)
+        col_sum, col_square = by_pixel(col_total, col_coord, hot_ref[64:112])
+        for half in range(HALVES):
+            first = ty * (2 * high) + half * high
+            table, coord, total = axis_rows(0, sides[b], first, lanes)
+            row_sum, row_square = by_pixel(total, coord, hot_ref[16:64])
+            put_table(b, half * GROUP + 16, table)
+            thigh_ref[b, half * GROUP + 64 : half * GROUP + GROUP] = zeros[64:]
+            tlow_ref[b, half * GROUP + 64 : half * GROUP + GROUP] = zeros[64:]
+            channel = row_at - (half * 8 + b * 4)
+            colour = (channel >= 0) & (channel < 3)
+            value = jnp.where(channel == lane_at, 1.0, 0.0) - (1.0 / FEAT) * lanes[6:7]
+            put_table(b, half * GROUP, jnp.where(colour, value, 0.0))
+            colours = [flatten(b * 3 + c, half) for c in range(3)]
+            mean = (colours[0] + colours[1] + colours[2] + row_sum + col_sum) * (1.0 / FEAT)
+            square = sum(c * c for c in colours) + row_square + col_square + 2.0 * BANDS
+            rate = lax.rsqrt(square * (1.0 / FEAT) - mean * mean + EPSILON)
+            side = sides[b]
+            first_row = jnp.zeros((1, 1), FLOAT) + first.astype(FLOAT)
+            first_col = jnp.zeros((1, 1), FLOAT) + (tx * wide).astype(FLOAT)
+            live = (
+                (flatten(6 + b, half) > 0.5)
+                & (ids[0:1] + first_row < side)
+                & (ids[1:2] + first_col < side)
+            )
+            for c, row in enumerate(colours + [jnp.where(live, rate, 0.0)]):
+                at = half * 8 + b * 4 + c
+                msg_rows[at : at + 1] = row
+    msg_ref[...] = msg_rows[...].astype(BFLOAT)
+    pl.semaphore_wait(barrier, len(partners))
     for d in range(7):
         message(d).start()
     msgs[tx] = msg_ref[...]
+    for b in range(2):
+        for t in range(8):
+            table, _, _ = axis_rows(1, sides[b], t * wide, lanes)
+            at = (2 + t) * GROUP
+            thigh_ref[b, at : at + 64] = zeros[:64]
+            tlow_ref[b, at : at + 64] = zeros[:64]
+            put_table(b, at + 64, table)
+            thigh_ref[b, at + 112 : at + GROUP] = zeros[:16]
+            tlow_ref[b, at + 112 : at + GROUP] = zeros[:16]
+    for raw_ref, padded in ((kraw_v, kproj_ref), (vraw_v, vproj_ref)):
+        padded[0:256] = raw_ref[0:256]
+        padded[256:272] = jnp.concatenate(
+            [raw_ref[256:FEAT].astype(FLOAT), jnp.zeros((272 - FEAT, width), FLOAT)], axis=0
+        ).astype(BFLOAT)
+        padded[272:LANES] = jnp.zeros((LANES - 272, width), BFLOAT)
+    fgain_ref[...] = jnp.zeros_like(fgain_ref)
+    fgain_ref[:, 0:FEAT] = fgain_v[...]
     pixels[0:GROUP] = hot_ref[...]
     pixels[GROUP : 2 * GROUP] = hot_ref[...]
     gains_out[...] = jnp.zeros_like(gains_out)
-    share = lat_ref.shape[1]
-    count, width = 2 * share, lat_ref.shape[2]
     cot = cot_ref[ty]
     give_g(0, cot)
     fgain = fgain_ref[...]
@@ -497,8 +687,8 @@
         gm_out[h] = g_mixed[:, 128 * h : 128 * h + 128]
     copies = spread(4, gm_out, gm_in)
     give_g(2, g_tower)
-    result_ref[ty] = (three + times(fact, fdown)).astype(BFLOAT)
-    later += to_ty(2, result_ref.at[ty], result_ref.at[ty])
+    result_v[...] = (three + times(fact, fdown)).astype(BFLOAT)
+    result_copies = hand_out(2, result_v, result_ref)
     pass_x(2)
     pass_x(1)
     pass_x(0)
@@ -544,11 +734,13 @@
     g_hidden = g_two.astype(BFLOAT)
     give_g(6, g_hidden)
     pass_g(3)
+    stage_two(0)
     stage_one(1)
     g_hlift = (times_back(g_hidden, down) * act_slope).astype(BFLOAT)
     give_g(7, g_hlift)
     pass_g(4)
     pass_g(5)
+    stage_two(1)
     stage_one(2)
     g_one, h_grad = norm_rows_back(times_back(g_hlift, up), hgain_ref[...], h_unit, h_rate)
     put_gain(0, h_grad)
@@ -568,8 +760,10 @@
     )
     copies = to_ty(5, up_ref.at[ty], up_ref.at[ty])
     pass_g(6)
+    stage_two(2)
     stage_one(3)
     finish(later, gain_copies, gcross_copies)
+    result_copies = hand_on(2, result_copies, result_ref)
     gain_rows = gains_all[0, 0] + gains_all[0, 1] + gains_all[0, 2] + gains_all[0, 3]
     ncopies = product_start(
         0, mix_all[...].reshape(4 * share, LANES), gcross_all[...].reshape(4 * share, 256), gain_rows
@@ -596,6 +790,7 @@
 
     def first_steps(t, _):
         back_step(t)
+        stage_two(3 + t)
         stage_one(4 + t)
         return 0
 
@@ -605,12 +800,14 @@
         return 0
 
     lax.fori_loop(0, 3, first_steps, 0)
-    ncopies = product_join(0, ncopies, value_ref)
+    ncopies = product_join(0, ncopies, value_v)
     lax.fori_loop(3, 4, first_steps, 0)
-    lax.fori_loop(4, 8, second_steps, 0)
+    lax.fori_loop(4, 6, second_steps, 0)
+    stage_two(7)
+    lax.fori_loop(6, 8, second_steps, 0)
     part_out[...] = features_of(sums, None, thigh_ref, tlow_ref).reshape(part_out.shape)
     copies = on_ty.start(9, lambda d: part_out.at[ty_at(d)], lambda d: part_in.at[d])
-    ncopies = product_end(0, ncopies, value_ref)
+    value_copies = product_end(0, ncopies, value_v, value_ref)
     unit, rate = norm_rows(lat_ref[ty].astype(FLOAT))
     raw_mix = part_out[ty]
     finish(copies)
@@ -627,28 +824,78 @@
     gains_out[1, 0, 1:2] = features[:, 0:256]
     gains_out[1, 1, 1:2, 0:128] = features[:, 256:384]
     mcopies += over_ty(10, gains_out.at[1], gains_all.at[1])
-    grad_ref[ty] = (g_one + grad).astype(BFLOAT)
-    ncopies += to_ty(11, grad_ref.at[ty], grad_ref.at[ty])
+    grad_v[...] = (g_one + grad).astype(BFLOAT)
+    grad_copies = hand_out(3, grad_v, grad_ref)
+    for w in range(4):
+        stage_four(w)
     finish(mcopies)
     gain_rows = gains_all[1, 0] + gains_all[1, 1] + gains_all[1, 2] + gains_all[1, 3]
     right = qrows[:, pl.ds(pl.multiple_of(ty * 256, 256), 256)]
     mcopies = product_start(1, gmix[...].reshape(4 * share, LANES), right, gain_rows)
     stage_three(4)
     stage_three(5)
-    mcopies = product_join(1, mcopies, key_ref)
+    mcopies = product_join(1, mcopies, key_v)
+    value_copies = hand_on(0, value_copies, value_ref)
+    grad_copies = hand_on(3, grad_copies, grad_ref)
     stage_three(6)
-    ncopies += product_end(1, mcopies, key_ref)
     stage_three(7)
-    finish(ncopies)
+    key_copies = product_end(1, mcopies, key_v, key_ref)
+    for w in range(4, 8):
+        stage_four(w)
+    key_copies = hand_on(1, key_copies, key_ref)
+    finish(result_copies, value_copies, grad_copies, key_copies)
     for w in range(8):
-        finish(out_copies(w))
-
-
-def main_call(msg, lat, cot, gains, key_rows, value_rows, thigh, tlow, hot, matrices):
+        stage_end(w)
+
+
+IN_NAMES = (
+    "pixels", "pixel_mask", "latents", "cotangent", "feature_gain", "query_gain", "hidden_gain", "tower_gain",
+    "final_gain", "key_proj", "value_proj", "hot", "hotcol", "ids", "lanes",
+) + tuple("w%d" % i for i in range(10))
+COPIED_NAMES = (
+    "pix_v", "mask_v", "lat_v", "cot_v", "fgain_v", "qgain_v", "hgain_v", "tgain_v", "ogain_v", "kraw_v", "vraw_v",
+    "hot_v", "hotcol_v", "ids_v", "lanes_v",
+)
+OUT_NAMES = ("result_ref", "grad_ref", "value_ref", "key_ref", "sums_ref")
+SCRATCH_NAMES = (
+    "ws", "msgs", "pixcoefs", "upcoefs", "pixels_v", "scores", "ups", "weights", "sums", "tops", "totals",
+    "raw_all", "qrows", "part_out", "part_in", "q_out", "q_in", "kv_out", "kv_in", "kv_more", "probs",
+    "mixed_out", "mixed_in", "gm_out", "gm_in", "kvx_out", "kvx_in", "gq_in", "gkv_in", "up_ref", "mix_all",
+    "gcross_out", "gcross_all", "gains_out", "gains_all", "gmix", "x_out", "x_pass", "x_all", "g_out", "g_all",
+    "own", "held", "relay_in", "zsend", "zrecv", "last", "nsend", "nextra", "nrecv", "nmore", "msg_rows", "msg", "thigh", "tlow",
+    "kproj", "vproj", "fgain", "result_v", "grad_v", "value_v", "key_v",
+    "w_sem", "l_sem", "ty_s", "ty_r", "tx_s", "tx_r", "mate_s", "mate_r", "xg_s", "xg_r", "y_s", "y_r",
+    "z_s", "z_r", "ac_s", "ac_r", "re_s", "re_r", "in_sem", "out_sem",
+) + COPIED_NAMES
+SINE = tuple((-1) ** n * math.pi ** (2 * n + 1) / math.factorial(2 * n + 1) for n in range(7))
+
+
+def pixel_constants(high, wide):
+    length = -(-high * wide // 128) * 128
+    hot = np.zeros((GROUP, length), np.float32)
+    ids = np.full((8, length), 1e6, np.float32)
+    for i in range(high):
+        for j in range(wide):
+            hot[16 + i, i * wide + j] = 1.0
+            hot[64 + j, i * wide + j] = 1.0
+            ids[0, i * wide + j], ids[1, i * wide + j] = i, j
+    lanes = np.zeros((8, LANES), np.float32)
+    for axis in range(2):
+        first = 5 + 2 * BANDS * axis
+        lanes[0, first : first + 2 * BANDS] = np.tile(np.arange(BANDS), 2)
+        lanes[1, first + BANDS : first + 2 * BANDS] = 0.5
+        lanes[2 + axis, first : first + 2 * BANDS] = 1.0
+        lanes[4 + axis, 3 + axis] = 1.0
+    lanes[6, :FEAT] = 1.0
+    return jnp.asarray(hot, BFLOAT), jnp.asarray(hot[64 : 64 + wide], BFLOAT), jnp.asarray(ids), jnp.asarray(lanes)
+
+
+def main_call(sizes, inputs, matrices):
+    pixels, mask, lat, cot = inputs[:4]
     _, share, width = lat.shape
-    rows, length = 8 * share, msg.shape[1]
+    inputs = inputs + pixel_constants(pixels.shape[2] // HALVES, pixels.shape[3])
+    rows, length = 8 * share, inputs[11].shape[1]
     dma = pltpu.SemaphoreType.DMA
-    vmem = pl.BlockSpec(memory_space=pltpu.VMEM)
     hbm = pl.BlockSpec(memory_space=pl.ANY)
     shape = jax.ShapeDtypeStruct
     half, full = (lambda *s: pltpu.VMEM(s, BFLOAT)), (lambda *s: pltpu.VMEM(s, FLOAT))
@@ -661,8 +908,8 @@
             shape((4, 272, 256), BFLOAT),
             shape((8, 4, 128, 256), BFLOAT),
         ),
-        in_specs=[vmem] * 13 + [hbm] * 10,
-        out_specs=(vmem, vmem, vmem, vmem, hbm),
+        in_specs=[pl.BlockSpec(memory_space=pltpu.SMEM)] + [hbm] * 25,
+        out_specs=(hbm,) * 5,
         scratch_shapes=[
             half(10, width, width), half(8, 16, length), half(8, rows, 2 * GROUP), half(8, rows, 2 * GROUP),
             half(2 * GROUP, length), full(rows, length), full(rows, length), half(rows, length),
@@ -675,31 +922,49 @@
             full(4, share, LANES), half(4, share, LANES), half(4, share, 256), half(4, share, 256),
             full(2, 4, 8, 256), full(2, 4, 8, 256), half(4, share, LANES),
             half(6, 2, 4, share, 128), half(6, 4, 4, share, 128), half(6, 4, 2, 4, share, 128),
-            half(8, 4, share, 256), half(8, 2, 4, share, 256), full(8, 128, 256),
+            half(8, 4, share, 256), half(8, 2, 4, share, 256), full(8, 128, 256), full(8, 128, 256), half(8, 128, 256),
             half(8, 3, 128, 256), half(8, 3, 128, 256), half(8, 128, 256),
             half(2, 8, 32, 256), half(2, 16, 256), half(2, 7, 32, 256), half(2, 7, 16, 256),
+            full(16, length), half(16, length), half(2, 10 * GROUP, LANES), half(2, 10 * GROUP, LANES),
+            half(LANES, width), half(LANES, width), full(1, LANES),
+            half(share, width), half(share, width), half(4, 272, 256), half(4, 272, 256),
             dma((10,)), dma((8,)), dma((12, 3)), dma((12, 3)), dma((13, 7)), dma((13, 7)),
-            dma((2, 1)), dma((2, 1)), dma((20, 3)), dma((20, 3)), dma((14, 1)), dma((14, 1)),
-            dma((8, 3)), dma((8, 3)), dma((8, 3)), dma((8, 3)),
-        ],
+            dma((26, 1)), dma((26, 1)), dma((20, 3)), dma((20, 3)), dma((14, 1)), dma((14, 1)),
+            dma((8, 3)), dma((8, 3)), dma((12, 1)), dma((12, 1)), dma((8,)), dma((8,)), dma((15,)), dma((4,)),
+        ] + [pltpu.VMEM(v.shape, v.dtype) for v in inputs],
         compiler_params=pltpu.CompilerParams(
-            collective_id=1, has_side_effects=True, vmem_limit_bytes=60 << 20
+            collective_id=1, has_side_effects=True, vmem_limit_bytes=62 << 20
         ),
         name="main",
-    )(msg, lat, cot, *gains, key_rows, value_rows, thigh, tlow, hot, *matrices)
-
-
-def finish_kernel(
-    sums_ref, cross_core_ref, query_core_ref, latent_ref, result_in_ref, cross_ref, query_ref, value_ref, key_ref,
-    *outs,
-):
+    )(sizes, *inputs, *matrices)
+
+
+def finish_kernel(*refs):
+    ins, outs, stage, held = refs[:9], refs[9:28], refs[28:37], refs[37:56]
+    in_sem, out_sem = refs[56:]
+    copies = [pltpu.make_async_copy(a, v, in_sem.at[i]) for i, (a, v) in enumerate(zip(ins, stage))]
+    for copy in copies:
+        copy.start()
     tx = lax.axis_index("tx")
-    result_ref, latent_out, feat_out, qgain_out, query_out, key_out, value_out, cross_out = outs[:8]
-    for w, out in enumerate(outs[8:16]):
+    sums_ref, cross_core_ref, query_core_ref, latent_ref, result_in_ref, cross_ref, query_ref, value_ref, key_ref = stage
+    result_ref, latent_out, feat_out, qgain_out, query_out, key_out, value_out, cross_out = held[:8]
+    written = []
+
+    def write(*places):
+        for i in places:
+            written.append(pltpu.make_async_copy(held[i], outs[i], out_sem.at[i]))
+            written[-1].start()
+
+    copies[0].wait()
+    for w in range(8):
         for h in range(4):
-            out[:, 256 * h : 256 * h + 256] = sums_ref[w, h].astype(FLOAT)
+            held[8 + w][:, 256 * h : 256 * h + 256] = sums_ref[w, h].astype(FLOAT)
+        write(8 + w)
+    for copy in copies[1:]:
+        copy.wait()
     result_ref[...] = result_in_ref[...]
     latent_out[...] = latent_ref[...].astype(FLOAT)
+    write(0, 1)
     here = pl.ds(pl.multiple_of(tx * 128, 128), 128)
     quarter = tx // 2
     inside = pl.ds(pl.multiple_of(lax.rem(tx, 2) * 128, 128), 128)
@@ -707,92 +972,44 @@
     cross_core = jnp.concatenate([cross_core_ref[h] for h in range(4)], axis=1)
     query_core = jnp.concatenate([query_core_ref[h] for h in range(4)], axis=1)
     value_out[...] = dot_nt(cross_core, cross_ref[...])[:FEAT]
+    write(6)
     key_out[...] = (dot_nn(query_core, query_ref[...]) * scale)[:FEAT]
-    row = lax.broadcasted_iota(jnp.int32, (272, 1024), 0)
-    core = jnp.where(row < FEAT, cross_core.astype(FLOAT), 0.0).astype(BFLOAT)
-    cross_out[...] = outer(value_ref[0:272, here], core)
-    row = lax.broadcasted_iota(jnp.int32, (272, 128), 0)
+    write(5)
+    cross_out[...] = outer(value_ref[:, here], cross_core[:FEAT])
     mine = query_core_ref[quarter, :, inside].astype(FLOAT)
-    core = jnp.where(row < FEAT, mine, 0.0).astype(BFLOAT)
-    query_out[...] = outer(core, key_ref[0:272]) * scale
+    query_out[...] = outer(mine[:FEAT].astype(BFLOAT), key_ref[...]) * scale
+    write(4, 7)
     qgain_out[...] = mine[264:265]
     more = jnp.concatenate([query_core_ref[h, 256:272] for h in range(2)], axis=1).astype(FLOAT)
     feat_out[...] = more[9:10, 0:FEAT]
     mine = cross_core_ref[quarter, 256:272, inside].astype(FLOAT)
-    for i, out in enumerate(outs[16:19]):
-        out[...] = mine[8 + i : 9 + i]
-
-
-def finish_call(sums, cross_core, query_core, latent_grad, result, cross_proj, query_proj, value_rows, key_rows):
-    width = cross_proj.shape[0]
+    for i in range(3):
+        held[16 + i][...] = mine[8 + i : 9 + i]
+    write(2, 3, 16, 17, 18)
+    for copy in written:
+        copy.wait()
+
+
+def finish_call(*inputs):
+    width = inputs[5].shape[0]
     shape = lambda *s: jax.ShapeDtypeStruct(s, FLOAT)
-    rows = latent_grad.shape
+    rows = inputs[3].shape
     block = [shape(128, width)]
-    vmem = pl.BlockSpec(memory_space=pltpu.VMEM)
+    hbm = pl.BlockSpec(memory_space=pl.ANY)
+    outs = (
+        [jax.ShapeDtypeStruct(rows, BFLOAT), shape(*rows), shape(1, FEAT), shape(1, 128)]
+        + block + [shape(FEAT, width)] * 2 + block + block * 8 + [shape(1, 128)] * 3
+    )
     return pl.pallas_call(
         finish_kernel,
-        out_shape=(
-            [jax.ShapeDtypeStruct(rows, BFLOAT), shape(*rows), shape(1, FEAT), shape(1, 128)]
-            + block + [shape(FEAT, width)] * 2 + block + block * 8 + [shape(1, 128)] * 3
-        ),
-        in_specs=[vmem] * 9,
-        out_specs=[vmem] * 19,
-        compiler_params=pltpu.CompilerParams(vmem_limit_bytes=48 << 20),
+        out_shape=outs,
+        in_specs=[hbm] * 9,
+        out_specs=[hbm] * 19,
+        scratch_shapes=[pltpu.VMEM(v.shape, v.dtype) for v in list(inputs) + outs]
+        + [pltpu.SemaphoreType.DMA((9,)), pltpu.SemaphoreType.DMA((19,))],
+        compiler_params=pltpu.CompilerParams(vmem_limit_bytes=62 << 20),
         name="finish",
-    )(sums, cross_core, query_core, latent_grad, result, cross_proj, query_proj, value_rows, key_rows)
-
-
-def pixel_tables(image_sizes, row_ids, tile_width):
-    high = len(row_ids) // HALVES
-    all_cols = jnp.arange(8 * tile_width, dtype=jnp.int32)
-    row_table, row_coord, row_sum = axis_tables(image_sizes, row_ids, 3, 5)
-    col_table, col_coord, col_sum = axis_tables(image_sizes, all_cols, 4, 5 + 2 * BANDS)
-    row_table = row_table - row_sum[:, :, None] * (1.0 / FEAT)
-    col_table = col_table - col_sum[:, :, None] * (1.0 / FEAT)
-    row_table = row_table.reshape(2, HALVES, high, FEAT)
-    col_table = col_table.reshape(2, 8, tile_width, FEAT)
-    colours = np.zeros((2, HALVES, 16, FEAT), np.float32)
-    for b in range(2):
-        for half in range(HALVES):
-            for c in range(3):
-                colours[b, half, half * 8 + b * 4 + c] = -1.0 / FEAT
-                colours[b, half, half * 8 + b * 4 + c, c] += 1.0
-    first = jnp.concatenate(
-        [jnp.asarray(colours), row_table, jnp.zeros((2, HALVES, GROUP - 16 - high, FEAT), FLOAT)], axis=2
-    )
-    col_from = 16 + -(-high // 8) * 8
-    second = jnp.pad(col_table, ((0, 0), (0, 0), (col_from, GROUP - col_from - tile_width), (0, 0)))
-    table = jnp.concatenate([first, second], axis=1).reshape(2, 10 * GROUP, FEAT)
-    table = jnp.pad(table, ((0, 0), (0, 0), (0, LANES - FEAT)))
-    hot = np.zeros((GROUP, -(-high * tile_width // 128) * 128), np.float32)
-    for i in range(high):
-        for j in range(tile_width):
-            hot[16 + i, i * tile_width + j] = 1.0
-            hot[col_from + j, i * tile_width + j] = 1.0
-    here = lax.dynamic_slice_in_dim
-    at = lax.axis_index("tx") * tile_width
-    return (
-        split_two(table), jnp.asarray(hot, BFLOAT),
-        (row_coord, row_sum), (here(col_coord, at, tile_width, 1), here(col_sum, at, tile_width, 1)),
-    )
-
-
-def pixel_message(pixels, live, rows, cols, length):
-    (row_coord, row_sum), (col_coord, col_sum) = rows, cols
-    _, _, height, width = pixels.shape
-    wide = pixels.astype(FLOAT)
-    mean = (jnp.sum(wide, axis=1) + row_sum[:, :, None] + col_sum[:, None, :]) * (1.0 / FEAT)
-    square = (
-        jnp.sum(wide * wide, axis=1)
-        + (row_coord * row_coord)[:, :, None]
-        + (col_coord * col_coord)[:, None, :]
-        + 2.0 * BANDS
-    ) * (1.0 / FEAT)
-    rate = jnp.where(live, lax.rsqrt(square - mean * mean + EPSILON), 0.0)
-    rows = jnp.concatenate([pixels, rate.astype(BFLOAT)[:, None]], axis=1)
-    rows = rows.reshape(2, 4, HALVES, height // HALVES * width)
-    rows = jnp.transpose(rows, (2, 0, 1, 3)).reshape(16, -1)
-    return jnp.pad(rows, ((0, 0), (0, length - rows.shape[1])))
+    )(*inputs)
 
 
 def on_device_fast(
@@ -824,36 +1041,22 @@
     tile_width = pixels.shape[3]
     model_width = latents.shape[2]
     rows_here = latents.shape[1]
-    cross_scale = 1.0 / math.sqrt(model_width)
-    row_ids = lax.axis_index("ty") * tile_height + jnp.arange(tile_height, dtype=jnp.int32)
-    col_ids = lax.axis_index("tx") * tile_width + jnp.arange(tile_width, dtype=jnp.int32)
-    side_sizes = image_sizes[:, None, None]
-    live = (
-        (pixel_mask > 0)
-        & (row_ids[None, :, None] < side_sizes)
-        & (col_ids[None, None, :] < side_sizes)
-    )
-    (thigh, tlow), hot, rows, cols = pixel_tables(image_sizes, row_ids, tile_width)
-    message = pixel_message(pixels, live, rows, cols, hot.shape[1])
     share = item_count * rows_here // 4
 
     def in_shares(rows):
         return rows.reshape(4, share, rows.shape[-1])
 
-    gain_lanes = jnp.pad(feature_gain, (0, LANES - FEAT))[None]
-    value_rows = jnp.pad(value_proj, ((0, LANES - FEAT), (0, 0)))
-    key_rows = jnp.pad(key_proj, ((0, LANES - FEAT), (0, 0)))
     result, latent_grad, cross_core, query_core, sums = main_call(
-        message, in_shares(latents), in_shares(cotangent),
-        (gain_lanes, query_gain[None], hidden_gain[None], tower_gain[None], final_gain[None]),
-        key_rows, value_rows, thigh, tlow, hot,
+        image_sizes,
+        (pixels, pixel_mask, in_shares(latents), in_shares(cotangent), feature_gain[None], query_gain[None],
+         hidden_gain[None], tower_gain[None], final_gain[None], key_proj, value_proj),
         (query_proj, cross_proj, hidden_up, hidden_down, tower_query, tower_key, tower_value,
          tower_proj, final_up, final_down),
     )
     (result, latent_grad, feature_sum, query_sum, query_grad, key_grad, value_grad, cross_grad,
      final_down_grad, final_up_grad, tower_proj_grad, tower_query_grad, tower_key_grad,
      tower_value_grad, hidden_down_grad, hidden_up_grad, hidden_sum, tower_sum, final_sum) = finish_call(
-        sums, cross_core, query_core, latent_grad, result, cross_proj, query_proj, value_rows, key_rows
+        sums, cross_core, query_core, latent_grad, result, cross_proj, query_proj, value_proj, key_proj
     )
     return (
         result.reshape(latents.shape),

time: 183 us -> 153 us (0.84)
  Pallas kernels: 157 us -> 146 us
  local copies, waits for them, and re-layouts: 13.9 us -> 4.32 us
  other arithmetic: 10.5 us -> 1.27 us
    pallas_call x1, Pallas kernels: 151 us -> 137 us  [main_call(): pl.pallas_call(main_kernel, out_shape=(shape((4, share, width), BFLOAT),...]
    unnamed x21 -> x2, local copies, waits for them, and re-layouts: 6.66 us -> 3.07 us
    pad x4 -> x0, local copies, waits for them, and re-layouts: 3.25 us -> none  [the longest x1 0.97 us: on_device_fast(): key_rows = jnp.pad(key_proj, ((0, LANES - FEAT), (0, 0)))]
    convert_element_type x3 -> x0, other arithmetic: 2.65 us -> none  [the longest x1 1.7 us: split_two(): return (high, (values - high.astype(FLOAT)).astype(BFLOAT))]
    reduce_sum x4 -> x0, other arithmetic: 2.13 us -> none  [the longest x3 1.14 us: axis_tables(): return (table, coord, jnp.sum(waves, axis=2) + coord)]
    pallas_call x1, Pallas kernels: 6.71 us -> 8.82 us  [finish_call(): pl.pallas_call(finish_kernel, out_shape=outs, in_specs=[hbm] * 9, out_spe...]
where the time goes in v5:
time: 153 us
  Pallas kernels  146 us (95%)
  local copies, waits for them, and re-layouts  4.32 us (3%)
    pallas_call x1, Pallas kernels, main_call(): pl.pallas_call(main_kernel, out_shape=(shape((4, share, width), BFLOAT),...  137 us
    pallas_call x1, Pallas kernels, finish_call(): pl.pallas_call(finish_kernel, out_shape=outs, in_specs=[hbm] * 9, out_spe...  8.82 us
    unnamed x2, local copies, waits for them, and re-layouts  3.07 us

profile of v5, /device:TPU:1, one launch (start us, length us, event | category | flops | bytes accessed | tf_op | source)
XLA Modules:
  0.0 152.5 jit_solution(7120744850382569751)
XLA Ops:
  0.7 1.2 broadcast_in_dim.15.refs_4_
  1.9 1.5 copy.46.refs_1_
  3.4 1.6 %copy.45.refs_0_ = bf16[2,3,72,36]{3,2,1,0:T(8,128)(2,1)} copy(bf16[2,3,72,36]{2,0,3,1:T(2,128)(2,1)} %param.26) | data formatting | bytes 62208 | tf_op args[0]
  5.0 137.4 %main.1 = (bf16[4,32,1024]{2,1,0:T(8,128)(2,1)}, bf16[4,32,1024]{2,1,0:T(8,128)(2,1)}, bf16[4,272,256]{2,1,0:T(8,128)(2,1)}, bf16[4,272,256]{2,1,0:T(8,128)(2,1)}, bf16[8,4,128,256]{3,2,1,0:T(8,128)(2,1)}) custom-call(s32[2]{0:T(128)} %sizes_ref.1, bf16[2,3,72,36]{3,2,1,0:T(8,128)(2,1)} %copy.45.refs_0_, s32[2,72,36]{2,1,0:T(8,128)} %copy.46.refs_1_, ...), custom_call_target="tpu_custom_call" | custom-call | tf_op jit(solution)/shard_map/main/pallas_call | solution.py:902
  142.4 8.8 %finish.1 = (bf16[4,32,1024]{2,1,0:T(8,128)(2,1)}, f32[4,32,1024]{2,1,0:T(8,128)}, f32[1,261]{1,0:T(1,128)}, f32[1,128]{1,0:T(1,128)}, f32[128,1024]{1,0:T(8,128...) custom-call(bf16[8,4,128,256]{3,2,1,0:T(8,128)(2,1)} %get-tuple-elem, ...), custom_call_target="tpu_custom_call" | custom-call | tf_op jit(solution)/shard_map/finish/pallas_call | solution.py:1003
  151.3 1.3 reduce

commit v6 on v5

--- a/solution.py
+++ b/solution.py
@@ -227,14 +227,14 @@
     matrices = [r["w%d" % i] for i in range(10)]
     result_ref, grad_ref, value_ref, key_ref, sums_ref = [r[n] for n in OUT_NAMES]
     (ws, msgs, pixcoefs, upcoefs, pixels, scores, ups, weights, sums, tops, totals, raw_all, qrows,
-     part_out, part_in, q_out, q_in, kv_out, kv_in, kv_more, probs, mixed_out, mixed_in, gm_out, gm_in,
+     part_out, part_in, half_out, half_in, up_sent, q_out, q_in, kv_out, kv_in, kv_more, probs, mixed_out, mixed_in, gm_out, gm_in,
      kvx_out, kvx_in, gq_in, gkv_in, up_ref, mix_all, gcross_out, gcross_all, gains_out, gains_all, gmix,
-     x_out, x_pass, x_all, g_out, g_all, own, held, relay_in, zsend, zrecv, last, nsend, nextra, nrecv, nmore,
+     x_out, x_all, g_out, g_all, own, held, relay_in, zsend, zrecv, last, nsend, nextra, nrecv, nmore,
      msg_rows, msg_ref, thigh_ref, tlow_ref, kproj_ref, vproj_ref, fgain_ref, result_v, grad_v, value_v, key_v,
-     w_sem, l_sem, ty_s, ty_r, tx_s, tx_r, mate_s, mate_r, xg_s, xg_r, y_s, y_r, z_s, z_r, ac_s, ac_r, re_s, re_r,
+     w_sem, l_sem, ty_s, ty_r, tx_s, tx_r, mate_s, mate_r, xg_s, xg_r, z_s, z_r, ac_s, ac_r, re_s, re_r, g_s, g_r,
      in_sem, out_sem,
      pix_v, mask_v, lat_ref, cot_ref, fgain_v, qgain_ref, hgain_ref, tgain_ref, ogain_ref,
-     kraw_v, vraw_v, hot_ref, hotcol_ref, ids_ref, lanes_ref) = [r[n] for n in SCRATCH_NAMES]
+     kraw_v, vraw_v, hot_ref, hotrow_ref, ids_ref, lanes_ref) = [r[n] for n in SCRATCH_NAMES]
     ty, tx = lax.axis_index("ty"), lax.axis_index("tx")
     z, y = tx // 2, lax.rem(tx, 2)
     tys = [{"ty": lax.rem(ty + d, 4), "tx": tx} for d in (1, 2, 3)]
@@ -243,7 +243,8 @@
     beside = {"ty": ty, "tx": 2 * z + 1 - y}
     on_ty, on_tx = Ring(tys, ty_s, ty_r), Ring(txs, tx_s, tx_r)
     on_mate, across = Ring([mate], mate_s, mate_r), Ring([tys[1]], ac_s, ac_r)
-    handing, passing = Ring(tys, xg_s, xg_r), Ring([beside], y_s, y_r)
+    over = [{"ty": lax.rem(ty + d, 4), "tx": 2 * z + 1 - y} for d in range(4)]
+    handing = Ring(tys + over, xg_s, xg_r)
     loads = []
     small = []
     for i, (name, into) in enumerate(zip(IN_NAMES, COPIED_NAMES)):
@@ -251,9 +252,9 @@
         small[i].start()
     for i, w in enumerate(matrices):
         loads.append(pltpu.make_async_copy(w, ws.at[i], w_sem.at[i]))
-        loads[i].start()
+    loads[0].start()
     cross, up, down, tq, tk, tv, tproj, fup, fdown = range(1, 10)
-    partners = tys + txs
+    partners = tys + txs + over[1:]
     barrier = pltpu.get_barrier_semaphore()
     for place in partners:
         pl.semaphore_signal(barrier, inc=1, device_id=place, device_id_type=MESH)
@@ -281,28 +282,32 @@
 
     xg = {}
 
+    def handed(i, source, into):
+        return [
+            handing.copy(i, k, source(k), into(0 if k < 3 else 1)) for k in range(7)
+        ]
+
     def give_x(i, rows):
         for c in range(8):
             x_out[i, c % 2, c // 2] = rows[:, 128 * c : 128 * c + 128]
         x_all[i, :, 0, ty] = x_out[i, y]
-        x_pass[i, :, ty] = x_out[i, 1 - y]
-        xg["x", i] = handing.start(
-            i, lambda d: x_out.at[i, y], lambda d: x_all.at[i, :, 0, ty]
-        ) + handing.start(14 + i, lambda d: x_out.at[i, 1 - y], lambda d: x_pass.at[i, :, ty])
+        xg["x", i] = handed(
+            i, lambda k: x_out.at[i, y if k < 3 else 1 - y], lambda slot: x_all.at[i, :, slot, ty]
+        )
+        for copy in xg["x", i]:
+            copy.start()
+
+    def g_copies(w):
+        return handed(
+            6 + w, lambda k: g_out.at[w, lax.rem(ty + k + 1, 4)], lambda slot: g_all.at[w, slot, ty]
+        )
 
     def give_g(w, rows):
         for h in range(4):
             g_out[w, h] = rows[:, 256 * h : 256 * h + 256]
         g_all[w, 0, ty] = g_out[w, ty]
-        xg["g", w] = handing.start(6 + w, lambda d: g_out.at[w, ty_at(d)], lambda d: g_all.at[w, 0, ty])
-
-    def pass_x(i):
-        finish(xg.pop(("x", i)))
-        xg["px", i] = passing.start(i, lambda d: x_pass.at[i], lambda d: x_all.at[i, :, 1])
-
-    def pass_g(w):
-        finish(xg.pop(("g", w)))
-        xg["pg", w] = passing.start(6 + w, lambda d: g_all.at[w, 0], lambda d: g_all.at[w, 1])
+        for copy in g_copies(w):
+            copy.start()
 
     def slot_x(w):
         return min(w, 3) + max(w - 5, 0) if isinstance(w, int) else jnp.minimum(w, 3) + jnp.maximum(w - 5, 0)
@@ -325,9 +330,8 @@
     def stage_one(w):
         i = slot_x(w)
         if isinstance(w, int):
-            finish(xg.pop(("px", i), ()), xg.pop(("pg", w)))
-        else:
-            finish([passing.copy(6 + w, 0, g_all.at[w, 0], g_all.at[w, 1])])
+            finish(xg.pop(("x", i), ()))
+        finish(g_copies(w))
         right = g_all[w].reshape(256, 256)
 
         def part(c):
@@ -401,8 +405,8 @@
     def stage_end(w):
         there = sums_ref.at[w, lax.rem(ty + 2, 4)]
         on_mate.copy(10 + w, 0, there, there).wait()
-        mine = out_copies(w)
-        finish(mine[:1], mine[2:])
+        on_mate.copy(2 + w, 0, last.at[w], sums_ref.at[w, ty]).wait()
+        pltpu.make_async_copy(last.at[w], sums_ref.at[w, ty], l_sem.at[w]).wait()
 
     def product_start(i, left, right, gains):
         product = outer(left, right)
@@ -443,28 +447,41 @@
         finish(copies)
         return hand_out(i, into.at[ty], out)
 
-    def message(d):
-        return on_tx.copy(0, d, msg_ref, msgs.at[tx])
+    def message(k, src, at, where):
+        return pltpu.make_async_remote_copy(
+            src_ref=src, dst_ref=msgs.at[at], send_sem=g_s.at[k], recv_sem=g_r.at[k],
+            device_id=where, device_id_type=MESH,
+        )
+
+    def message_from(k):
+        far = lax.rem(z + 8 - jnp.where(k < 5, k - 1, k - 4), 4)
+        return jnp.where(
+            k == 0, tx, jnp.where(k == 1, 2 * z + 1 - y, 2 * far + jnp.where(k < 5, y, 1 - y))
+        )
 
     share, width = lat_ref.shape[1], lat_ref.shape[2]
     count = 2 * share
-    high, wide = pix_v.shape[2] // HALVES, pix_v.shape[3]
+    high, wide = pix_v.shape[3] // HALVES, pix_v.shape[1]
     for copy in small:
         copy.wait()
     lanes = lanes_ref[...]
     ids = ids_ref[...]
     sides = [jnp.zeros((1, 1), FLOAT) + sizes_ref[b].astype(FLOAT) for b in range(2)]
-    live_planes = jnp.where(mask_v[...] > 0, 1.0, 0.0).reshape(4 * high, wide)
-    planes = jnp.concatenate(
-        [pix_v[...].astype(FLOAT).reshape(12 * high, wide), live_planes], axis=0
-    ).astype(BFLOAT)
-    flat = dot_nn(planes, hotcol_ref[...])
-    row_of = lax.broadcasted_iota(jnp.int32, (2 * high, 1), 0).astype(FLOAT)
-    picks = [ids[0:1] + half * high == row_of for half in range(HALVES)]
+    colours_in, live_in = pix_v[...].astype(FLOAT), jnp.where(mask_v[...] > 0, 1.0, 0.0)
+    plane_rows = -(-wide // 8) * 8
+    filler = [jnp.zeros((plane_rows - wide, HALVES * high), FLOAT)] if plane_rows > wide else []
+    planes = []
+    for b in range(2):
+        for plane in [colours_in[c, :, b, :] for c in range(3)] + [live_in[:, b, :]]:
+            planes += [plane] + filler
+    planes = jnp.concatenate(planes, axis=0).astype(BFLOAT)
+    flat = [dot_nn(planes, hotrow_ref[half]) for half in range(HALVES)]
+    row_of = lax.broadcasted_iota(jnp.int32, (plane_rows, 1), 0).astype(FLOAT)
+    pick = ids[1:2] == row_of
 
     def flatten(plane, half):
-        rows = flat[plane * 2 * high : (plane + 1) * 2 * high]
-        return jnp.sum(jnp.where(picks[half], rows, 0.0), axis=0, keepdims=True)
+        rows = flat[half][plane * plane_rows : (plane + 1) * plane_rows]
+        return jnp.sum(jnp.where(pick, rows, 0.0), axis=0, keepdims=True)
 
     def put_table(b, at, rows):
         high_part, low_part = split_two(rows)
@@ -496,7 +513,7 @@
             colour = (channel >= 0) & (channel < 3)
             value = jnp.where(channel == lane_at, 1.0, 0.0) - (1.0 / FEAT) * lanes[6:7]
             put_table(b, half * GROUP, jnp.where(colour, value, 0.0))
-            colours = [flatten(b * 3 + c, half) for c in range(3)]
+            colours = [flatten(b * 4 + c, half) for c in range(3)]
             mean = (colours[0] + colours[1] + colours[2] + row_sum + col_sum) * (1.0 / FEAT)
             square = sum(c * c for c in colours) + row_square + col_square + 2.0 * BANDS
             rate = lax.rsqrt(square * (1.0 / FEAT) - mean * mean + EPSILON)
@@ -504,7 +521,7 @@
             first_row = jnp.zeros((1, 1), FLOAT) + first.astype(FLOAT)
             first_col = jnp.zeros((1, 1), FLOAT) + (tx * wide).astype(FLOAT)
             live = (
-                (flatten(6 + b, half) > 0.5)
+                (flatten(4 * b + 3, half) > 0.5)
                 & (ids[0:1] + first_row < side)
                 & (ids[1:2] + first_col < side)
             )
@@ -513,9 +530,12 @@
                 msg_rows[at : at + 1] = row
     msg_ref[...] = msg_rows[...].astype(BFLOAT)
     pl.semaphore_wait(barrier, len(partners))
-    for d in range(7):
-        message(d).start()
+    message(0, msg_ref, tx, beside).start()
+    for d in range(3):
+        message(1 + d, msg_ref, tx, {"ty": ty, "tx": 2 * lax.rem(z + 1 + d, 4) + y}).start()
     msgs[tx] = msg_ref[...]
+    for load in loads[1:]:
+        load.start()
     for b in range(2):
         for t in range(8):
             table, _, _ = axis_rows(1, sides[b], t * wide, lanes)
@@ -532,7 +552,7 @@
         ).astype(BFLOAT)
         padded[272:LANES] = jnp.zeros((LANES - 272, width), BFLOAT)
     fgain_ref[...] = jnp.zeros_like(fgain_ref)
-    fgain_ref[:, 0:FEAT] = fgain_v[...]
+    fgain_ref[:, 0:FEAT] = fgain_v[...].reshape(1, FEAT)
     pixels[0:GROUP] = hot_ref[...]
     pixels[GROUP : 2 * GROUP] = hot_ref[...]
     gains_out[...] = jnp.zeros_like(gains_out)
@@ -556,15 +576,17 @@
         scores[...] = dot_nn(pixcoefs[t], pixels[...])
         return block
 
-    def front_step(d, _):
-        @pl.when(d > 0)
+    def front_step(k, _):
+        t = message_from(k)
+
+        @pl.when(k > 0)
         def _():
-            pltpu.make_async_remote_copy(
-                src_ref=msg_ref, dst_ref=msgs.at[tx], send_sem=tx_s.at[0, d - 1],
-                recv_sem=tx_r.at[0, d - 1], device_id=beside, device_id_type=MESH,
-            ).wait()
-
-        t = lax.rem(tx + 8 - d, 8)
+            message(k - 1, msg_ref, tx, beside).wait()
+
+        @pl.when((k > 1) & (k < 5))
+        def _():
+            message(k + 2, msgs.at[t], t, beside).start()
+
         block = take_block(t)
         for group in range(4):
             at = pl.ds(group * count, count)
@@ -628,8 +650,6 @@
     for h in range(8):
         q_out[h] = value[:, 128 * h : 128 * h + 128]
     q_copies = spread(2, q_out, q_in)
-    give_x(5, hidden)
-    give_x(4, act)
     give_x(3, trows)
     back_four = times_back(cot, fdown)
     finish(kv_copies)
@@ -656,10 +676,6 @@
         .reshape(8, share, 128)
     )
     copies = spread(3, mixed_out, mixed_in)
-    pass_g(0)
-    pass_x(5)
-    pass_x(4)
-    pass_x(3)
     finish(copies)
     mixed = jnp.concatenate([mixed_in[h] for h in range(8)], axis=1)
     give_x(2, mixed)
@@ -670,7 +686,6 @@
     give_x(1, frows)
     fact, fact_slope = gelu_pair(times(frows, fup))
     fact = fact.astype(BFLOAT)
-    give_x(0, fact)
 
     def put_gain(row, grad):
         for h in range(4):
@@ -689,11 +704,8 @@
     give_g(2, g_tower)
     result_v[...] = (three + times(fact, fdown)).astype(BFLOAT)
     result_copies = hand_out(2, result_v, result_ref)
-    pass_x(2)
-    pass_x(1)
-    pass_x(0)
-    pass_g(1)
     finish(copies)
+    give_x(0, fact)
     gm = gm_in[...].reshape(8 * share, 128)
     q = q_in[...].reshape(8 * share, 128)
     k1 = kv_in[:, 0:32].reshape(8 * share, 128)
@@ -717,7 +729,6 @@
     kv_out[:, 0:32] = (gk + kvx_in[0].astype(FLOAT)).astype(BFLOAT).reshape(8, share, 128)
     kv_out[:, 32:64] = (gv + kvx_in[1].astype(FLOAT)).astype(BFLOAT).reshape(8, share, 128)
     kv_copies = spread(12, kv_out, gkv_in)
-    pass_g(2)
     stage_one(0)
     finish(q_copies)
     value = jnp.concatenate([gq_in[h] for h in range(8)], axis=1)
@@ -732,14 +743,9 @@
     put_gain(1, t_grad)
     g_two = g_three + g_two
     g_hidden = g_two.astype(BFLOAT)
-    give_g(6, g_hidden)
-    pass_g(3)
     stage_two(0)
     stage_one(1)
     g_hlift = (times_back(g_hidden, down) * act_slope).astype(BFLOAT)
-    give_g(7, g_hlift)
-    pass_g(4)
-    pass_g(5)
     stage_two(1)
     stage_one(2)
     g_one, h_grad = norm_rows_back(times_back(g_hlift, up), hgain_ref[...], h_unit, h_rate)
@@ -755,11 +761,18 @@
     feat_part = jnp.sum(raw_mix * raw_up, axis=0, keepdims=True)
     delta = jnp.sum(g_att.astype(FLOAT) * attended, axis=1, keepdims=True)
     lane = lax.broadcasted_iota(jnp.int32, raw_up.shape, 1)
-    up_ref[ty] = jnp.where(
-        lane < FEAT, raw_up * fgain, jnp.where(lane == FEAT, delta, shift)
-    )
-    copies = to_ty(5, up_ref.at[ty], up_ref.at[ty])
-    pass_g(6)
+    sent = raw_up * fgain
+    for at, number in ((FEAT, delta), (FEAT + 3, shift)):
+        for k in range(3):
+            piece = number.astype(BFLOAT).astype(FLOAT)
+            sent = jnp.where(lane == at + k, piece, sent)
+            number = number - piece
+    up_sent[ty] = sent.astype(BFLOAT)
+    copies = to_ty(5, up_sent.at[ty], up_sent.at[ty])
+    give_x(4, act)
+    give_g(6, g_hidden)
+    give_x(5, hidden)
+    give_g(7, g_hlift)
     stage_two(2)
     stage_one(3)
     finish(later, gain_copies, gcross_copies)
@@ -769,10 +782,17 @@
         0, mix_all[...].reshape(4 * share, LANES), gcross_all[...].reshape(4 * share, 256), gain_rows
     )
     finish(copies)
-    pass_g(7)
-    for i in (3, 4, 5):
-        finish(xg.pop(("px", i), ()))
-
+    finish(xg.pop(("x", 3), ()))
+
+    sent = up_sent[...].astype(FLOAT).reshape(4 * share, LANES)
+    lane = lax.broadcasted_iota(jnp.int32, sent.shape, 1)
+    delta, shift = [
+        sent[:, at : at + 1] + sent[:, at + 1 : at + 2] + sent[:, at + 2 : at + 3]
+        for at in (FEAT, FEAT + 3)
+    ]
+    up_ref[...] = jnp.where(
+        lane < FEAT, sent, jnp.where(lane == FEAT, delta, shift)
+    ).reshape(up_ref.shape)
     coefs_by_pixel(up_ref[...].reshape(4 * share, LANES), thigh_ref, tlow_ref, upcoefs)
 
     def back_step(t):
@@ -799,20 +819,23 @@
         stage_three(t - 4)
         return 0
 
-    lax.fori_loop(0, 3, first_steps, 0)
+    lax.fori_loop(0, 2, first_steps, 0)
+    finish(xg.pop(("x", 4)), xg.pop(("x", 5)))
+    lax.fori_loop(2, 3, first_steps, 0)
     ncopies = product_join(0, ncopies, value_v)
     lax.fori_loop(3, 4, first_steps, 0)
     lax.fori_loop(4, 6, second_steps, 0)
     stage_two(7)
     lax.fori_loop(6, 8, second_steps, 0)
     part_out[...] = features_of(sums, None, thigh_ref, tlow_ref).reshape(part_out.shape)
-    copies = on_ty.start(9, lambda d: part_out.at[ty_at(d)], lambda d: part_in.at[d])
+    half_out[...] = part_out[...].astype(BFLOAT)
+    copies = on_ty.start(9, lambda d: half_out.at[ty_at(d)], lambda d: half_in.at[d])
     value_copies = product_end(0, ncopies, value_v, value_ref)
     unit, rate = norm_rows(lat_ref[ty].astype(FLOAT))
     raw_mix = part_out[ty]
     finish(copies)
     for d in range(3):
-        raw_mix = raw_mix + part_in[d]
+        raw_mix = raw_mix + half_in[d].astype(FLOAT)
     mix = (raw_mix * fgain).astype(BFLOAT)
     gmix[ty] = mix
     mcopies = to_ty(6, gmix.at[ty], gmix.at[ty])
@@ -850,22 +873,22 @@
 
 IN_NAMES = (
     "pixels", "pixel_mask", "latents", "cotangent", "feature_gain", "query_gain", "hidden_gain", "tower_gain",
-    "final_gain", "key_proj", "value_proj", "hot", "hotcol", "ids", "lanes",
+    "final_gain", "key_proj", "value_proj", "hot", "hotrow", "ids", "lanes",
 ) + tuple("w%d" % i for i in range(10))
 COPIED_NAMES = (
     "pix_v", "mask_v", "lat_v", "cot_v", "fgain_v", "qgain_v", "hgain_v", "tgain_v", "ogain_v", "kraw_v", "vraw_v",
-    "hot_v", "hotcol_v", "ids_v", "lanes_v",
+    "hot_v", "hotrow_v", "ids_v", "lanes_v",
 )
 OUT_NAMES = ("result_ref", "grad_ref", "value_ref", "key_ref", "sums_ref")
 SCRATCH_NAMES = (
     "ws", "msgs", "pixcoefs", "upcoefs", "pixels_v", "scores", "ups", "weights", "sums", "tops", "totals",
-    "raw_all", "qrows", "part_out", "part_in", "q_out", "q_in", "kv_out", "kv_in", "kv_more", "probs",
+    "raw_all", "qrows", "part_out", "part_in", "half_out", "half_in", "up_sent", "q_out", "q_in", "kv_out", "kv_in", "kv_more", "probs",
     "mixed_out", "mixed_in", "gm_out", "gm_in", "kvx_out", "kvx_in", "gq_in", "gkv_in", "up_ref", "mix_all",
-    "gcross_out", "gcross_all", "gains_out", "gains_all", "gmix", "x_out", "x_pass", "x_all", "g_out", "g_all",
+    "gcross_out", "gcross_all", "gains_out", "gains_all", "gmix", "x_out", "x_all", "g_out", "g_all",
     "own", "held", "relay_in", "zsend", "zrecv", "last", "nsend", "nextra", "nrecv", "nmore", "msg_rows", "msg", "thigh", "tlow",
     "kproj", "vproj", "fgain", "result_v", "grad_v", "value_v", "key_v",
-    "w_sem", "l_sem", "ty_s", "ty_r", "tx_s", "tx_r", "mate_s", "mate_r", "xg_s", "xg_r", "y_s", "y_r",
-    "z_s", "z_r", "ac_s", "ac_r", "re_s", "re_r", "in_sem", "out_sem",
+    "w_sem", "l_sem", "ty_s", "ty_r", "tx_s", "tx_r", "mate_s", "mate_r", "xg_s", "xg_r",
+    "z_s", "z_r", "ac_s", "ac_r", "re_s", "re_r", "g_s", "g_r", "in_sem", "out_sem",
 ) + COPIED_NAMES
 SINE = tuple((-1) ** n * math.pi ** (2 * n + 1) / math.factorial(2 * n + 1) for n in range(7))
 
@@ -887,13 +910,16 @@
         lanes[2 + axis, first : first + 2 * BANDS] = 1.0
         lanes[4 + axis, 3 + axis] = 1.0
     lanes[6, :FEAT] = 1.0
-    return jnp.asarray(hot, BFLOAT), jnp.asarray(hot[64 : 64 + wide], BFLOAT), jnp.asarray(ids), jnp.asarray(lanes)
+    rows = np.zeros((HALVES, HALVES * high, length), np.float32)
+    for half in range(HALVES):
+        rows[half, half * high : (half + 1) * high] = hot[16 : 16 + high]
+    return jnp.asarray(hot, BFLOAT), jnp.asarray(rows, BFLOAT), jnp.asarray(ids), jnp.asarray(lanes)
 
 
 def main_call(sizes, inputs, matrices):
     pixels, mask, lat, cot = inputs[:4]
     _, share, width = lat.shape
-    inputs = inputs + pixel_constants(pixels.shape[2] // HALVES, pixels.shape[3])
+    inputs = inputs + pixel_constants(pixels.shape[3] // HALVES, pixels.shape[1])
     rows, length = 8 * share, inputs[11].shape[1]
     dma = pltpu.SemaphoreType.DMA
     hbm = pl.BlockSpec(memory_space=pl.ANY)
@@ -915,13 +941,14 @@
             half(2 * GROUP, length), full(rows, length), full(rows, length), half(rows, length),
             full(8, rows, GROUP), full(8, rows, 1), full(8, rows, 1), full(4, share, LANES), half(4 * share, width),
             full(4, share, LANES), full(3, share, LANES),
+            half(4, share, LANES), half(3, share, LANES), half(4, share, LANES),
             half(8, share, 128), half(8, share, 128), half(8, 2 * share, 128), half(8, 2 * share, 128),
             half(8, 2 * share, 128), full(2, rows, rows), half(8, share, 128), half(8, share, 128),
             half(8, share, 128), half(8, share, 128), half(2, rows, 128), half(2, rows, 128),
             half(8, share, 128), half(8, 2 * share, 128),
             full(4, share, LANES), half(4, share, LANES), half(4, share, 256), half(4, share, 256),
             full(2, 4, 8, 256), full(2, 4, 8, 256), half(4, share, LANES),
-            half(6, 2, 4, share, 128), half(6, 4, 4, share, 128), half(6, 4, 2, 4, share, 128),
+            half(6, 2, 4, share, 128), half(6, 4, 2, 4, share, 128),
             half(8, 4, share, 256), half(8, 2, 4, share, 256), full(8, 128, 256), full(8, 128, 256), half(8, 128, 256),
             half(8, 3, 128, 256), half(8, 3, 128, 256), half(8, 128, 256),
             half(2, 8, 32, 256), half(2, 16, 256), half(2, 7, 32, 256), half(2, 7, 16, 256),
@@ -929,8 +956,8 @@
             half(LANES, width), half(LANES, width), full(1, LANES),
             half(share, width), half(share, width), half(4, 272, 256), half(4, 272, 256),
             dma((10,)), dma((8,)), dma((12, 3)), dma((12, 3)), dma((13, 7)), dma((13, 7)),
-            dma((26, 1)), dma((26, 1)), dma((20, 3)), dma((20, 3)), dma((14, 1)), dma((14, 1)),
-            dma((8, 3)), dma((8, 3)), dma((12, 1)), dma((12, 1)), dma((8,)), dma((8,)), dma((15,)), dma((4,)),
+            dma((26, 1)), dma((26, 1)), dma((14, 7)), dma((14, 7)),
+            dma((8, 3)), dma((8, 3)), dma((12, 1)), dma((12, 1)), dma((8,)), dma((8,)), dma((7,)), dma((7,)), dma((15,)), dma((4,)),
         ] + [pltpu.VMEM(v.shape, v.dtype) for v in inputs],
         compiler_params=pltpu.CompilerParams(
             collective_id=1, has_side_effects=True, vmem_limit_bytes=62 << 20
@@ -981,7 +1008,7 @@
     write(4, 7)
     qgain_out[...] = mine[264:265]
     more = jnp.concatenate([query_core_ref[h, 256:272] for h in range(2)], axis=1).astype(FLOAT)
-    feat_out[...] = more[9:10, 0:FEAT]
+    feat_out[...] = more[9:10, 0:FEAT].reshape(FEAT)
     mine = cross_core_ref[quarter, 256:272, inside].astype(FLOAT)
     for i in range(3):
         held[16 + i][...] = mine[8 + i : 9 + i]
@@ -997,7 +1024,7 @@
     block = [shape(128, width)]
     hbm = pl.BlockSpec(memory_space=pl.ANY)
     outs = (
-        [jax.ShapeDtypeStruct(rows, BFLOAT), shape(*rows), shape(1, FEAT), shape(1, 128)]
+        [jax.ShapeDtypeStruct(rows, BFLOAT), shape(*rows), shape(FEAT), shape(1, 128)]
         + block + [shape(FEAT, width)] * 2 + block + block * 8 + [shape(1, 128)] * 3
     )
     return pl.pallas_call(
@@ -1048,7 +1075,8 @@
 
     result, latent_grad, cross_core, query_core, sums = main_call(
         image_sizes,
-        (pixels, pixel_mask, in_shares(latents), in_shares(cotangent), feature_gain[None], query_gain[None],
+        (jnp.transpose(pixels, (1, 3, 0, 2)), jnp.transpose(pixel_mask, (2, 0, 1)), in_shares(latents),
+         in_shares(cotangent), feature_gain, query_gain[None],
          hidden_gain[None], tower_gain[None], final_gain[None], key_proj, value_proj),
         (query_proj, cross_proj, hidden_up, hidden_down, tower_query, tower_key, tower_value,
          tower_proj, final_up, final_down),
@@ -1061,7 +1089,7 @@
     return (
         result.reshape(latents.shape),
         latent_grad.reshape(latents.shape),
-        feature_sum[0],
+        feature_sum,
         query_sum[0],
         query_grad,
         key_grad,

time: 153 us -> 137 us (0.90)
  Pallas kernels: 146 us -> 135 us
  local copies, waits for them, and re-layouts: 4.32 us -> 0 us
    pallas_call x1, Pallas kernels: 137 us -> 127 us  [main_call(): pl.pallas_call(main_kernel, out_shape=(shape((4, share, width), BFLOAT),...]
    unnamed x2 -> x0, local copies, waits for them, and re-layouts: 3.07 us -> none
where the time goes in v6:
time: 137 us; the launch traced here: 136 us
  Pallas kernels  135 us (99%)
    pallas_call x1, Pallas kernels, main_call(): pl.pallas_call(main_kernel, out_shape=(shape((4, share, width), BFLOAT),...  127 us
    pallas_call x1, Pallas kernels, finish_call(): pl.pallas_call(finish_kernel, out_shape=outs, in_specs=[hbm] * 9, out_spe...  8.82 us

profile of v6, /device:TPU:1, one launch (start us, length us, event | category | flops | bytes accessed | tf_op | source)
XLA Modules:
  0.0 136.2 jit_solution(3641200398377285338)
XLA Ops:
  0.7 126.6 %main.1 = (bf16[4,32,1024]{2,1,0:T(8,128)(2,1)}, bf16[4,32,1024]{2,1,0:T(8,128)(2,1)}, bf16[4,272,256]{2,1,0:T(8,128)(2,1)}, bf16[4,272,256]{2,1,0:T(8,128)(2,1)}, bf16[8,4,128,256]{3,2,1,0:T(8,128)(2,1)}) custom-call(s32[2]{0:T(128)} %sizes_ref.1, bf16[3,36,2,72]{3,2,1,0:T(2,128)(2,1)} %bitcast.16, s32[36,2,72]{2,1,0:T(2,128)} %bitcast.17, ...), custom_call_target="tpu_custom_call" | custom-call | tf_op jit(solution)/shard_map/main/pallas_call | solution.py:928
  127.2 8.8 %finish.1 = (bf16[4,32,1024]{2,1,0:T(8,128)(2,1)}, f32[4,32,1024]{2,1,0:T(8,128)}, f32[261]{0:T(512)}, f32[1,128]{1,0:T(1,128)}, f32[128,1024]{1,0:T(8,128)}, /*...) custom-call(bf16[8,4,128,256]{3,2,1,0:T(8,128)(2,1)} %get-tuple-elem, ...), custom_call_target="tpu_custom_call" | custom-call | tf_op jit(solution)/shard_map/finish/pallas_call | solution.py:1030

commit v7 on v6

--- a/solution.py
+++ b/solution.py
@@ -229,7 +229,7 @@
     (ws, msgs, pixcoefs, upcoefs, pixels, scores, ups, weights, sums, tops, totals, raw_all, qrows,
      part_out, part_in, half_out, half_in, up_sent, q_out, q_in, kv_out, kv_in, kv_more, probs, mixed_out, mixed_in, gm_out, gm_in,
      kvx_out, kvx_in, gq_in, gkv_in, up_ref, mix_all, gcross_out, gcross_all, gains_out, gains_all, gmix,
-     x_out, x_all, g_out, g_all, own, held, relay_in, zsend, zrecv, last, nsend, nextra, nrecv, nmore,
+     x_out, x_all, g_out, g_all, own, held, relay_in, zsend, zrecv, last, nrest, nsend, nextra, nrecv, nmore,
      msg_rows, msg_ref, thigh_ref, tlow_ref, kproj_ref, vproj_ref, fgain_ref, result_v, grad_v, value_v, key_v,
      w_sem, l_sem, ty_s, ty_r, tx_s, tx_r, mate_s, mate_r, xg_s, xg_r, z_s, z_r, ac_s, ac_r, re_s, re_r, g_s, g_r,
      in_sem, out_sem,
@@ -408,15 +408,17 @@
         on_mate.copy(2 + w, 0, last.at[w], sums_ref.at[w, ty]).wait()
         pltpu.make_async_copy(last.at[w], sums_ref.at[w, ty], l_sem.at[w]).wait()
 
-    def product_start(i, left, right, gains):
+    def product_main(i, left, right):
         product = outer(left, right)
         nsend[i] = product[0:256].astype(BFLOAT).reshape(8, 32, 256)
+        nrest[i] = product[256:272]
+        return on_tx.start(6 + 3 * i, lambda d: nsend.at[i, tx_at(d)], lambda d: nrecv.at[i, d])
+
+    def product_rest(i, gains):
         row = lax.broadcasted_iota(jnp.int32, (16, 256), 0)
-        more = product[256:272] + jnp.where(row < 8, 0.0, jnp.concatenate([gains, gains], axis=0))
+        more = nrest[i] + jnp.where(row < 8, 0.0, jnp.concatenate([gains, gains], axis=0))
         nextra[i] = more.astype(BFLOAT)
-        return on_tx.start(
-            6 + 3 * i, lambda d: nsend.at[i, tx_at(d)], lambda d: nrecv.at[i, d]
-        ) + on_tx.start(7 + 3 * i, lambda d: nextra.at[i], lambda d: nmore.at[i, d])
+        return on_tx.start(7 + 3 * i, lambda d: nextra.at[i], lambda d: nmore.at[i, d])
 
     def product_join(i, copies, into):
         finish(copies)
@@ -442,6 +444,35 @@
         finish(far)
         there = out.at[lax.rem(ty + 2, 4)]
         return near + on_mate.start(22 + k, lambda d: there, lambda d: there)
+
+    def block_end(copies, into, out):
+        near, far, places = [], [], []
+        for k in range(8):
+            if k:
+                copies[k - 1].wait()
+            rows = pl.ds(pl.multiple_of(lax.rem(tx + 8 - k, 8) * 32, 32), 32)
+            block = into.at[ty, rows]
+            near += on_mate.start(26 + k, lambda d: block, lambda d: out.at[ty, rows])
+            far += across.start(12 + k, lambda d: block, lambda d: out.at[ty, rows])
+            mine = pltpu.make_async_copy(block, out.at[ty, rows], out_sem.at[4 + k])
+            mine.start()
+            near.append(mine)
+            places.append(rows)
+        rows = pl.ds(256, 16)
+        block = into.at[ty, rows]
+        near += on_mate.start(34, lambda d: block, lambda d: out.at[ty, rows])
+        far += across.start(20, lambda d: block, lambda d: out.at[ty, rows])
+        mine = pltpu.make_async_copy(block, out.at[ty, rows], out_sem.at[12])
+        mine.start()
+        return near + [mine], far, places + [rows]
+
+    def block_on(state, out):
+        near, far, places = state
+        for k in range(9):
+            far[k].wait()
+            there = out.at[lax.rem(ty + 2, 4), places[k]]
+            near += on_mate.start(35 + k, lambda d: there, lambda d: there)
+        return near
 
     def product_end(i, copies, into, out):
         finish(copies)
@@ -778,9 +809,9 @@
     finish(later, gain_copies, gcross_copies)
     result_copies = hand_on(2, result_copies, result_ref)
     gain_rows = gains_all[0, 0] + gains_all[0, 1] + gains_all[0, 2] + gains_all[0, 3]
-    ncopies = product_start(
-        0, mix_all[...].reshape(4 * share, LANES), gcross_all[...].reshape(4 * share, 256), gain_rows
-    )
+    ncopies = product_main(
+        0, mix_all[...].reshape(4 * share, LANES), gcross_all[...].reshape(4 * share, 256)
+    ) + product_rest(0, gain_rows)
     finish(copies)
     finish(xg.pop(("x", 3), ()))
 
@@ -823,10 +854,9 @@
     finish(xg.pop(("x", 4)), xg.pop(("x", 5)))
     lax.fori_loop(2, 3, first_steps, 0)
     ncopies = product_join(0, ncopies, value_v)
-    lax.fori_loop(3, 4, first_steps, 0)
-    lax.fori_loop(4, 6, second_steps, 0)
-    stage_two(7)
-    lax.fori_loop(6, 8, second_steps, 0)
+    back_step(3)
+    stage_two(6)
+    lax.fori_loop(4, 8, second_steps, 0)
     part_out[...] = features_of(sums, None, thigh_ref, tlow_ref).reshape(part_out.shape)
     half_out[...] = part_out[...].astype(BFLOAT)
     copies = on_ty.start(9, lambda d: half_out.at[ty_at(d)], lambda d: half_in.at[d])
@@ -840,32 +870,38 @@
     gmix[ty] = mix
     mcopies = to_ty(6, gmix.at[ty], gmix.at[ty])
     grad_q = (dot_nn(mix, kproj_ref[...]) * cross_scale).astype(BFLOAT)
+    finish(mcopies)
+    right = qrows[:, pl.ds(pl.multiple_of(ty * 256, 256), 256)]
+    mcopies = product_main(1, gmix[...].reshape(4 * share, LANES), right)
+    stage_one(7)
     grad, qgain_grad = norm_rows_back(times_back(grad_q, 0), qgain_ref[...], unit, rate)
     features = feat_part + jnp.sum(raw_mix * raw_all[ty], axis=0, keepdims=True)
     for h in range(4):
         gains_out[1, h, 0:1] = qgain_grad[:, 256 * h : 256 * h + 256]
     gains_out[1, 0, 1:2] = features[:, 0:256]
     gains_out[1, 1, 1:2, 0:128] = features[:, 256:384]
-    mcopies += over_ty(10, gains_out.at[1], gains_all.at[1])
+    gain_copies = over_ty(10, gains_out.at[1], gains_all.at[1])
     grad_v[...] = (g_one + grad).astype(BFLOAT)
     grad_copies = hand_out(3, grad_v, grad_ref)
     for w in range(4):
         stage_four(w)
-    finish(mcopies)
+    finish(gain_copies)
     gain_rows = gains_all[1, 0] + gains_all[1, 1] + gains_all[1, 2] + gains_all[1, 3]
-    right = qrows[:, pl.ds(pl.multiple_of(ty * 256, 256), 256)]
-    mcopies = product_start(1, gmix[...].reshape(4 * share, LANES), right, gain_rows)
+    mcopies += product_rest(1, gain_rows)
     stage_three(4)
     stage_three(5)
+    stage_two(7)
     mcopies = product_join(1, mcopies, key_v)
     value_copies = hand_on(0, value_copies, value_ref)
     grad_copies = hand_on(3, grad_copies, grad_ref)
     stage_three(6)
     stage_three(7)
-    key_copies = product_end(1, mcopies, key_v, key_ref)
-    for w in range(4, 8):
+    key_copies = block_end(mcopies, key_v, key_ref)
+    for w in range(4, 6):
         stage_four(w)
-    key_copies = hand_on(1, key_copies, key_ref)
+    key_copies = block_on(key_copies, key_ref)
+    for w in range(6, 8):
+        stage_four(w)
     finish(result_copies, value_copies, grad_copies, key_copies)
     for w in range(8):
         stage_end(w)
@@ -885,7 +921,7 @@
     "raw_all", "qrows", "part_out", "part_in", "half_out", "half_in", "up_sent", "q_out", "q_in", "kv_out", "kv_in", "kv_more", "probs",
     "mixed_out", "mixed_in", "gm_out", "gm_in", "kvx_out", "kvx_in", "gq_in", "gkv_in", "up_ref", "mix_all",
     "gcross_out", "gcross_all", "gains_out", "gains_all", "gmix", "x_out", "x_all", "g_out", "g_all",
-    "own", "held", "relay_in", "zsend", "zrecv", "last", "nsend", "nextra", "nrecv", "nmore", "msg_rows", "msg", "thigh", "tlow",
+    "own", "held", "relay_in", "zsend", "zrecv", "last", "nrest", "nsend", "nextra", "nrecv", "nmore", "msg_rows", "msg", "thigh", "tlow",
     "kproj", "vproj", "fgain", "result_v", "grad_v", "value_v", "key_v",
     "w_sem", "l_sem", "ty_s", "ty_r", "tx_s", "tx_r", "mate_s", "mate_r", "xg_s", "xg_r",
     "z_s", "z_r", "ac_s", "ac_r", "re_s", "re_r", "g_s", "g_r", "in_sem", "out_sem",
@@ -951,13 +987,13 @@
             half(6, 2, 4, share, 128), half(6, 4, 2, 4, share, 128),
             half(8, 4, share, 256), half(8, 2, 4, share, 256), full(8, 128, 256), full(8, 128, 256), half(8, 128, 256),
             half(8, 3, 128, 256), half(8, 3, 128, 256), half(8, 128, 256),
-            half(2, 8, 32, 256), half(2, 16, 256), half(2, 7, 32, 256), half(2, 7, 16, 256),
+            full(2, 16, 256), half(2, 8, 32, 256), half(2, 16, 256), half(2, 7, 32, 256), half(2, 7, 16, 256),
             full(16, length), half(16, length), half(2, 10 * GROUP, LANES), half(2, 10 * GROUP, LANES),
             half(LANES, width), half(LANES, width), full(1, LANES),
             half(share, width), half(share, width), half(4, 272, 256), half(4, 272, 256),
             dma((10,)), dma((8,)), dma((12, 3)), dma((12, 3)), dma((13, 7)), dma((13, 7)),
-            dma((26, 1)), dma((26, 1)), dma((14, 7)), dma((14, 7)),
-            dma((8, 3)), dma((8, 3)), dma((12, 1)), dma((12, 1)), dma((8,)), dma((8,)), dma((7,)), dma((7,)), dma((15,)), dma((4,)),
+            dma((44, 1)), dma((44, 1)), dma((14, 7)), dma((14, 7)),
+            dma((8, 3)), dma((8, 3)), dma((21, 1)), dma((21, 1)), dma((8,)), dma((8,)), dma((7,)), dma((7,)), dma((15,)), dma((13,)),
         ] + [pltpu.VMEM(v.shape, v.dtype) for v in inputs],
         compiler_params=pltpu.CompilerParams(
             collective_id=1, has_side_effects=True, vmem_limit_bytes=62 << 20
@@ -970,8 +1006,8 @@
     ins, outs, stage, held = refs[:9], refs[9:28], refs[28:37], refs[37:56]
     in_sem, out_sem = refs[56:]
     copies = [pltpu.make_async_copy(a, v, in_sem.at[i]) for i, (a, v) in enumerate(zip(ins, stage))]
-    for copy in copies:
-        copy.start()
+    for i in (1, 5, 2, 6, 7, 8, 0, 4, 3):
+        copies[i].start()
     tx = lax.axis_index("tx")
     sums_ref, cross_core_ref, query_core_ref, latent_ref, result_in_ref, cross_ref, query_ref, value_ref, key_ref = stage
     result_ref, latent_out, feat_out, qgain_out, query_out, key_out, value_out, cross_out = held[:8]
@@ -982,37 +1018,43 @@
             written.append(pltpu.make_async_copy(held[i], outs[i], out_sem.at[i]))
             written[-1].start()
 
-    copies[0].wait()
-    for w in range(8):
-        for h in range(4):
-            held[8 + w][:, 256 * h : 256 * h + 256] = sums_ref[w, h].astype(FLOAT)
-        write(8 + w)
-    for copy in copies[1:]:
-        copy.wait()
-    result_ref[...] = result_in_ref[...]
-    latent_out[...] = latent_ref[...].astype(FLOAT)
-    write(0, 1)
     here = pl.ds(pl.multiple_of(tx * 128, 128), 128)
     quarter = tx // 2
     inside = pl.ds(pl.multiple_of(lax.rem(tx, 2) * 128, 128), 128)
     scale = 1.0 / math.sqrt(query_ref.shape[0])
+    copies[1].wait()
+    copies[5].wait()
     cross_core = jnp.concatenate([cross_core_ref[h] for h in range(4)], axis=1)
-    query_core = jnp.concatenate([query_core_ref[h] for h in range(4)], axis=1)
     value_out[...] = dot_nt(cross_core, cross_ref[...])[:FEAT]
     write(6)
+    copies[2].wait()
+    copies[6].wait()
+    query_core = jnp.concatenate([query_core_ref[h] for h in range(4)], axis=1)
     key_out[...] = (dot_nn(query_core, query_ref[...]) * scale)[:FEAT]
     write(5)
+    copies[7].wait()
     cross_out[...] = outer(value_ref[:, here], cross_core[:FEAT])
+    write(7)
+    copies[8].wait()
     mine = query_core_ref[quarter, :, inside].astype(FLOAT)
     query_out[...] = outer(mine[:FEAT].astype(BFLOAT), key_ref[...]) * scale
-    write(4, 7)
     qgain_out[...] = mine[264:265]
     more = jnp.concatenate([query_core_ref[h, 256:272] for h in range(2)], axis=1).astype(FLOAT)
     feat_out[...] = more[9:10, 0:FEAT].reshape(FEAT)
     mine = cross_core_ref[quarter, 256:272, inside].astype(FLOAT)
     for i in range(3):
         held[16 + i][...] = mine[8 + i : 9 + i]
-    write(2, 3, 16, 17, 18)
+    write(4, 2, 3, 16, 17, 18)
+    copies[0].wait()
+    for w in range(8):
+        for h in range(4):
+            held[8 + w][:, 256 * h : 256 * h + 256] = sums_ref[w, h].astype(FLOAT)
+        write(8 + w)
+    copies[4].wait()
+    copies[3].wait()
+    result_ref[...] = result_in_ref[...]
+    latent_out[...] = latent_ref[...].astype(FLOAT)
+    write(0, 1)
     for copy in written:
         copy.wait()
 

time: 137 us -> 134 us (0.978)
  Pallas kernels: 135 us -> 133 us
    pallas_call x1, Pallas kernels: 8.82 us -> 6.59 us  [finish_call(): pl.pallas_call(finish_kernel, out_shape=outs, in_specs=[hbm] * 9, out_spe...]
where the time goes in v7:
time: 134 us
  Pallas kernels  133 us (99%)
    pallas_call x1, Pallas kernels, main_call(): pl.pallas_call(main_kernel, out_shape=(shape((4, share, width), BFLOAT),...  126 us
    pallas_call x1, Pallas kernels, finish_call(): pl.pallas_call(finish_kernel, out_shape=outs, in_specs=[hbm] * 9, out_spe...  6.59 us

profile of v7, /device:TPU:1, one launch (start us, length us, event | category | flops | bytes accessed | tf_op | source)
XLA Modules:
  0.0 133.7 jit_solution(13779247715022768984)
XLA Ops:
  0.7 126.3 %main.1 = (bf16[4,32,1024]{2,1,0:T(8,128)(2,1)}, bf16[4,32,1024]{2,1,0:T(8,128)(2,1)}, bf16[4,272,256]{2,1,0:T(8,128)(2,1)}, bf16[4,272,256]{2,1,0:T(8,128)(2,1)}, bf16[8,4,128,256]{3,2,1,0:T(8,128)(2,1)}) custom-call(s32[2]{0:T(128)} %sizes_ref.1, bf16[3,36,2,72]{3,2,1,0:T(2,128)(2,1)} %bitcast.16, s32[36,2,72]{2,1,0:T(2,128)} %bitcast.17, ...), custom_call_target="tpu_custom_call" | custom-call | tf_op jit(solution)/shard_map/main/pallas_call | solution.py:964
  126.9 6.6 %finish.1 = (bf16[4,32,1024]{2,1,0:T(8,128)(2,1)}, f32[4,32,1024]{2,1,0:T(8,128)}, f32[261]{0:T(512)}, f32[1,128]{1,0:T(1,128)}, f32[128,1024]{1,0:T(8,128)}, /*...) custom-call(bf16[8,4,128,256]{3,2,1,0:T(8,128)(2,1)} %get-tuple-elem, ...), custom_call_target="tpu_custom_call" | custom-call | tf_op jit(solution)/shard_map/finish/pallas_call | solution.py:1072

commit v8 on v7

--- a/solution.py
+++ b/solution.py
@@ -219,13 +219,9 @@
     return table, coord, total
 
 
-def main_kernel(
-    sizes_ref, *refs
-):
-    names = IN_NAMES + OUT_NAMES + SCRATCH_NAMES
-    r = dict(zip(names, refs))
-    matrices = [r["w%d" % i] for i in range(10)]
-    result_ref, grad_ref, value_ref, key_ref, sums_ref = [r[n] for n in OUT_NAMES]
+def main_kernel(sizes_ref, *refs):
+    matrices = refs[15:25]
+    result_ref, grad_ref, value_ref, key_ref, sums_ref = refs[25:30]
     (ws, msgs, pixcoefs, upcoefs, pixels, scores, ups, weights, sums, tops, totals, raw_all, qrows,
      part_out, part_in, half_out, half_in, up_sent, q_out, q_in, kv_out, kv_in, kv_more, probs, mixed_out, mixed_in, gm_out, gm_in,
      kvx_out, kvx_in, gq_in, gkv_in, up_ref, mix_all, gcross_out, gcross_all, gains_out, gains_all, gmix,
@@ -234,7 +230,7 @@
      w_sem, l_sem, ty_s, ty_r, tx_s, tx_r, mate_s, mate_r, xg_s, xg_r, z_s, z_r, ac_s, ac_r, re_s, re_r, g_s, g_r,
      in_sem, out_sem,
      pix_v, mask_v, lat_ref, cot_ref, fgain_v, qgain_ref, hgain_ref, tgain_ref, ogain_ref,
-     kraw_v, vraw_v, hot_ref, hotrow_ref, ids_ref, lanes_ref) = [r[n] for n in SCRATCH_NAMES]
+     kraw_v, vraw_v, hot_ref, hotrow_ref, ids_ref, lanes_ref) = refs[30:]
     ty, tx = lax.axis_index("ty"), lax.axis_index("tx")
     z, y = tx // 2, lax.rem(tx, 2)
     tys = [{"ty": lax.rem(ty + d, 4), "tx": tx} for d in (1, 2, 3)]
@@ -247,8 +243,8 @@
     handing = Ring(tys + over, xg_s, xg_r)
     loads = []
     small = []
-    for i, (name, into) in enumerate(zip(IN_NAMES, COPIED_NAMES)):
-        small.append(pltpu.make_async_copy(r[name], r[into], in_sem.at[i]))
+    for i, (source, into) in enumerate(zip(refs[:15], refs[-15:])):
+        small.append(pltpu.make_async_copy(source, into, in_sem.at[i]))
         small[i].start()
     for i, w in enumerate(matrices):
         loads.append(pltpu.make_async_copy(w, ws.at[i], w_sem.at[i]))
@@ -907,25 +903,6 @@
         stage_end(w)
 
 
-IN_NAMES = (
-    "pixels", "pixel_mask", "latents", "cotangent", "feature_gain", "query_gain", "hidden_gain", "tower_gain",
-    "final_gain", "key_proj", "value_proj", "hot", "hotrow", "ids", "lanes",
-) + tuple("w%d" % i for i in range(10))
-COPIED_NAMES = (
-    "pix_v", "mask_v", "lat_v", "cot_v", "fgain_v", "qgain_v", "hgain_v", "tgain_v", "ogain_v", "kraw_v", "vraw_v",
-    "hot_v", "hotrow_v", "ids_v", "lanes_v",
-)
-OUT_NAMES = ("result_ref", "grad_ref", "value_ref", "key_ref", "sums_ref")
-SCRATCH_NAMES = (
-    "ws", "msgs", "pixcoefs", "upcoefs", "pixels_v", "scores", "ups", "weights", "sums", "tops", "totals",
-    "raw_all", "qrows", "part_out", "part_in", "half_out", "half_in", "up_sent", "q_out", "q_in", "kv_out", "kv_in", "kv_more", "probs",
-    "mixed_out", "mixed_in", "gm_out", "gm_in", "kvx_out", "kvx_in", "gq_in", "gkv_in", "up_ref", "mix_all",
-    "gcross_out", "gcross_all", "gains_out", "gains_all", "gmix", "x_out", "x_all", "g_out", "g_all",
-    "own", "held", "relay_in", "zsend", "zrecv", "last", "nrest", "nsend", "nextra", "nrecv", "nmore", "msg_rows", "msg", "thigh", "tlow",
-    "kproj", "vproj", "fgain", "result_v", "grad_v", "value_v", "key_v",
-    "w_sem", "l_sem", "ty_s", "ty_r", "tx_s", "tx_r", "mate_s", "mate_r", "xg_s", "xg_r",
-    "z_s", "z_r", "ac_s", "ac_r", "re_s", "re_r", "g_s", "g_r", "in_sem", "out_sem",
-) + COPIED_NAMES
 SINE = tuple((-1) ** n * math.pi ** (2 * n + 1) / math.factorial(2 * n + 1) for n in range(7))
 
 

time: 134 us -> 134 us (level)
  no operation moved by 1% of the time
where the time goes in v8:
time: 134 us
  Pallas kernels  133 us (99%)
    pallas_call x1, Pallas kernels, main_call(): pl.pallas_call(main_kernel, out_shape=(shape((4, share, width), BFLOAT),...  126 us
    pallas_call x1, Pallas kernels, finish_call(): pl.pallas_call(finish_kernel, out_shape=outs, in_specs=[hbm] * 9, out_spe...  6.59 us

profile of v8, /device:TPU:1, one launch (start us, length us, event | category | flops | bytes accessed | tf_op | source)
XLA Modules:
  0.0 133.7 jit_solution(13779247715022768984)
XLA Ops:
  0.7 126.3 %main.1 = (bf16[4,32,1024]{2,1,0:T(8,128)(2,1)}, bf16[4,32,1024]{2,1,0:T(8,128)(2,1)}, bf16[4,272,256]{2,1,0:T(8,128)(2,1)}, bf16[4,272,256]{2,1,0:T(8,128)(2,1)}, bf16[8,4,128,256]{3,2,1,0:T(8,128)(2,1)}) custom-call(s32[2]{0:T(128)} %sizes_ref.1, bf16[3,36,2,72]{3,2,1,0:T(2,128)(2,1)} %bitcast.16, s32[36,2,72]{2,1,0:T(2,128)} %bitcast.17, ...), custom_call_target="tpu_custom_call" | custom-call | tf_op jit(solution)/shard_map/main/pallas_call | solution.py:941
  126.9 6.6 %finish.1 = (bf16[4,32,1024]{2,1,0:T(8,128)(2,1)}, f32[4,32,1024]{2,1,0:T(8,128)}, f32[261]{0:T(512)}, f32[1,128]{1,0:T(1,128)}, f32[128,1024]{1,0:T(8,128)}, /*...) custom-call(bf16[8,4,128,256]{3,2,1,0:T(8,128)(2,1)} %get-tuple-elem, ...), custom_call_target="tpu_custom_call" | custom-call | tf_op jit(solution)/shard_map/finish/pallas_call | solution.py:1049
